TPU v7x, 256 devices: a whole 4x4x8 slice. The times are simulated.
256 devices in a mesh: clip: 4 (over y_lo, core), seq: 64 (over z, y_hi, x).
Axes of the slice: x: 4, y: 4 (y_hi: 2, y_lo: 2; y = y_hi * 2 + y_lo), z: 8, core: 2. Of those that a mesh axis runs over, the one named last changes fastest.
Arguments:
- queries: bfloat16 [4, 32768, 3072], P('clip', 'seq'), may hold values from -6 to 6
- grad_out: bfloat16 [4, 32768, 3072], P('clip', 'seq'), may hold values from -6 to 6
- kept_pos: int32 [4, 32768], P('clip', 'seq'), may hold values from 0 to 511, as said below
- kept_count: int32 [4, 64], P('clip'), may hold values from 1 to 512, as said below
- caption_len: int32 [4], P('clip'), may hold values from 256 to 512, as said below
- cap_keys: bfloat16 [4, 512, 3072], P('clip', 'seq'), may hold values from -150 to 150
- cap_values: bfloat16 [4, 512, 3072], P('clip', 'seq'), may hold values from -6 to 6
- query_gain: float32 [3072], replicated, may hold values from 0.5 to 1.5
Outputs:
- query_grad: bfloat16 [4, 32768, 3072], P('clip', 'seq')
- key_grad: bfloat16 [4, 512, 3072], P('clip', 'seq')
- value_grad: bfloat16 [4, 512, 3072], P('clip', 'seq')
- gain_grad: float32 [3072], P('clip')
Inputs may be any that keep to these rules, and one draw needn't show every extreme that they name: `kept_pos`: for each clip and each device along seq, its 512 entries are a permutation of 0 to 511: first the positions of its kept rows in ascending order, then the other positions in ascending order. `kept_count`: in every clip some device keeps all 512 tokens. `caption_len`: some clip has all 512 caption tokens.
All inputs are finite; a program needn't handle non-finite values.
Results may differ from a plain program's by a relative error of at most 0.005.
The roundings to bfloat16 on the way count: a program that leaves them out, or rounds other values in their place, can miss the bound.
Values may be sent and summed in bfloat16 or wider, within the bound.
No kernel may reach another device: no remote copies, remote signals or barrier semaphores. Data moves between devices by JAX's collectives and lax.ppermute only.
A program may use at most 192 MiB of HBM per device.

v0:
```python
import math

import jax
import jax.numpy as jnp
from jax import lax
from jax.sharding import PartitionSpec as P

HEAD_DIM = 128
TILE = 128


def tile_grads(rows_q, rows_d, live_rows, keys_h, values_h, key_mask, gain_h):
    row_count = rows_q.shape[0]
    head_count, head_width = gain_h.shape
    scale = 1.0 / math.sqrt(head_width)
    inputs_f = rows_q.astype(jnp.float32).reshape(row_count, head_count, head_width)
    inv_rms = lax.rsqrt(jnp.mean(inputs_f * inputs_f, axis=-1, keepdims=True) + 1e-06)
    normed = inputs_f * inv_rms
    q_normed = (normed * gain_h).astype(jnp.bfloat16)
    live_grad = jnp.where(live_rows[:, None], rows_d, jnp.zeros_like(rows_d)).reshape(
        row_count, head_count, head_width
    )
    scores = (
        jnp.einsum("thd,chd->htc", q_normed, keys_h, preferred_element_type=jnp.float32) * scale
    )
    scores = jnp.where(key_mask, scores, -jnp.inf)
    highest = jnp.max(scores, axis=-1, keepdims=True)
    expo = jnp.exp(scores - highest)
    probs = expo / jnp.sum(expo, axis=-1, keepdims=True)
    probs_bf = probs.astype(jnp.bfloat16)
    dprobs = jnp.einsum("thd,chd->htc", live_grad, values_h, preferred_element_type=jnp.float32)
    row_delta = jnp.sum(probs * dprobs, axis=-1, keepdims=True)
    dscores = (probs * (dprobs - row_delta) * scale).astype(jnp.bfloat16)
    dnormed = jnp.einsum("htc,chd->thd", dscores, keys_h, preferred_element_type=jnp.float32)
    key_term = jnp.einsum("htc,thd->chd", dscores, q_normed, preferred_element_type=jnp.float32)
    value_term = jnp.einsum("htc,thd->chd", probs_bf, live_grad, preferred_element_type=jnp.float32)
    gain_term = jnp.sum(dnormed * normed, axis=0)
    scaled = gain_h * dnormed
    dinput = inv_rms * (scaled - normed * jnp.mean(scaled * normed, axis=-1, keepdims=True))
    return (
        dinput.astype(jnp.bfloat16).reshape(row_count, head_count * head_width),
        key_term,
        value_term,
        gain_term,
    )


def run_tiles(q_src, d_src, first_row, last_row, carry_state, keys_h, values_h, key_mask, gain_h):

    def step(tile_index, current_state):
        key_acc, value_acc, gain_acc, output = current_state
        row_start = tile_index * TILE
        rows_q = lax.dynamic_slice_in_dim(q_src, row_start, TILE, 0)
        rows_d = lax.dynamic_slice_in_dim(d_src, row_start, TILE, 0)
        row_ids = row_start + jnp.arange(TILE, dtype=jnp.int32)
        live_rows = (row_ids >= first_row) & (row_ids < last_row)
        dinput, key_term, value_term, gain_term = tile_grads(
            rows_q, rows_d, live_rows, keys_h, values_h, key_mask, gain_h
        )
        previous = lax.dynamic_slice_in_dim(output, row_start, TILE, 0)
        output = lax.dynamic_update_slice_in_dim(
            output, jnp.where(live_rows[:, None], dinput, previous), row_start, 0
        )
        return (key_acc + key_term, value_acc + value_term, gain_acc + gain_term, output)

    return lax.fori_loop(first_row // TILE, (last_row + TILE - 1) // TILE, step, carry_state)


def body(queries, grad_out, kept_pos, kept_count, caption_len, cap_keys, cap_values, query_gain):
    q_all = queries[0]
    d_all = grad_out[0]
    shard_rows, feat = q_all.shape
    head_count = feat // HEAD_DIM
    gain_h = query_gain.reshape(head_count, HEAD_DIM)
    caption_keys, caption_values = (
        lax.all_gather(cap_keys[0], "seq", axis=0, tiled=True),
        lax.all_gather(cap_values[0], "seq", axis=0, tiled=True),
    )
    cap_rows = caption_keys.shape[0]
    keys_h = caption_keys.reshape(cap_rows, head_count, HEAD_DIM)
    values_h = caption_values.reshape(cap_rows, head_count, HEAD_DIM)
    key_mask = jnp.arange(cap_rows, dtype=jnp.int32) < caption_len[0]
    position = lax.axis_index("seq")
    counts = kept_count[0]
    own_count = counts[position]
    start_state = (
        jnp.zeros((cap_rows, head_count, HEAD_DIM), jnp.float32),
        jnp.zeros((cap_rows, head_count, HEAD_DIM), jnp.float32),
        jnp.zeros((head_count, HEAD_DIM), jnp.float32),
        jnp.zeros((shard_rows, feat), jnp.bfloat16),
    )
    key_acc, value_acc, gain_acc, dx_all = run_tiles(
        q_all, d_all, 0, own_count, start_state, keys_h, values_h, key_mask, gain_h
    )
    query_grad = jnp.zeros((shard_rows, feat), jnp.bfloat16).at[kept_pos[0]].set(dx_all)
    key_flat = key_acc.reshape(cap_rows, feat)
    value_flat = value_acc.reshape(cap_rows, feat)
    key_part, value_part = (
        lax.psum_scatter(key_flat, "seq", scatter_dimension=0, tiled=True),
        lax.psum_scatter(value_flat, "seq", scatter_dimension=0, tiled=True),
    )
    gain_flat = gain_acc.reshape(feat)
    gain_total = lax.psum(gain_flat, "seq")
    gain_grad = lax.psum_scatter(gain_total, "clip", scatter_dimension=0, tiled=True)
    return (
        query_grad[None],
        key_part.astype(jnp.bfloat16)[None],
        value_part.astype(jnp.bfloat16)[None],
        gain_grad,
    )


def solution(mesh):
    return jax.shard_map(
        body,
        mesh=mesh,
        in_specs=(
            P("clip", "seq", None),
            P("clip", "seq", None),
            P("clip", "seq"),
            P("clip", None),
            P("clip"),
            P("clip", "seq", None),
            P("clip", "seq", None),
            P(),
        ),
        out_specs=(
            P("clip", "seq", None),
            P("clip", "seq", None),
            P("clip", "seq", None),
            P("clip"),
        ),
        check_vma=False,
    )
```

profile of v0, /device:TPU:2, one launch (start us, length us, event | category | flops | bytes accessed | tf_op | source)
XLA Modules:
  0.0 2205.6 jit_solution(18418771501817355599)
XLA Ops:
  10.0 4.8 copy.37
  14.8 2.8 copy.39
  17.6 119.8 %all-gather.7.cloned.1.call-done = bf16[1,512,3072]{2,1,0:T(8,128)(2,1)} async-done(((bf16[1,8,3072]{2,1,0:T(8,128)(2,1)}), bf16[1,512,3072]{2,1,0:T(8,128)(2,1)}) %all-gather.7.cloned.1.call-update) | async-done | bytes 3145744 | tf_op jit(solution)/shard_map/all_gather | solution.py:77
  137.4 3.2 copy.40
  140.6 2.8 copy.42
  143.4 117.0 %all-gather.5.cloned.1.call-done = bf16[1,512,3072]{2,1,0:T(8,128)(2,1)} async-done(((bf16[1,8,3072]{2,1,0:T(8,128)(2,1)}), bf16[1,512,3072]{2,1,0:T(8,128)(2,1)}) %all-gather.5.cloned.1.call-update) | async-done | bytes 3145744 | tf_op jit(solution)/shard_map/all_gather | solution.py:76
  260.4 4.7 copy.38
  265.1 3.4 broadcast.69
  268.5 3.4 broadcast.69.clone
  271.9 2.1 broadcast.68
  274.0 325.9 %while.17 = (s32[]{:T(128)}, f32[512,24,128]{0,2,1:T(8,128)}, f32[512,24,128]{0,2,1:T(8,128)}, f32[24,128]{1,0:T(8,128)S(1)}, bf16[512,3072]{1,0:T(8,128)(2,1)},...) while((s32[]{:T(128)}, f32[512,24,128]{0,2,1:T(8,128)}, ...), condition=%wide.region_7.8_spmd.clone, body=%wide.region_0.7_spmd.clone.sunk | while | flops 2061643264 | bytes 137909904 | solution.py:66
  274.8 1.7 dynamic-slice_select_fusion.2
  276.7 2.0 fusion.82
  279.4 3.7 fusion.83
  283.1 3.7 fusion.80
  286.8 26.7 %fusion.84 = (f32[128,24]{0,1:T(8,128)S(1)}, f32[24,128]{1,0:T(8,128)S(1)}, f32[24,128,128]{1,2,0:T(8,128)S(1)}) fusion(bf16[128,24,128]{0,2,1:T(8,128)(2,1)S(1)} %bitcast.68, f32[24,128]{1,0:T(8,128)S(1)} %bitcast.81, f32[128,24]{0,1:T(8,128)S(1)} %add_rsqrt_fusion.2, bf16[512,24,128]{0,2,1:T(8,128)(2,1)} %get-tuple-element.317, ...), kind=kOutput, calls=%fused_computation.28.clone.1 | convolution fusion | flops 416413184 | bytes 18149376 | tf_op jit(solution)/shard_map/while/body/htc,chd->thd/dot_general | solution.py:34
  319.1 8.3 bitcast_add_fusion.5
  327.4 28.1 %bitcast_add_fusion.4 = f32[512,24,128]{0,2,1:T(8,128)} fusion(f32[512,24,128]{0,2,1:T(8,128)} %get-tuple-element.293, f32[24,128,512]{2,1,0:T(8,128)} %fusion.80, bf16[128,24,128]{0,2,1:T(8,128)(2,1)S(1)} %bitcast.70, f32[24,128]{1,0:T(8,128)S(1)} %bitcast.83, f32[128,24]{0,1:T(8,128)S(1)} %add_rsqrt_fusion.2, ...), kind=kOutput, calls=%fused_computation.5.clone.1 | convolution fusion | flops 416812544 | bytes 25989120 | tf_op jit(solution)/shard_map/while/body/htc,thd->chd/dot_general | solution.py:35
  356.3 1.7 dynamic-slice_select_fusion.2
  358.2 2.0 fusion.82
  360.9 3.7 fusion.83
  364.6 3.7 fusion.80
  368.3 26.7 %fusion.84 = (f32[128,24]{0,1:T(8,128)S(1)}, f32[24,128]{1,0:T(8,128)S(1)}, f32[24,128,128]{1,2,0:T(8,128)S(1)}) fusion(bf16[128,24,128]{0,2,1:T(8,128)(2,1)S(1)} %bitcast.68, f32[24,128]{1,0:T(8,128)S(1)} %bitcast.81, f32[128,24]{0,1:T(8,128)S(1)} %add_rsqrt_fusion.2, bf16[512,24,128]{0,2,1:T(8,128)(2,1)} %get-tuple-element.317, ...), kind=kOutput, calls=%fused_computation.28.clone.1 | convolution fusion | flops 416413184 | bytes 18149376 | tf_op jit(solution)/shard_map/while/body/htc,chd->thd/dot_general | solution.py:34
  400.6 8.3 bitcast_add_fusion.5
  408.9 28.1 %bitcast_add_fusion.4 = f32[512,24,128]{0,2,1:T(8,128)} fusion(f32[512,24,128]{0,2,1:T(8,128)} %get-tuple-element.293, f32[24,128,512]{2,1,0:T(8,128)} %fusion.80, bf16[128,24,128]{0,2,1:T(8,128)(2,1)S(1)} %bitcast.70, f32[24,128]{1,0:T(8,128)S(1)} %bitcast.83, f32[128,24]{0,1:T(8,128)S(1)} %add_rsqrt_fusion.2, ...), kind=kOutput, calls=%fused_computation.5.clone.1 | convolution fusion | flops 416812544 | bytes 25989120 | tf_op jit(solution)/shard_map/while/body/htc,thd->chd/dot_general | solution.py:35
  437.8 1.7 dynamic-slice_select_fusion.2
  439.7 2.0 fusion.82
  442.4 3.7 fusion.83
  446.1 3.7 fusion.80
  449.8 26.7 %fusion.84 = (f32[128,24]{0,1:T(8,128)S(1)}, f32[24,128]{1,0:T(8,128)S(1)}, f32[24,128,128]{1,2,0:T(8,128)S(1)}) fusion(bf16[128,24,128]{0,2,1:T(8,128)(2,1)S(1)} %bitcast.68, f32[24,128]{1,0:T(8,128)S(1)} %bitcast.81, f32[128,24]{0,1:T(8,128)S(1)} %add_rsqrt_fusion.2, bf16[512,24,128]{0,2,1:T(8,128)(2,1)} %get-tuple-element.317, ...), kind=kOutput, calls=%fused_computation.28.clone.1 | convolution fusion | flops 416413184 | bytes 18149376 | tf_op jit(solution)/shard_map/while/body/htc,chd->thd/dot_general | solution.py:34
  482.0 8.3 bitcast_add_fusion.5
  490.3 28.1 %bitcast_add_fusion.4 = f32[512,24,128]{0,2,1:T(8,128)} fusion(f32[512,24,128]{0,2,1:T(8,128)} %get-tuple-element.293, f32[24,128,512]{2,1,0:T(8,128)} %fusion.80, bf16[128,24,128]{0,2,1:T(8,128)(2,1)S(1)} %bitcast.70, f32[24,128]{1,0:T(8,128)S(1)} %bitcast.83, f32[128,24]{0,1:T(8,128)S(1)} %add_rsqrt_fusion.2, ...), kind=kOutput, calls=%fused_computation.5.clone.1 | convolution fusion | flops 416812544 | bytes 25989120 | tf_op jit(solution)/shard_map/while/body/htc,thd->chd/dot_general | solution.py:35
  519.2 1.7 dynamic-slice_select_fusion.2
  521.1 2.0 fusion.82
  523.8 3.7 fusion.83
  527.5 3.7 fusion.80
  531.2 26.7 %fusion.84 = (f32[128,24]{0,1:T(8,128)S(1)}, f32[24,128]{1,0:T(8,128)S(1)}, f32[24,128,128]{1,2,0:T(8,128)S(1)}) fusion(bf16[128,24,128]{0,2,1:T(8,128)(2,1)S(1)} %bitcast.68, f32[24,128]{1,0:T(8,128)S(1)} %bitcast.81, f32[128,24]{0,1:T(8,128)S(1)} %add_rsqrt_fusion.2, bf16[512,24,128]{0,2,1:T(8,128)(2,1)} %get-tuple-element.317, ...), kind=kOutput, calls=%fused_computation.28.clone.1 | convolution fusion | flops 416413184 | bytes 18149376 | tf_op jit(solution)/shard_map/while/body/htc,chd->thd/dot_general | solution.py:34
  563.6 8.3 bitcast_add_fusion.5
  571.8 28.1 %bitcast_add_fusion.4 = f32[512,24,128]{0,2,1:T(8,128)} fusion(f32[512,24,128]{0,2,1:T(8,128)} %get-tuple-element.293, f32[24,128,512]{2,1,0:T(8,128)} %fusion.80, bf16[128,24,128]{0,2,1:T(8,128)(2,1)S(1)} %bitcast.70, f32[24,128]{1,0:T(8,128)S(1)} %bitcast.83, f32[128,24]{0,1:T(8,128)S(1)} %add_rsqrt_fusion.2, ...), kind=kOutput, calls=%fused_computation.5.clone.1 | convolution fusion | flops 416812544 | bytes 25989120 | tf_op jit(solution)/shard_map/while/body/htc,thd->chd/dot_general | solution.py:35
  599.9 6.6 copy.50
  606.8 6.5 copy.49
  615.3 8.2 scatter_custom_fusion
  623.5 10.9 all-reduce
  634.5 177.9 %psum.8 = f32[768]{0:T(1024)} all-reduce(f32[768]{0:T(1024)S(1)} %dynamic-slice.2), channel_id=1, replica_groups=mesh['clip'=4,'seq'=64] {'seq'}, use_global_device_ids=true, to_apply=%region_11.12 | all-reduce | flops 768 | bytes 6144 | tf_op jit(solution)/shard_map/psum | solution.py:103
  812.4 582.4 %reduce-scatter.5.cloned.1.call-done = f32[8,3072]{1,0:T(8,128)} async-done(((f32[512,3072]{1,0:T(8,128)}), f32[8,3072]{1,0:T(8,128)}) %reduce-scatter.5.cloned.1.call-update) | async-done | bytes 98320 | tf_op jit(solution)/shard_map/reduce_scatter | solution.py:100
  1394.8 1.5 convert_bitcast_fusion
  1396.3 801.3 %reduce-scatter.3.cloned.1.call-done = f32[8,3072]{1,0:T(8,128)} async-done(((f32[512,3072]{1,0:T(8,128)}), f32[8,3072]{1,0:T(8,128)}) %reduce-scatter.3.cloned.1.call-update) | async-done | bytes 98320 | tf_op jit(solution)/shard_map/reduce_scatter | solution.py:99
  2197.6 1.5 convert_bitcast_fusion.1
  (89 shorter events, 32.4 us)
Async XLA Ops:
  7.2 1.6 copy-start
  7.2 130.2 %all-gather.7.cloned.1.call-start = ((), (), s32[]{:S(2)}) async-start(), calls=%async_computation.5 | async-start | bytes 3194880 | tf_op jit(solution)/shard_map/all_gather | solution.py:77
  7.9 252.5 %all-gather.5.cloned.1.call-start = ((), (), s32[]{:S(2)}) async-start(), calls=%async_computation.4 | async-start | bytes 3194880 | tf_op jit(solution)/shard_map/all_gather | solution.py:76
  8.7 1386.1 %reduce-scatter.5.cloned.1.call-start = ((), (), s32[]{:S(2)}) async-start(), calls=%async_computation.3 | async-start | bytes 6389760 | tf_op jit(solution)/shard_map/reduce_scatter | solution.py:100
  10.0 4.8 copy-start.4
  271.9 2.1 copy-start.5
  274.0 2.7 copy-start.3
  279.4 3.7 copy-start.2
  355.5 2.7 copy-start.3
  360.9 3.7 copy-start.2
  436.9 2.7 copy-start.3
  442.3 3.7 copy-start.2
  518.4 2.7 copy-start.3
  523.8 3.7 copy-start.2
  606.5 1591.0 %reduce-scatter.3.cloned.1.call-start = ((), (), s32[]{:S(2)}) async-start(), calls=%async_computation.2 | async-start | bytes 6389760 | tf_op jit(solution)/shard_map/reduce_scatter | solution.py:99
  613.4 0.7 copy-start.7
  613.4 1.9 copy-start.6
  613.4 1585.7 %copy-start.1 = (s32[1,64]{1,0:T(1,128)S(1)}, s32[1,64]{1,0:T(1,128)}, u32[]{:S(2)}) copy-start(s32[1,64]{1,0:T(1,128)} %param.13) | copy-start | bytes 772
Sparse Core Ops, SparseCore 0:
  11.7 125.7 all-gather.6
  141.1 119.2 all-gather.4
  606.7 788.0 reduce-scatter.4
  1400.4 797.1 reduce-scatter.2
where the time goes:
time: 2210 us
  waiting for transfers between devices  1620 us (73%)
  matrix products  275 us (12%)
  blocking collectives  189 us (9%)
  local copies, waits for them, and re-layouts  61.7 us (3%)
  other arithmetic  42.1 us (2%)
    reduce_scatter x1, waiting for transfers between devices, body(): lax.psum_scatter(key_flat, 'seq', scatter_dimension=0, tiled=True)  801 us
    reduce_scatter x1, waiting for transfers between devices, body(): lax.psum_scatter(value_flat, 'seq', scatter_dimension=0, tiled=True)  582 us
    psum x1, blocking collectives, body(): gain_total = lax.psum(gain_flat, 'seq')  178 us
    all_gather x1, waiting for transfers between devices, body(): lax.all_gather(cap_values[0], 'seq', axis=0, tiled=True)  120 us
    all_gather x1, waiting for transfers between devices, body(): lax.all_gather(cap_keys[0], 'seq', axis=0, tiled=True)  117 us
    dot_general x4, matrix products, tile_grads(): jnp.einsum('htc,thd->chd', dscores, q_normed, preferred_element_type=jnp....  112 us
    dot_general x4, matrix products, tile_grads(): jnp.einsum('htc,chd->thd', dscores, keys_h, preferred_element_type=jnp.fl...  107 us
  transfers between devices with their start and end apart: 4, of which 4 were waited for; matrix products, arithmetic and copies ran while one was open for 1% of the time, Pallas kernels for 0%

commit v1 on v0

v1 whole, which is shorter than its diff:
```python
import functools
import math

import jax
import jax.numpy as jnp
from jax import lax
from jax.experimental import pallas as pl
from jax.experimental.pallas import tpu as pltpu
from jax.sharding import Mesh, PartitionSpec as P

HEAD_DIM = 128
ROWS = 8
NZ, NY, NX = 8, 2, 4
SEQ = ("z", "yh", "x")
CHUNKS = (24,)
F32, BF16 = jnp.float32, jnp.bfloat16
NT = (((1,), (1,)), ((), ()))
TN = (((0,), (0,)), ((), ()))
NN = (((1,), (0,)), ((), ()))


def dot(a, b, dims):
    return lax.dot_general(a, b, dims, preferred_element_type=F32)


def send(value, axis, size, by):
    return lax.ppermute(value, axis, [(i, (i + by) % size) for i in range(size)])


UNIT = NY * ROWS
ZROWS = NX * UNIT
XROWS = NZ * UNIT
ZORDER = (0, 1, 2, 3, 5, 6, 7)


def kernel(first, *refs):
    (count_ref, q_ref, d_ref, gain_ref, pos_ref, bias_ref) = refs[:6]
    k_refs, v_refs = refs[6:15], refs[15:19]
    rest = refs[19 + (0 if first else 1):]
    qg_ref, dk_ref, dka_ref, dkb_ref, dv0_ref, dv1_ref, dv2_ref, dv3_ref, gg_ref, perm, bias = rest
    rows = q_ref.shape[0]
    count = count_ref[0]
    scale = 1.0 / math.sqrt(HEAD_DIM)

    @pl.when(pl.program_id(0) == 0)
    def _():
        place = lax.broadcasted_iota(jnp.int32, (rows, rows), 0)
        row = lax.broadcasted_iota(jnp.int32, (rows, rows), 1)
        hit = (place == pos_ref[...]) & (row < count)
        perm[...] = jnp.where(hit, 1.0, 0.0).astype(BF16)
        bias[...] = jnp.broadcast_to(bias_ref[...], bias.shape)

    gain = gain_ref[...]
    k = jnp.concatenate([r[...] for r in k_refs], axis=0)
    v_parts = [r[...] for r in v_refs]
    v = jnp.concatenate(
        [v_parts[dx][dz * UNIT : (dz + 1) * UNIT] for dz in range(NZ) for dx in range(NX)], axis=0
    )
    qf = q_ref[...].astype(F32)
    inv = lax.rsqrt(jnp.mean(qf * qf, axis=-1, keepdims=True) + 1e-6)
    normed = qf * inv
    qn = (normed * gain).astype(BF16)
    row = lax.broadcasted_iota(jnp.int32, (rows, HEAD_DIM), 0)
    live = jnp.where(row < count, d_ref[...].astype(F32), 0.0).astype(BF16)
    s = dot(k, qn, NT)
    wide = jnp.concatenate([bias[...]] * (rows // HEAD_DIM), axis=1)
    s = s * (scale * math.log2(math.e)) + wide
    e = jnp.exp2(s - jnp.max(s, axis=0, keepdims=True))
    p = e * (1.0 / jnp.sum(e, axis=0, keepdims=True))
    dp = dot(v, live, NT)
    delta = jnp.sum(p * dp, axis=0, keepdims=True)
    ds = (p * ((dp - delta) * scale)).astype(BF16)
    dk = dot(ds, qn, NN)
    dv = dot(p.astype(BF16), live, NN)
    dn = dot(k, ds, TN).T
    for n, dz in enumerate(ZORDER):
        dk_ref[n * ZROWS : (n + 1) * ZROWS] = dk[dz * ZROWS : (dz + 1) * ZROWS]
    half = ZROWS // 2
    dka_ref[...] = dk[4 * ZROWS : 4 * ZROWS + half].astype(BF16)
    dkb_ref[...] = dk[4 * ZROWS + half : 5 * ZROWS].astype(BF16)
    for dx, ref in enumerate((dv0_ref, dv1_ref, dv2_ref, dv3_ref)):
        for dz in range(NZ):
            at = dz * ZROWS + dx * UNIT
            ref[dz * UNIT : (dz + 1) * UNIT] = dv[at : at + UNIT].astype(ref.dtype)
    prod = dn * normed
    gg_ref[...] = jnp.sum(prod, axis=0, keepdims=True)[None]
    mean = jnp.mean(prod * gain, axis=-1, keepdims=True)
    dx_rows = inv * (gain * dn - normed * mean)
    qg_ref[...] = dot(perm[...], dx_rows.astype(BF16), NN).astype(BF16)


def grads(head, heads, count, q, d, gain, pos, bias, k_parts, v_parts, before):
    rows, feat = q.shape
    cols = heads * HEAD_DIM
    at = lambda i, *_: (0, head + i)
    here = lambda i, *_: (0, i)
    fixed = lambda i, *_: (0, 0)
    half = ZROWS // 2
    outs = [
        (rows, feat, BF16, at),
        (7 * ZROWS, cols, F32, here),
        (half, cols, BF16, here),
        (half, cols, BF16, here),
        (XROWS, cols, F32, here),
        (XROWS, cols, BF16, here),
        (XROWS, cols, BF16, here),
        (XROWS, cols, BF16, here),
    ]
    first = before is None
    in_specs = [
        pl.BlockSpec((rows, HEAD_DIM), at),
        pl.BlockSpec((rows, HEAD_DIM), at),
        pl.BlockSpec((1, HEAD_DIM), at),
        pl.BlockSpec(pos.shape, fixed),
        pl.BlockSpec(bias.shape, fixed),
    ] + [pl.BlockSpec((part.shape[0], HEAD_DIM), here) for part in k_parts + v_parts]
    args = [count, q, d, gain, pos, bias, *k_parts, *v_parts]
    aliases = {}
    if not first:
        in_specs.append(pl.BlockSpec(memory_space=pl.ANY))
        aliases = {len(args): 0}
        args.append(before)
    scores = heads * rows * bias.shape[0]
    return pl.pallas_call(
        functools.partial(kernel, first),
        grid_spec=pltpu.PrefetchScalarGridSpec(
            num_scalar_prefetch=1,
            grid=(heads,),
            in_specs=in_specs,
            out_specs=[pl.BlockSpec((r, HEAD_DIM), where) for r, _, _, where in outs]
            + [pl.BlockSpec((1, 1, HEAD_DIM), lambda i, *_: (i, 0, 0))],
            scratch_shapes=[
                pltpu.VMEM((rows, rows), BF16),
                pltpu.VMEM((bias.shape[0], HEAD_DIM), F32),
            ],
        ),
        out_shape=[jax.ShapeDtypeStruct((r, c), t) for r, c, t, _ in outs]
        + [jax.ShapeDtypeStruct((heads, 1, HEAD_DIM), F32)],
        input_output_aliases=aliases,
        compiler_params=pltpu.CompilerParams(vmem_limit_bytes=40 * 1024 * 1024),
        cost_estimate=pl.CostEstimate(
            flops=12 * scores * HEAD_DIM, bytes_accessed=20 * rows * cols, transcendentals=scores
        ),
        name="head_grads",
    )(*args)


def gather_keys(rows):
    half = ZROWS // 2
    parts = {0: rows}
    ahead = behind = rows
    for step in range(1, NZ // 2):
        ahead, behind = send(ahead, "z", NZ, 1), send(behind, "z", NZ, -1)
        parts[NZ - step], parts[step] = ahead, behind
    ahead, behind = send(ahead[:half], "z", NZ, 1), send(behind[half:], "z", NZ, -1)
    return [parts[dz] for dz in range(4)] + [ahead, behind] + [parts[dz] for dz in range(5, NZ)]


def gather_values(rows):
    return [rows] + [send(rows, "x", NX, -dx) for dx in range(1, NX)]


def sum_keys(terms, ahead, behind):
    half = ZROWS // 2
    term = lambda dz: terms[ZORDER.index(dz) * ZROWS : (ZORDER.index(dz) + 1) * ZROWS]
    wide = lambda part: part.astype(F32)
    ahead, behind = send(ahead, "z", NZ, 1), send(behind, "z", NZ, -1)
    three, five = term(3), term(5)
    ahead = jnp.concatenate([wide(ahead) + three[:half], three[half:]], axis=0)
    behind = jnp.concatenate([five[:half], wide(behind) + five[half:]], axis=0)
    for dz in (2, 1):
        ahead = send(ahead.astype(BF16), "z", NZ, 1)
        behind = send(behind.astype(BF16), "z", NZ, -1)
        ahead, behind = wide(ahead) + term(dz), wide(behind) + term(NZ - dz)
    ahead = send(ahead.astype(BF16), "z", NZ, 1)
    behind = send(behind.astype(BF16), "z", NZ, -1)
    total = term(0) + wide(ahead) + wide(behind)
    parts = [
        send(total[dx * UNIT : (dx + 1) * UNIT].astype(BF16), "x", NX, dx) for dx in range(1, NX)
    ]
    return total[:UNIT] + sum(wide(part) for part in parts)


def sum_values(own, others):
    parts = [send(part, "x", NX, dx + 1) for dx, part in enumerate(others)]
    total = own + sum(part.astype(F32) for part in parts)
    parts = [
        send(total[dz * UNIT : (dz + 1) * UNIT].astype(BF16), "z", NZ, dz) for dz in range(1, NZ)
    ]
    return total[:UNIT] + sum(part.astype(F32) for part in parts)


def sum_gain(gain):
    clips = lax.axis_size("clip")
    quarter = gain.shape[0] // clips
    mine = lax.axis_index("clip")
    pieces = [
        lax.dynamic_slice_in_dim(gain, ((mine + by) % clips) * quarter, quarter)
        for by in range(clips)
    ]
    total = pieces[0] + sum(send(pieces[by], "clip", clips, by) for by in range(1, clips))
    total = total + sum(send(total, "x", NX, by) for by in range(1, NX))
    for step in (1, 2, 4):
        total = total + lax.ppermute(total, "z", [(i, i ^ step) for i in range(NZ)])
    return total + send(total, "yh", NY, 1)


def body(queries, grad_out, kept_pos, kept_count, caption_len, cap_keys, cap_values, query_gain):
    z, yh, x = (lax.axis_index(name) for name in SEQ)
    feat = queries.shape[-1]
    cap = cap_keys.shape[1] * NZ * NY * NX
    count = lax.dynamic_slice_in_dim(kept_count[0], (z * NY + yh) * NX + x, 1)
    slot = jnp.arange(cap, dtype=jnp.int32)[:, None]
    at_z, at_x = (z + slot // ZROWS) % NZ, (x + slot // UNIT) % NX
    at_y = (yh + slot // ROWS) % NY
    caption = ((at_z * NY + at_y) * NX + at_x) * ROWS + slot % ROWS
    bias = jnp.where(caption < caption_len[0], 0.0, -jnp.inf).astype(F32)

    both = jnp.concatenate([cap_keys[0], cap_values[0]], axis=1)
    both = jnp.concatenate([both, send(both, "yh", NY, 1)], axis=0)
    keys, values = both[:, :feat], both[:, feat:]
    keys = jnp.concatenate([keys] + [send(keys, "x", NX, -dx) for dx in range(1, NX)], axis=0)
    values = jnp.concatenate([values] + [send(values, "z", NZ, -dz) for dz in range(1, NZ)], axis=0)

    gain_row = query_gain[None]
    query_grad = None
    key_sums, value_sums, gains = [], [], []
    head = 0
    for heads in CHUNKS:
        cols = slice(head * HEAD_DIM, (head + heads) * HEAD_DIM)
        k_parts, v_parts = gather_keys(keys[:, cols]), gather_values(values[:, cols])
        query_grad, dk, dka, dkb, dv0, dv1, dv2, dv3, gain = grads(
            head, heads, count, queries[0], grad_out[0], gain_row, kept_pos, bias, k_parts, v_parts,
            query_grad,
        )
        key_sums.append(sum_keys(dk, dka, dkb))
        value_sums.append(sum_values(dv0, (dv1, dv2, dv3)))
        gains.append(gain.reshape(-1))
        head += heads
    total = jnp.concatenate(key_sums + value_sums, axis=1)
    total = total[:ROWS] + send(total[ROWS:], "yh", NY, 1)
    total = total.astype(BF16)[None]
    gain_grad = sum_gain(jnp.concatenate(gains))
    return query_grad[None], total[..., :feat], total[..., feat:], gain_grad


def solution(mesh):
    parts = Mesh(mesh.devices.reshape(-1, NZ, NY, NX), ("clip",) + SEQ)
    return jax.shard_map(
        body,
        mesh=parts,
        in_specs=(
            P("clip", SEQ, None),
            P("clip", SEQ, None),
            P("clip", SEQ),
            P("clip", None),
            P("clip"),
            P("clip", SEQ, None),
            P("clip", SEQ, None),
            P(),
        ),
        out_specs=(P("clip", SEQ, None), P("clip", SEQ, None), P("clip", SEQ, None), P("clip")),
        check_vma=False,
    )
```

time: 2210 us -> 289 us (0.13)
  waiting for transfers between devices: 1620 us -> 88.5 us
  matrix products: 275 us -> 0 us
  blocking collectives: 189 us -> 0 us
  starting transfers between devices: 0.38 us -> 112 us
  Pallas kernels: 0 us -> 50.5 us
  local copies, waits for them, and re-layouts: 61.7 us -> 16.3 us
  other arithmetic: 42.1 us -> 14.3 us
    reduce_scatter x2 -> x0, waiting for transfers between devices: 1380 us -> none  [the longest x1 801 us: body(): lax.psum_scatter(key_flat, 'seq', scatter_dimension=0, tiled=True)]
    dot_general x20 -> x0, matrix products: 275 us -> none  [the longest x4 112 us: tile_grads(): jnp.einsum('htc,thd->chd', dscores, q_normed, preferred_element_type=jnp....]
    all_gather x2 -> x0, waiting for transfers between devices: 237 us -> none  [the longest x1 120 us: body(): lax.all_gather(cap_values[0], 'seq', axis=0, tiled=True)]
    psum x1 -> x0, blocking collectives: 178 us -> none  [body(): gain_total = lax.psum(gain_flat, 'seq')]
    ppermute x0 -> x54, starting transfers between devices: none -> 112 us  [the longest x51 103 us: send(): lax.ppermute(value, axis, [(i, (i + by) % size) for i in range(size)])]
    ppermute x0 -> x54, waiting for transfers between devices: none -> 88.5 us  [the longest x51 80.4 us: send(): lax.ppermute(value, axis, [(i, (i + by) % size) for i in range(size)])]
    pallas_call x0 -> x1, Pallas kernels: none -> 50.5 us  [grads(): pl.pallas_call(functools.partial(kernel, first), grid_spec=pltpu.Prefetch...]
  transfers between devices with their start and end apart: 4 -> 54, of which waited for: 4 -> 25; matrix products, arithmetic and copies ran while one was open for 1% -> 4% of each run, Pallas kernels for 0% -> 0%
where the time goes in v1:
time: 289 us; the launch traced here: 284 us
  starting transfers between devices  112 us (39%)
  waiting for transfers between devices  88.5 us (31%)
  Pallas kernels  50.5 us (17%)
  local copies, waits for them, and re-layouts  16.3 us (6%)
  other arithmetic  14.3 us (5%)
    ppermute x51, starting transfers between devices, send(): lax.ppermute(value, axis, [(i, (i + by) % size) for i in range(size)])  103 us
    ppermute x51, waiting for transfers between devices, send(): lax.ppermute(value, axis, [(i, (i + by) % size) for i in range(size)])  80.4 us
    pallas_call x1, Pallas kernels, grads(): pl.pallas_call(functools.partial(kernel, first), grid_spec=pltpu.Prefetch...  50.5 us
    unnamed x48, local copies, waits for them, and re-layouts  12.9 us
    ppermute x3, starting transfers between devices, sum_gain(): total = total + lax.ppermute(total, 'z', [(i, i ^ step) for i in range(NZ)])  8.91 us
    ppermute x3, waiting for transfers between devices, sum_gain(): total = total + lax.ppermute(total, 'z', [(i, i ^ step) for i in range(NZ)])  8.08 us
    another operation x4, other arithmetic  5.87 us
  transfers between devices with their start and end apart: 54, of which 25 were waited for; matrix products, arithmetic and copies ran while one was open for 4% of the time, Pallas kernels for 0%

profile of v1, /device:TPU:2, one launch (start us, length us, event | category | flops | bytes accessed | tf_op | source)
XLA Modules:
  0.0 283.8 jit_solution(7056805208614199310)
XLA Ops:
  1.5 3.3 %collective-permute-start = (bf16[8,6144]{1,0:T(8,128)(2,1)S(1)}, bf16[8,6144]{1,0:T(8,128)(2,1)S(1)}, u32[]{:S(2)}, u32[]{:S(2)}) collective-permute-start(bf16[8,6144]{1,0:T(8,128)(2,1)S(1)} %pad_maximum_fusion.5), channel_id=1, source_target_pairs={{0,4},{4,0},{1,5},{5,1},{2,6},{6,2},{3,7},{7,3},{8,12},{12,8},{9,1... | collective-permute-start | bytes 294920 | tf_op jit(solution)/shard_map/ppermute | solution.py:27
  4.7 2.9 %collective-permute-done = bf16[8,6144]{1,0:T(8,128)(2,1)S(1)} collective-permute-done((bf16[8,6144]{1,0:T(8,128)(2,1)S(1)}, bf16[8,6144]{1,0:T(8,128)(2,1)S(1)}, u32[]{:S(2)}, u32[]{:S(2)}) %collective-permute-start) | collective-permute-done | bytes 98336 | tf_op jit(solution)/shard_map/ppermute | solution.py:27
  8.5 2.3 collective-permute-start.1
  11.6 1.8 collective-permute-start.3
  13.4 5.9 %collective-permute-start.12 = (bf16[16,3072]{1,0:T(8,128)(2,1)S(1)}, bf16[16,3072]{1,0:T(8,128)(2,1)S(1)}, u32[]{:S(2)}, u32[]{:S(2)}) collective-permute-start(bf16[16,3072]{1,0:T(8,128)(2,1)S(1)} %get-tuple-element.44), channel_id=1, source_target_pairs={{0,56},{8,0},{16,8},{24,16},{32,24},{40,32},{48,40},{56,48},{1,57}... | collective-permute-start | bytes 294920 | tf_op jit(solution)/shard_map/ppermute | solution.py:27
  21.1 5.0 %collective-permute-start.15 = (bf16[16,3072]{1,0:T(8,128)(2,1)S(1)}, bf16[16,3072]{1,0:T(8,128)(2,1)S(1)}, u32[]{:S(2)}, u32[]{:S(2)}) collective-permute-start(bf16[16,3072]{1,0:T(8,128)(2,1)S(1)} %get-tuple-element.44), channel_id=1, source_target_pairs={{0,32},{8,40},{16,48},{24,56},{32,0},{40,8},{48,16},{56,24},{1,33}... | collective-permute-start | bytes 294920 | tf_op jit(solution)/shard_map/ppermute | solution.py:27
  26.2 2.5 collective-permute-start.17
  29.1 1.6 collective-permute-start.18
  30.8 3.8 %collective-permute-done.14 = bf16[16,3072]{1,0:T(8,128)(2,1)S(1)} collective-permute-done((bf16[16,3072]{1,0:T(8,128)(2,1)S(1)}, bf16[16,3072]{1,0:T(8,128)(2,1)S(1)}, u32[]{:S(2)}, u32[]{:S(2)}) %collective-permute-start.14) | collective-permute-done | bytes 98336 | tf_op jit(solution)/shard_map/ppermute | solution.py:27
  34.6 3.3 %collective-permute-start.4 = (bf16[64,3072]{1,0:T(8,128)(2,1)S(1)}, bf16[64,3072]{1,0:T(8,128)(2,1)S(1)}, u32[]{:S(2)}, u32[]{:S(2)}) collective-permute-start(bf16[64,3072]{1,0:T(8,128)(2,1)S(1)} %pad_maximum_fusion.refs_6_), channel_id=1, source_target_pairs={{0,56},{8,0},{16,8},{24,16},{32,24},{40,32},{48,40},{56,48},{1,57}... | collective-permute-start | bytes 1179656 | tf_op jit(solution)/shard_map/ppermute | solution.py:27
  38.6 3.2 %collective-permute-done.17 = bf16[16,3072]{1,0:T(8,128)(2,1)S(1)} collective-permute-done((bf16[16,3072]{1,0:T(8,128)(2,1)S(1)}, bf16[16,3072]{1,0:T(8,128)(2,1)S(1)}, u32[]{:S(2)}, u32[]{:S(2)}) %collective-permute-start.17) | collective-permute-done | bytes 98336 | tf_op jit(solution)/shard_map/ppermute | solution.py:27
  41.9 8.2 %collective-permute-done.7.refs_14_ = bf16[64,3072]{1,0:T(8,128)(2,1)S(1)} collective-permute-done((bf16[64,3072]{1,0:T(8,128)(2,1)S(1)}, bf16[64,3072]{1,0:T(8,128)(2,1)S(1)}, u32[]{:S(2)}, u32[]{:S(2)}) %collective-permute-start.7) | collective-permute-done | bytes 393248 | tf_op jit(solution)/shard_map/ppermute | solution.py:27
  51.1 2.2 collective-permute-start.5
  53.8 2.2 collective-permute-start.20
  55.9 2.5 collective-permute-start.21
  58.5 2.1 collective-permute-done.8.refs_13_
  61.7 2.9 %collective-permute-start.6 = (bf16[64,3072]{1,0:T(8,128)(2,1)S(1)}, bf16[64,3072]{1,0:T(8,128)(2,1)S(1)}, u32[]{:S(2)}, u32[]{:S(2)}) collective-permute-start(bf16[64,3072]{1,0:T(8,128)(2,1)S(1)} %collective-permute-done.5.refs_8_), channel_id=1, source_target_pairs={{0,56},{8,0},{16,8},{24,16},{32,24},{40,32},{48,40},{56,48},{1,57}... | collective-permute-start | bytes 1179656 | tf_op jit(solution)/shard_map/ppermute | solution.py:27
  65.3 4.9 %collective-permute-done.9.refs_12_ = bf16[64,3072]{1,0:T(8,128)(2,1)S(1)} collective-permute-done((bf16[64,3072]{1,0:T(8,128)(2,1)S(1)}, bf16[64,3072]{1,0:T(8,128)(2,1)S(1)}, u32[]{:S(2)}, u32[]{:S(2)}) %collective-permute-start.9) | collective-permute-done | bytes 393248 | tf_op jit(solution)/shard_map/ppermute | solution.py:27
  72.8 2.0 collective-permute-start.11
  77.4 10.7 %collective-permute-done.20.refs_17_ = bf16[128,3072]{1,0:T(8,128)(2,1)S(1)} collective-permute-done((bf16[128,3072]{1,0:T(8,128)(2,1)S(1)}, bf16[128,3072]{1,0:T(8,128)(2,1)S(1)}, u32[]{:S(2)}, u32[]{:S(2)}) %collective-permute-start.20) | collective-permute-done | bytes 786464 | tf_op jit(solution)/shard_map/ppermute | solution.py:27
  89.6 1.9 copy-done.1
  99.1 50.5 %head_grads.1 = (bf16[512,3072]{1,0:T(8,128)(2,1)}, f32[448,3072]{1,0:T(8,128)}, bf16[32,3072]{1,0:T(8,128)(2,1)S(1)}, bf16[32,3072]{1,0:T(8,128)(2,1)S(1)}, f32...) custom-call(s32[1]{0:T(128)} %bitcast.refs_0_, ...), custom_call_target="tpu_custom_call" | custom-call | flops 9663676416 | bytes 31457280 | tf_op jit(solution)/shard_map/head_grads/pallas_call | solution.py:124
  150.9 2.1 collective-permute-start.26
  153.0 2.9 %convert.27 = bf16[448,3072]{1,0:T(8,128)(2,1)S(1)} convert(f32[448,3072]{1,0:T(8,128)} %get-tuple-element.14) | non-fusion elementwise | flops 1376256 | bytes 8257536 | tf_op jit(solution)/shard_map/convert.15
  158.6 3.2 %collective-permute-start.27 = (bf16[64,3072]{1,0:T(8,128)(2,1)}, bf16[64,3072]{1,0:T(8,128)(2,1)S(1)}, u32[]{:S(2)}, u32[]{:S(2)}) collective-permute-start(bf16[64,3072]{1,0:T(8,128)(2,1)} %pad_maximum_fusion.2), channel_id=1, source_target_pairs={{0,56},{8,0},{16,8},{24,16},{32,24},{40,32},{48,40},{56,48},{1,57}... | collective-permute-start | bytes 1179656 | tf_op jit(solution)/shard_map/ppermute | solution.py:27
  166.7 10.9 %collective-permute-start.33 = (bf16[128,3072]{1,0:T(8,128)(2,1)}, bf16[128,3072]{1,0:T(8,128)(2,1)S(1)}, u32[]{:S(2)}, u32[]{:S(2)}) collective-permute-start(bf16[128,3072]{1,0:T(8,128)(2,1)} %copy-done.6), channel_id=1, source_target_pairs={{0,1},{1,2},{2,3},{3,0},{4,5},{5,6},{6,7},{7,4},{8,9},{9,10},{10,1... | collective-permute-start | bytes 2359304 | tf_op jit(solution)/shard_map/ppermute | solution.py:27
  177.6 3.5 %collective-permute-start.34 = (bf16[128,3072]{1,0:T(8,128)(2,1)S(1)}, bf16[128,3072]{1,0:T(8,128)(2,1)S(1)}, u32[]{:S(2)}, u32[]{:S(2)}) collective-permute-start(bf16[128,3072]{1,0:T(8,128)(2,1)S(1)} %copy-done.5), channel_id=1, source_target_pairs={{0,2},{1,3},{2,0},{3,1},{4,6},{5,7},{6,4},{7,5},{8,10},{9,11},{10,... | collective-permute-start | bytes 2359304 | tf_op jit(solution)/shard_map/ppermute | solution.py:27
  182.0 1.6 add_convert_fusion.3
  183.7 3.4 %collective-permute-start.28 = (bf16[64,3072]{1,0:T(8,128)(2,1)S(1)}, bf16[64,3072]{1,0:T(8,128)(2,1)S(1)}, u32[]{:S(2)}, u32[]{:S(2)}) collective-permute-start(bf16[64,3072]{1,0:T(8,128)(2,1)S(1)} %get-tuple-element.29), channel_id=1, source_target_pairs={{0,56},{8,0},{16,8},{24,16},{32,24},{40,32},{48,40},{56,48},{1,57}... | collective-permute-start | bytes 1179656 | tf_op jit(solution)/shard_map/ppermute | solution.py:27
  187.1 10.6 %collective-permute-done.33 = bf16[128,3072]{1,0:T(8,128)(2,1)S(1)} collective-permute-done((bf16[128,3072]{1,0:T(8,128)(2,1)}, bf16[128,3072]{1,0:T(8,128)(2,1)S(1)}, u32[]{:S(2)}, u32[]{:S(2)}) %collective-permute-start.33) | collective-permute-done | bytes 786464 | tf_op jit(solution)/shard_map/ppermute | solution.py:27
  197.7 2.0 collective-permute-done.34
  199.6 15.0 %collective-permute-done.35 = bf16[128,3072]{1,0:T(8,128)(2,1)S(1)} collective-permute-done((bf16[128,3072]{1,0:T(8,128)(2,1)S(1)}, bf16[128,3072]{1,0:T(8,128)(2,1)S(1)}, u32[]{:S(2)}, u32[]{:S(2)}) %collective-permute-start.35) | collective-permute-done | bytes 786464 | tf_op jit(solution)/shard_map/ppermute | solution.py:27
  216.8 3.4 %collective-permute-start.29 = (bf16[64,3072]{1,0:T(8,128)(2,1)S(1)}, bf16[64,3072]{1,0:T(8,128)(2,1)S(1)}, u32[]{:S(2)}, u32[]{:S(2)}) collective-permute-start(bf16[64,3072]{1,0:T(8,128)(2,1)S(1)} %get-tuple-element.27), channel_id=1, source_target_pairs={{0,56},{8,0},{16,8},{24,16},{32,24},{40,32},{48,40},{56,48},{1,57}... | collective-permute-start | bytes 1179656 | tf_op jit(solution)/shard_map/ppermute | solution.py:27
  220.3 4.1 %collective-permute-start.37 = (bf16[16,3072]{1,0:T(8,128)(2,1)S(1)}, bf16[16,3072]{1,0:T(8,128)(2,1)S(1)}, u32[]{:S(2)}, u32[]{:S(2)}) collective-permute-start(bf16[16,3072]{1,0:T(8,128)(2,1)S(1)} %get-tuple-element.40), channel_id=1, source_target_pairs={{0,16},{8,24},{16,32},{24,40},{32,48},{40,56},{48,0},{56,8},{1,17}... | collective-permute-start | bytes 294920 | tf_op jit(solution)/shard_map/ppermute | solution.py:27
  225.2 4.9 %collective-permute-done.25 = bf16[64,3072]{1,0:T(8,128)(2,1)S(1)} collective-permute-done((bf16[64,3072]{1,0:T(8,128)(2,1)S(1)}, bf16[64,3072]{1,0:T(8,128)(2,1)S(1)}, u32[]{:S(2)}, u32[]{:S(2)}) %collective-permute-start.25) | collective-permute-done | bytes 393248 | tf_op jit(solution)/shard_map/ppermute | solution.py:27
  230.0 4.3 %collective-permute-start.39 = (bf16[16,3072]{1,0:T(8,128)(2,1)S(1)}, bf16[16,3072]{1,0:T(8,128)(2,1)S(1)}, u32[]{:S(2)}, u32[]{:S(2)}) collective-permute-start(bf16[16,3072]{1,0:T(8,128)(2,1)S(1)} %get-tuple-element.38), channel_id=1, source_target_pairs={{0,32},{8,40},{16,48},{24,56},{32,0},{40,8},{48,16},{56,24},{1,33}... | collective-permute-start | bytes 294920 | tf_op jit(solution)/shard_map/ppermute | solution.py:27
  235.6 5.4 %collective-permute-start.41 = (bf16[16,3072]{1,0:T(8,128)(2,1)S(1)}, bf16[16,3072]{1,0:T(8,128)(2,1)S(1)}, u32[]{:S(2)}, u32[]{:S(2)}) collective-permute-start(bf16[16,3072]{1,0:T(8,128)(2,1)S(1)} %get-tuple-element.36), channel_id=1, source_target_pairs={{0,48},{8,56},{16,0},{24,8},{32,16},{40,24},{48,32},{56,40},{1,49}... | collective-permute-start | bytes 294920 | tf_op jit(solution)/shard_map/ppermute | solution.py:27
  241.0 3.1 %collective-permute-done.37 = bf16[16,3072]{1,0:T(8,128)(2,1)S(1)} collective-permute-done((bf16[16,3072]{1,0:T(8,128)(2,1)S(1)}, bf16[16,3072]{1,0:T(8,128)(2,1)S(1)}, u32[]{:S(2)}, u32[]{:S(2)}) %collective-permute-start.37) | collective-permute-done | bytes 98336 | tf_op jit(solution)/shard_map/ppermute | solution.py:27
  245.0 2.9 %collective-permute-start.48 = (f32[768]{0:T(1024)S(1)}, f32[768]{0:T(1024)S(1)}, u32[]{:S(2)}, u32[]{:S(2)}) collective-permute-start(f32[768]{0:T(1024)S(1)} %add_add_fusion.2), channel_id=1, source_target_pairs={{0,2},{1,3},{2,0},{3,1},{4,6},{5,7},{6,4},{7,5},{8,10},{9,11},{10,... | collective-permute-start | bytes 9224 | tf_op jit(solution)/shard_map/ppermute | solution.py:27
  248.2 1.6 collective-permute-done.41
  249.9 2.6 collective-permute-start.31
  252.8 4.3 %collective-permute-start.49 = (f32[768]{0:T(1024)S(1)}, f32[768]{0:T(1024)S(1)}, u32[]{:S(2)}, u32[]{:S(2)}) collective-permute-start(f32[768]{0:T(1024)S(1)} %add_add_fusion.2), channel_id=1, source_target_pairs={{0,3},{1,0},{2,1},{3,2},{4,7},{5,4},{6,5},{7,6},{8,11},{9,8},{10,9... | collective-permute-start | bytes 9224 | tf_op jit(solution)/shard_map/ppermute | solution.py:27
  257.2 3.0 %collective-permute-start.43 = (f32[8,6144]{1,0:T(8,128)S(1)}, f32[8,6144]{1,0:T(8,128)S(1)}, u32[]{:S(2)}, u32[]{:S(2)}) collective-permute-start(f32[8,6144]{1,0:T(8,128)S(1)} %pad_maximum_fusion.3), channel_id=1, source_target_pairs={{0,4},{4,0},{1,5},{5,1},{2,6},{6,2},{3,7},{7,3},{8,12},{12,8},{9,1... | collective-permute-start | bytes 589832 | tf_op jit(solution)/shard_map/ppermute | solution.py:27
  260.2 3.4 %collective-permute-start.50 = (f32[768]{0:T(1024)S(1)}, f32[768]{0:T(1024)S(1)}, u32[]{:S(2)}, u32[]{:S(2)}) collective-permute-start(f32[768]{0:T(1024)S(1)} %add_add_fusion.1), channel_id=1, source_target_pairs={{0,8},{8,0},{16,24},{24,16},{32,40},{40,32},{48,56},{56,48},{1,9},... | collective-permute-start | bytes 9224 | tf_op jit(solution)/shard_map/ppermute | solution.py:204
  266.8 2.9 %collective-permute-done.51 = f32[768]{0:T(1024)S(1)} collective-permute-done((f32[768]{0:T(1024)S(1)}, f32[768]{0:T(1024)S(1)}, u32[]{:S(2)}, u32[]{:S(2)}) %collective-permute-start.51) | collective-permute-done | bytes 3104 | tf_op jit(solution)/shard_map/ppermute | solution.py:204
  269.7 3.9 %collective-permute-start.52 = (f32[768]{0:T(1024)S(1)}, f32[768]{0:T(1024)S(1)}, u32[]{:S(2)}, u32[]{:S(2)}) collective-permute-start(f32[768]{0:T(1024)S(1)} %add.347), channel_id=1, source_target_pairs={{0,32},{8,40},{16,48},{24,56},{32,0},{40,8},{48,16},{56,24},{1,33}... | collective-permute-start | bytes 9224 | tf_op jit(solution)/shard_map/ppermute | solution.py:204
  273.6 3.6 %collective-permute-done.52 = f32[768]{0:T(1024)S(1)} collective-permute-done((f32[768]{0:T(1024)S(1)}, f32[768]{0:T(1024)S(1)}, u32[]{:S(2)}, u32[]{:S(2)}) %collective-permute-start.52) | collective-permute-done | bytes 3104 | tf_op jit(solution)/shard_map/ppermute | solution.py:204
  278.3 4.1 %collective-permute-done.53 = f32[768]{0:T(1024)S(1)} collective-permute-done((f32[768]{0:T(1024)S(1)}, f32[768]{0:T(1024)S(1)}, u32[]{:S(2)}, u32[]{:S(2)}) %collective-permute-start.53) | collective-permute-done | bytes 3104 | tf_op jit(solution)/shard_map/ppermute | solution.py:27
  (141 shorter events, 43.4 us)
Async XLA Ops:
  1.5 6.2 %collective-permute-start = (bf16[8,6144]{1,0:T(8,128)(2,1)S(1)}, bf16[8,6144]{1,0:T(8,128)(2,1)S(1)}, u32[]{:S(2)}, u32[]{:S(2)}) collective-permute-start(bf16[8,6144]{1,0:T(8,128)(2,1)S(1)} %pad_maximum_fusion.5), channel_id=1, source_target_pairs={{0,4},{4,0},{1,5},{5,1},{2,6},{6,2},{3,7},{7,3},{8,12},{12,8},{9,1... | collective-permute-start | bytes 294920 | tf_op jit(solution)/shard_map/ppermute | solution.py:27
  8.5 12.1 %collective-permute-start.1 = (bf16[16,3072]{1,0:T(8,128)(2,1)S(1)}, bf16[16,3072]{1,0:T(8,128)(2,1)S(1)}, u32[]{:S(2)}, u32[]{:S(2)}) collective-permute-start(bf16[16,3072]{1,0:T(8,128)(2,1)S(1)} %get-tuple-element.46), channel_id=1, source_target_pairs={{0,3},{1,0},{2,1},{3,2},{4,7},{5,4},{6,5},{7,6},{8,11},{9,8},{10,9... | collective-permute-start | bytes 294920 | tf_op jit(solution)/shard_map/ppermute | solution.py:27
  10.9 10.2 %collective-permute-start.2 = (bf16[16,3072]{1,0:T(8,128)(2,1)S(1)}, bf16[16,3072]{1,0:T(8,128)(2,1)S(1)}, u32[]{:S(2)}, u32[]{:S(2)}) collective-permute-start(bf16[16,3072]{1,0:T(8,128)(2,1)S(1)} %get-tuple-element.46), channel_id=1, source_target_pairs={{0,2},{1,3},{2,0},{3,1},{4,6},{5,7},{6,4},{7,5},{8,10},{9,11},{10,... | collective-permute-start | bytes 294920 | tf_op jit(solution)/shard_map/ppermute | solution.py:27
  11.6 14.6 %collective-permute-start.3 = (bf16[16,3072]{1,0:T(8,128)(2,1)S(1)}, bf16[16,3072]{1,0:T(8,128)(2,1)S(1)}, u32[]{:S(2)}, u32[]{:S(2)}) collective-permute-start(bf16[16,3072]{1,0:T(8,128)(2,1)S(1)} %get-tuple-element.46), channel_id=1, source_target_pairs={{0,1},{1,2},{2,3},{3,0},{4,5},{5,6},{6,7},{7,4},{8,9},{9,10},{10,1... | collective-permute-start | bytes 294920 | tf_op jit(solution)/shard_map/ppermute | solution.py:27
  13.4 12.8 %collective-permute-start.12 = (bf16[16,3072]{1,0:T(8,128)(2,1)S(1)}, bf16[16,3072]{1,0:T(8,128)(2,1)S(1)}, u32[]{:S(2)}, u32[]{:S(2)}) collective-permute-start(bf16[16,3072]{1,0:T(8,128)(2,1)S(1)} %get-tuple-element.44), channel_id=1, source_target_pairs={{0,56},{8,0},{16,8},{24,16},{32,24},{40,32},{48,40},{56,48},{1,57}... | collective-permute-start | bytes 294920 | tf_op jit(solution)/shard_map/ppermute | solution.py:27
  19.2 9.9 %collective-permute-start.13 = (bf16[16,3072]{1,0:T(8,128)(2,1)S(1)}, bf16[16,3072]{1,0:T(8,128)(2,1)S(1)}, u32[]{:S(2)}, u32[]{:S(2)}) collective-permute-start(bf16[16,3072]{1,0:T(8,128)(2,1)S(1)} %get-tuple-element.44), channel_id=1, source_target_pairs={{0,48},{8,56},{16,0},{24,8},{32,16},{40,24},{48,32},{56,40},{1,49}... | collective-permute-start | bytes 294920 | tf_op jit(solution)/shard_map/ppermute | solution.py:27
  20.7 13.9 %collective-permute-start.14 = (bf16[16,3072]{1,0:T(8,128)(2,1)S(1)}, bf16[16,3072]{1,0:T(8,128)(2,1)S(1)}, u32[]{:S(2)}, u32[]{:S(2)}) collective-permute-start(bf16[16,3072]{1,0:T(8,128)(2,1)S(1)} %get-tuple-element.44), channel_id=1, source_target_pairs={{0,40},{8,48},{16,56},{24,0},{32,8},{40,16},{48,24},{56,32},{1,41}... | collective-permute-start | bytes 294920 | tf_op jit(solution)/shard_map/ppermute | solution.py:27
  21.1 13.4 %collective-permute-start.15 = (bf16[16,3072]{1,0:T(8,128)(2,1)S(1)}, bf16[16,3072]{1,0:T(8,128)(2,1)S(1)}, u32[]{:S(2)}, u32[]{:S(2)}) collective-permute-start(bf16[16,3072]{1,0:T(8,128)(2,1)S(1)} %get-tuple-element.44), channel_id=1, source_target_pairs={{0,32},{8,40},{16,48},{24,56},{32,0},{40,8},{48,16},{56,24},{1,33}... | collective-permute-start | bytes 294920 | tf_op jit(solution)/shard_map/ppermute | solution.py:27
  26.2 12.4 %collective-permute-start.16 = (bf16[16,3072]{1,0:T(8,128)(2,1)S(1)}, bf16[16,3072]{1,0:T(8,128)(2,1)S(1)}, u32[]{:S(2)}, u32[]{:S(2)}) collective-permute-start(bf16[16,3072]{1,0:T(8,128)(2,1)S(1)} %get-tuple-element.44), channel_id=1, source_target_pairs={{0,24},{8,32},{16,40},{24,48},{32,56},{40,0},{48,8},{56,16},{1,25}... | collective-permute-start | bytes 294920 | tf_op jit(solution)/shard_map/ppermute | solution.py:27
  26.2 15.6 %collective-permute-start.17 = (bf16[16,3072]{1,0:T(8,128)(2,1)S(1)}, bf16[16,3072]{1,0:T(8,128)(2,1)S(1)}, u32[]{:S(2)}, u32[]{:S(2)}) collective-permute-start(bf16[16,3072]{1,0:T(8,128)(2,1)S(1)} %get-tuple-element.44), channel_id=1, source_target_pairs={{0,16},{8,24},{16,32},{24,40},{32,48},{40,56},{48,0},{56,8},{1,17}... | collective-permute-start | bytes 294920 | tf_op jit(solution)/shard_map/ppermute | solution.py:27
  29.1 24.2 %collective-permute-start.18 = (bf16[16,3072]{1,0:T(8,128)(2,1)S(1)}, bf16[16,3072]{1,0:T(8,128)(2,1)S(1)}, u32[]{:S(2)}, u32[]{:S(2)}) collective-permute-start(bf16[16,3072]{1,0:T(8,128)(2,1)S(1)} %get-tuple-element.44), channel_id=1, source_target_pairs={{0,8},{8,16},{16,24},{24,32},{32,40},{40,48},{48,56},{56,0},{1,9},... | collective-permute-start | bytes 294920 | tf_op jit(solution)/shard_map/ppermute | solution.py:27
  34.6 15.5 %collective-permute-start.7 = (bf16[64,3072]{1,0:T(8,128)(2,1)S(1)}, bf16[64,3072]{1,0:T(8,128)(2,1)S(1)}, u32[]{:S(2)}, u32[]{:S(2)}) collective-permute-start(bf16[64,3072]{1,0:T(8,128)(2,1)S(1)} %pad_maximum_fusion.refs_6_), channel_id=1, source_target_pairs={{0,8},{8,16},{16,24},{24,32},{32,40},{40,48},{48,56},{56,0},{1,9},... | collective-permute-start | bytes 1179656 | tf_op jit(solution)/shard_map/ppermute | solution.py:27
  34.6 16.5 %collective-permute-start.4 = (bf16[64,3072]{1,0:T(8,128)(2,1)S(1)}, bf16[64,3072]{1,0:T(8,128)(2,1)S(1)}, u32[]{:S(2)}, u32[]{:S(2)}) collective-permute-start(bf16[64,3072]{1,0:T(8,128)(2,1)S(1)} %pad_maximum_fusion.refs_6_), channel_id=1, source_target_pairs={{0,56},{8,0},{16,8},{24,16},{32,24},{40,32},{48,40},{56,48},{1,57}... | collective-permute-start | bytes 1179656 | tf_op jit(solution)/shard_map/ppermute | solution.py:27
  50.1 10.5 %collective-permute-start.8 = (bf16[64,3072]{1,0:T(8,128)(2,1)S(1)}, bf16[64,3072]{1,0:T(8,128)(2,1)S(1)}, u32[]{:S(2)}, u32[]{:S(2)}) collective-permute-start(bf16[64,3072]{1,0:T(8,128)(2,1)S(1)} %collective-permute-done.7.refs_14_), channel_id=1, source_target_pairs={{0,8},{8,16},{16,24},{24,32},{32,40},{40,48},{48,56},{56,0},{1,9},... | collective-permute-start | bytes 1179656 | tf_op jit(solution)/shard_map/ppermute | solution.py:27
  51.1 10.6 %collective-permute-start.5 = (bf16[64,3072]{1,0:T(8,128)(2,1)S(1)}, bf16[64,3072]{1,0:T(8,128)(2,1)S(1)}, u32[]{:S(2)}, u32[]{:S(2)}) collective-permute-start(bf16[64,3072]{1,0:T(8,128)(2,1)S(1)} %collective-permute-done.4.refs_7_), channel_id=1, source_target_pairs={{0,56},{8,0},{16,8},{24,16},{32,24},{40,32},{48,40},{56,48},{1,57}... | collective-permute-start | bytes 1179656 | tf_op jit(solution)/shard_map/ppermute | solution.py:27
  53.3 23.2 %collective-permute-start.19 = (bf16[128,3072]{1,0:T(8,128)(2,1)S(1)}, bf16[128,3072]{1,0:T(8,128)(2,1)S(1)}, u32[]{:S(2)}, u32[]{:S(2)}) collective-permute-start(bf16[128,3072]{1,0:T(8,128)(2,1)S(1)} %constant_dynamic-update-slice_fusion.refs_15_), channel_id=1, source_target_pairs={{0,3},{1,0},{2,1},{3,2},{4,7},{5,4},{6,5},{7,6},{8,11},{9,8},{10,9... | collective-permute-start | bytes 2359304 | tf_op jit(solution)/shard_map/ppermute | solution.py:27
  53.8 34.3 %collective-permute-start.20 = (bf16[128,3072]{1,0:T(8,128)(2,1)S(1)}, bf16[128,3072]{1,0:T(8,128)(2,1)S(1)}, u32[]{:S(2)}, u32[]{:S(2)}) collective-permute-start(bf16[128,3072]{1,0:T(8,128)(2,1)S(1)} %constant_dynamic-update-slice_fusion.refs_15_), channel_id=1, source_target_pairs={{0,2},{1,3},{2,0},{3,1},{4,6},{5,7},{6,4},{7,5},{8,10},{9,11},{10,... | collective-permute-start | bytes 2359304 | tf_op jit(solution)/shard_map/ppermute | solution.py:27
  55.9 33.6 %collective-permute-start.21 = (bf16[128,3072]{1,0:T(8,128)(2,1)S(1)}, bf16[128,3072]{1,0:T(8,128)(2,1)}, u32[]{:S(2)}, u32[]{:S(2)}) collective-permute-start(bf16[128,3072]{1,0:T(8,128)(2,1)S(1)} %constant_dynamic-update-slice_fusion.refs_15_), channel_id=1, source_target_pairs={{0,1},{1,2},{2,3},{3,0},{4,5},{5,6},{6,7},{7,4},{8,9},{9,10},{10,1... | collective-permute-start | bytes 2359304 | tf_op jit(solution)/shard_map/ppermute | solution.py:27
  60.6 9.6 %collective-permute-start.9 = (bf16[64,3072]{1,0:T(8,128)(2,1)S(1)}, bf16[64,3072]{1,0:T(8,128)(2,1)S(1)}, u32[]{:S(2)}, u32[]{:S(2)}) collective-permute-start(bf16[64,3072]{1,0:T(8,128)(2,1)S(1)} %collective-permute-done.8.refs_13_), channel_id=1, source_target_pairs={{0,8},{8,16},{16,24},{24,32},{32,40},{40,48},{48,56},{56,0},{1,9},... | collective-permute-start | bytes 1179656 | tf_op jit(solution)/shard_map/ppermute | solution.py:27
  61.7 10.4 %collective-permute-start.6 = (bf16[64,3072]{1,0:T(8,128)(2,1)S(1)}, bf16[64,3072]{1,0:T(8,128)(2,1)S(1)}, u32[]{:S(2)}, u32[]{:S(2)}) collective-permute-start(bf16[64,3072]{1,0:T(8,128)(2,1)S(1)} %collective-permute-done.5.refs_8_), channel_id=1, source_target_pairs={{0,56},{8,0},{16,8},{24,16},{32,24},{40,32},{48,40},{56,48},{1,57}... | collective-permute-start | bytes 1179656 | tf_op jit(solution)/shard_map/ppermute | solution.py:27
  70.9 18.7 %collective-permute-start.10 = (bf16[32,3072]{1,0:T(8,128)(2,1)}, bf16[32,3072]{1,0:T(8,128)(2,1)}, u32[]{:S(2)}, u32[]{:S(2)}) collective-permute-start(bf16[32,3072]{1,0:T(8,128)(2,1)} %slice.135), channel_id=1, source_target_pairs={{0,8},{8,16},{16,24},{24,32},{32,40},{40,48},{48,56},{56,0},{1,9},... | collective-permute-start | bytes 589832 | tf_op jit(solution)/shard_map/ppermute | solution.py:27
  72.8 16.8 %collective-permute-start.11 = (bf16[32,3072]{1,0:T(8,128)(2,1)}, bf16[32,3072]{1,0:T(8,128)(2,1)}, u32[]{:S(2)}, u32[]{:S(2)}) collective-permute-start(bf16[32,3072]{1,0:T(8,128)(2,1)} %slice.136), channel_id=1, source_target_pairs={{0,56},{8,0},{16,8},{24,16},{32,24},{40,32},{48,40},{56,48},{1,57}... | collective-permute-start | bytes 589832 | tf_op jit(solution)/shard_map/ppermute | solution.py:27
  149.7 7.0 %collective-permute-start.22 = (bf16[32,3072]{1,0:T(8,128)(2,1)S(1)}, bf16[32,3072]{1,0:T(8,128)(2,1)S(1)}, u32[]{:S(2)}, u32[]{:S(2)}) collective-permute-start(bf16[32,3072]{1,0:T(8,128)(2,1)S(1)} %get-tuple-element.15), channel_id=1, source_target_pairs={{0,8},{8,16},{16,24},{24,32},{32,40},{40,48},{48,56},{56,0},{1,9},... | collective-permute-start | bytes 589832 | tf_op jit(solution)/shard_map/ppermute | solution.py:27
  150.9 5.8 %collective-permute-start.26 = (bf16[32,3072]{1,0:T(8,128)(2,1)S(1)}, bf16[32,3072]{1,0:T(8,128)(2,1)S(1)}, u32[]{:S(2)}, u32[]{:S(2)}) collective-permute-start(bf16[32,3072]{1,0:T(8,128)(2,1)S(1)} %get-tuple-element.16), channel_id=1, source_target_pairs={{0,56},{8,0},{16,8},{24,16},{32,24},{40,32},{48,40},{56,48},{1,57}... | collective-permute-start | bytes 589832 | tf_op jit(solution)/shard_map/ppermute | solution.py:27
  158.6 23.4 %collective-permute-start.27 = (bf16[64,3072]{1,0:T(8,128)(2,1)}, bf16[64,3072]{1,0:T(8,128)(2,1)S(1)}, u32[]{:S(2)}, u32[]{:S(2)}) collective-permute-start(bf16[64,3072]{1,0:T(8,128)(2,1)} %pad_maximum_fusion.2), channel_id=1, source_target_pairs={{0,56},{8,0},{16,8},{24,16},{32,24},{40,32},{48,40},{56,48},{1,57}... | collective-permute-start | bytes 1179656 | tf_op jit(solution)/shard_map/ppermute | solution.py:27
  162.6 19.3 %collective-permute-start.23 = (bf16[64,3072]{1,0:T(8,128)(2,1)}, bf16[64,3072]{1,0:T(8,128)(2,1)}, u32[]{:S(2)}, u32[]{:S(2)}) collective-permute-start(bf16[64,3072]{1,0:T(8,128)(2,1)} %pad_maximum_fusion.1), channel_id=1, source_target_pairs={{0,8},{8,16},{16,24},{24,32},{32,40},{40,48},{48,56},{56,0},{1,9},... | collective-permute-start | bytes 1179656 | tf_op jit(solution)/shard_map/ppermute | solution.py:27
  163.3 14.3 %collective-permute-start.45 = (f32[768]{0:T(1024)}, f32[768]{0:T(1024)}, u32[]{:S(2)}, u32[]{:S(2)}) collective-permute-start(f32[768]{0:T(1024)} %get-tuple-element.49), channel_id=1, source_target_pairs={{0,128},{64,192},{128,0},{192,64},{1,129},{65,193},{129,1},{193,65... | collective-permute-start | bytes 9224 | tf_op jit(solution)/shard_map/ppermute | solution.py:27
  164.9 16.2 %collective-permute-start.46 = (f32[768]{0:T(1024)}, f32[768]{0:T(1024)}, u32[]{:S(2)}, u32[]{:S(2)}) collective-permute-start(f32[768]{0:T(1024)} %get-tuple-element.50), channel_id=1, source_target_pairs={{0,192},{64,0},{128,64},{192,128},{1,193},{65,1},{129,65},{193,129... | collective-permute-start | bytes 9224 | tf_op jit(solution)/shard_map/ppermute | solution.py:27
  166.7 31.0 %collective-permute-start.33 = (bf16[128,3072]{1,0:T(8,128)(2,1)}, bf16[128,3072]{1,0:T(8,128)(2,1)S(1)}, u32[]{:S(2)}, u32[]{:S(2)}) collective-permute-start(bf16[128,3072]{1,0:T(8,128)(2,1)} %copy-done.6), channel_id=1, source_target_pairs={{0,1},{1,2},{2,3},{3,0},{4,5},{5,6},{6,7},{7,4},{8,9},{9,10},{10,1... | collective-permute-start | bytes 2359304 | tf_op jit(solution)/shard_map/ppermute | solution.py:27
  177.6 22.0 %collective-permute-start.34 = (bf16[128,3072]{1,0:T(8,128)(2,1)S(1)}, bf16[128,3072]{1,0:T(8,128)(2,1)S(1)}, u32[]{:S(2)}, u32[]{:S(2)}) collective-permute-start(bf16[128,3072]{1,0:T(8,128)(2,1)S(1)} %copy-done.5), channel_id=1, source_target_pairs={{0,2},{1,3},{2,0},{3,1},{4,6},{5,7},{6,4},{7,5},{8,10},{9,11},{10,... | collective-permute-start | bytes 2359304 | tf_op jit(solution)/shard_map/ppermute | solution.py:27
  181.1 33.6 %collective-permute-start.35 = (bf16[128,3072]{1,0:T(8,128)(2,1)S(1)}, bf16[128,3072]{1,0:T(8,128)(2,1)S(1)}, u32[]{:S(2)}, u32[]{:S(2)}) collective-permute-start(bf16[128,3072]{1,0:T(8,128)(2,1)S(1)} %copy-done.3), channel_id=1, source_target_pairs={{0,3},{1,0},{2,1},{3,2},{4,7},{5,4},{6,5},{7,6},{8,11},{9,8},{10,9... | collective-permute-start | bytes 2359304 | tf_op jit(solution)/shard_map/ppermute | solution.py:27
  183.6 31.5 %collective-permute-start.24 = (bf16[64,3072]{1,0:T(8,128)(2,1)S(1)}, bf16[64,3072]{1,0:T(8,128)(2,1)S(1)}, u32[]{:S(2)}, u32[]{:S(2)}) collective-permute-start(bf16[64,3072]{1,0:T(8,128)(2,1)S(1)} %get-tuple-element.28), channel_id=1, source_target_pairs={{0,8},{8,16},{16,24},{24,32},{32,40},{40,48},{48,56},{56,0},{1,9},... | collective-permute-start | bytes 1179656 | tf_op jit(solution)/shard_map/ppermute | solution.py:27
  183.7 31.5 %collective-permute-start.28 = (bf16[64,3072]{1,0:T(8,128)(2,1)S(1)}, bf16[64,3072]{1,0:T(8,128)(2,1)S(1)}, u32[]{:S(2)}, u32[]{:S(2)}) collective-permute-start(bf16[64,3072]{1,0:T(8,128)(2,1)S(1)} %get-tuple-element.29), channel_id=1, source_target_pairs={{0,56},{8,0},{16,8},{24,16},{32,24},{40,32},{48,40},{56,48},{1,57}... | collective-permute-start | bytes 1179656 | tf_op jit(solution)/shard_map/ppermute | solution.py:27
  216.7 13.3 %collective-permute-start.25 = (bf16[64,3072]{1,0:T(8,128)(2,1)S(1)}, bf16[64,3072]{1,0:T(8,128)(2,1)S(1)}, u32[]{:S(2)}, u32[]{:S(2)}) collective-permute-start(bf16[64,3072]{1,0:T(8,128)(2,1)S(1)} %get-tuple-element.26), channel_id=1, source_target_pairs={{0,8},{8,16},{16,24},{24,32},{32,40},{40,48},{48,56},{56,0},{1,9},... | collective-permute-start | bytes 1179656 | tf_op jit(solution)/shard_map/ppermute | solution.py:27
  216.8 17.5 %collective-permute-start.29 = (bf16[64,3072]{1,0:T(8,128)(2,1)S(1)}, bf16[64,3072]{1,0:T(8,128)(2,1)S(1)}, u32[]{:S(2)}, u32[]{:S(2)}) collective-permute-start(bf16[64,3072]{1,0:T(8,128)(2,1)S(1)} %get-tuple-element.27), channel_id=1, source_target_pairs={{0,56},{8,0},{16,8},{24,16},{32,24},{40,32},{48,40},{56,48},{1,57}... | collective-permute-start | bytes 1179656 | tf_op jit(solution)/shard_map/ppermute | solution.py:27
  220.2 15.4 %collective-permute-start.36 = (bf16[16,3072]{1,0:T(8,128)(2,1)S(1)}, bf16[16,3072]{1,0:T(8,128)(2,1)S(1)}, u32[]{:S(2)}, u32[]{:S(2)}) collective-permute-start(bf16[16,3072]{1,0:T(8,128)(2,1)S(1)} %get-tuple-element.34), channel_id=1, source_target_pairs={{0,8},{8,16},{16,24},{24,32},{32,40},{40,48},{48,56},{56,0},{1,9},... | collective-permute-start | bytes 294920 | tf_op jit(solution)/shard_map/ppermute | solution.py:27
  220.3 23.8 %collective-permute-start.37 = (bf16[16,3072]{1,0:T(8,128)(2,1)S(1)}, bf16[16,3072]{1,0:T(8,128)(2,1)S(1)}, u32[]{:S(2)}, u32[]{:S(2)}) collective-permute-start(bf16[16,3072]{1,0:T(8,128)(2,1)S(1)} %get-tuple-element.40), channel_id=1, source_target_pairs={{0,16},{8,24},{16,32},{24,40},{32,48},{40,56},{48,0},{56,8},{1,17}... | collective-permute-start | bytes 294920 | tf_op jit(solution)/shard_map/ppermute | solution.py:27
  224.4 19.8 %collective-permute-start.38 = (bf16[16,3072]{1,0:T(8,128)(2,1)S(1)}, bf16[16,3072]{1,0:T(8,128)(2,1)S(1)}, u32[]{:S(2)}, u32[]{:S(2)}) collective-permute-start(bf16[16,3072]{1,0:T(8,128)(2,1)S(1)} %get-tuple-element.39), channel_id=1, source_target_pairs={{0,24},{8,32},{16,40},{24,48},{32,56},{40,0},{48,8},{56,16},{1,25}... | collective-permute-start | bytes 294920 | tf_op jit(solution)/shard_map/ppermute | solution.py:27
  230.0 14.9 %collective-permute-start.39 = (bf16[16,3072]{1,0:T(8,128)(2,1)S(1)}, bf16[16,3072]{1,0:T(8,128)(2,1)S(1)}, u32[]{:S(2)}, u32[]{:S(2)}) collective-permute-start(bf16[16,3072]{1,0:T(8,128)(2,1)S(1)} %get-tuple-element.38), channel_id=1, source_target_pairs={{0,32},{8,40},{16,48},{24,56},{32,0},{40,8},{48,16},{56,24},{1,33}... | collective-permute-start | bytes 294920 | tf_op jit(solution)/shard_map/ppermute | solution.py:27
  234.3 13.5 %collective-permute-start.40 = (bf16[16,3072]{1,0:T(8,128)(2,1)S(1)}, bf16[16,3072]{1,0:T(8,128)(2,1)S(1)}, u32[]{:S(2)}, u32[]{:S(2)}) collective-permute-start(bf16[16,3072]{1,0:T(8,128)(2,1)S(1)} %get-tuple-element.37), channel_id=1, source_target_pairs={{0,40},{8,48},{16,56},{24,0},{32,8},{40,16},{48,24},{56,32},{1,41}... | collective-permute-start | bytes 294920 | tf_op jit(solution)/shard_map/ppermute | solution.py:27
  235.6 14.2 %collective-permute-start.41 = (bf16[16,3072]{1,0:T(8,128)(2,1)S(1)}, bf16[16,3072]{1,0:T(8,128)(2,1)S(1)}, u32[]{:S(2)}, u32[]{:S(2)}) collective-permute-start(bf16[16,3072]{1,0:T(8,128)(2,1)S(1)} %get-tuple-element.36), channel_id=1, source_target_pairs={{0,48},{8,56},{16,0},{24,8},{32,16},{40,24},{48,32},{56,40},{1,49}... | collective-permute-start | bytes 294920 | tf_op jit(solution)/shard_map/ppermute | solution.py:27
  244.2 8.4 %collective-permute-start.42 = (bf16[16,3072]{1,0:T(8,128)(2,1)S(1)}, bf16[16,3072]{1,0:T(8,128)(2,1)S(1)}, u32[]{:S(2)}, u32[]{:S(2)}) collective-permute-start(bf16[16,3072]{1,0:T(8,128)(2,1)S(1)} %get-tuple-element.35), channel_id=1, source_target_pairs={{0,56},{8,0},{16,8},{24,16},{32,24},{40,32},{48,40},{56,48},{1,57}... | collective-permute-start | bytes 294920 | tf_op jit(solution)/shard_map/ppermute | solution.py:27
  244.2 16.0 %collective-permute-start.47 = (f32[768]{0:T(1024)S(1)}, f32[768]{0:T(1024)S(1)}, u32[]{:S(2)}, u32[]{:S(2)}) collective-permute-start(f32[768]{0:T(1024)S(1)} %add_add_fusion.2), channel_id=1, source_target_pairs={{0,1},{1,2},{2,3},{3,0},{4,5},{5,6},{6,7},{7,4},{8,9},{9,10},{10,1... | collective-permute-start | bytes 9224 | tf_op jit(solution)/shard_map/ppermute | solution.py:27
  245.0 15.2 %collective-permute-start.48 = (f32[768]{0:T(1024)S(1)}, f32[768]{0:T(1024)S(1)}, u32[]{:S(2)}, u32[]{:S(2)}) collective-permute-start(f32[768]{0:T(1024)S(1)} %add_add_fusion.2), channel_id=1, source_target_pairs={{0,2},{1,3},{2,0},{3,1},{4,6},{5,7},{6,4},{7,5},{8,10},{9,11},{10,... | collective-permute-start | bytes 9224 | tf_op jit(solution)/shard_map/ppermute | solution.py:27
  249.9 7.2 %collective-permute-start.31 = (bf16[16,3072]{1,0:T(8,128)(2,1)S(1)}, bf16[16,3072]{1,0:T(8,128)(2,1)S(1)}, u32[]{:S(2)}, u32[]{:S(2)}) collective-permute-start(bf16[16,3072]{1,0:T(8,128)(2,1)S(1)} %get-tuple-element.43), channel_id=1, source_target_pairs={{0,2},{1,3},{2,0},{3,1},{4,6},{5,7},{6,4},{7,5},{8,10},{9,11},{10,... | collective-permute-start | bytes 294920 | tf_op jit(solution)/shard_map/ppermute | solution.py:27
  252.8 7.4 %collective-permute-start.49 = (f32[768]{0:T(1024)S(1)}, f32[768]{0:T(1024)S(1)}, u32[]{:S(2)}, u32[]{:S(2)}) collective-permute-start(f32[768]{0:T(1024)S(1)} %add_add_fusion.2), channel_id=1, source_target_pairs={{0,3},{1,0},{2,1},{3,2},{4,7},{5,4},{6,5},{7,6},{8,11},{9,8},{10,9... | collective-permute-start | bytes 9224 | tf_op jit(solution)/shard_map/ppermute | solution.py:27
  257.2 25.7 %collective-permute-start.43 = (f32[8,6144]{1,0:T(8,128)S(1)}, f32[8,6144]{1,0:T(8,128)S(1)}, u32[]{:S(2)}, u32[]{:S(2)}) collective-permute-start(f32[8,6144]{1,0:T(8,128)S(1)} %pad_maximum_fusion.3), channel_id=1, source_target_pairs={{0,4},{4,0},{1,5},{5,1},{2,6},{6,2},{3,7},{7,3},{8,12},{12,8},{9,1... | collective-permute-start | bytes 589832 | tf_op jit(solution)/shard_map/ppermute | solution.py:27
  269.7 7.5 %collective-permute-start.52 = (f32[768]{0:T(1024)S(1)}, f32[768]{0:T(1024)S(1)}, u32[]{:S(2)}, u32[]{:S(2)}) collective-permute-start(f32[768]{0:T(1024)S(1)} %add.347), channel_id=1, source_target_pairs={{0,32},{8,40},{16,48},{24,56},{32,0},{40,8},{48,16},{56,24},{1,33}... | collective-permute-start | bytes 9224 | tf_op jit(solution)/shard_map/ppermute | solution.py:204
  (27 other events, 224.5 us)

commit v2 on v1

v2 whole, which is shorter than its diff:
```python
import functools
import math

import jax
import jax.numpy as jnp
from jax import lax
from jax.experimental import pallas as pl
from jax.experimental.pallas import tpu as pltpu
from jax.sharding import Mesh, PartitionSpec as P

HEAD_DIM = 128
ROWS = 8
NZ, NY, NX = 8, 2, 4
SEQ = ("z", "yh", "x")
F32, BF16 = jnp.float32, jnp.bfloat16
NT = (((1,), (1,)), ((), ()))
TN = (((0,), (0,)), ((), ()))
NN = (((1,), (0,)), ((), ()))


def dot(a, b, dims):
    return lax.dot_general(a, b, dims, preferred_element_type=F32)


def send(value, axis, size, by):
    return lax.ppermute(value, axis, [(i, (i + by) % size) for i in range(size)])


NXY = NX * NY
ZROWS = NXY * ROWS
XROWS = NZ * ROWS
UNIT = NY * ROWS
PART = XROWS + ROWS
CHUNKS = (12, 12)
PACK = 2
FAR, HALF = NZ // 2, ZROWS // 2
EARLY = (FAR * ZROWS, FAR * ZROWS + HALF, FAR * ZROWS - HALF, (FAR + 1) * ZROWS)
KEPT = 2 + len(EARLY)


def two_terms(value, high):
    row = lax.broadcasted_iota(jnp.int32, (ROWS, value.shape[1]), 0)
    return jnp.where(row == 0, high, jnp.where(row == 1, value - high, 0.0))


def kernel(first, *refs):
    (scalar_ref, q_ref, d_ref, gain_ref, pos_ref, bias_ref, v_ref) = refs[:7]
    k_refs = refs[7:16]
    rest = refs[16 + (0 if first else KEPT):]
    qg_ref, dk_ref, *dk_refs, dv_ref, perm, bias = rest
    at_x = scalar_ref[1]
    rows = q_ref.shape[0]
    count = scalar_ref[0]
    scale = 1.0 / math.sqrt(HEAD_DIM)

    @pl.when(pl.program_id(0) == 0)
    def _():
        place = lax.broadcasted_iota(jnp.int32, (rows, rows), 0)
        row = lax.broadcasted_iota(jnp.int32, (rows, rows), 1)
        hit = (place == pos_ref[...]) & (row < count)
        perm[...] = jnp.where(hit, 1.0, 0.0).astype(BF16)
        bias[...] = jnp.broadcast_to(bias_ref[...], bias.shape)

    xs = [lax.rem(at_x + dx, NX) for dx in range(NX)]
    wide = NY * XROWS
    v = [v_ref[pl.ds(pl.multiple_of(x * wide, wide), wide)].astype(F32) for x in xs]
    v_all = jnp.concatenate(
        [
            v[dx][(y * NZ + dz) * ROWS : (y * NZ + dz + 1) * ROWS]
            for dz in range(NZ) for dx in range(NX) for y in range(NY)
        ],
        axis=0,
    ).astype(BF16)
    k_all = jnp.concatenate([r[...] for r in k_refs], axis=0)
    mask = jnp.concatenate([bias[...]] * (rows // HEAD_DIM), axis=1)
    row = lax.broadcasted_iota(jnp.int32, (rows, HEAD_DIM), 0)
    columns = [slice(n * HEAD_DIM, (n + 1) * HEAD_DIM) for n in range(PACK)]
    before = []
    for at in columns:
        gain, k, v = gain_ref[:, at], k_all[:, at], v_all[:, at]
        qf = q_ref[:, at].astype(F32)
        inv = lax.rsqrt(jnp.mean(qf * qf, axis=-1, keepdims=True) + 1e-6)
        normed = qf * inv
        qn = (normed * gain).astype(BF16)
        live = jnp.where(row < count, d_ref[:, at].astype(F32), 0.0).astype(BF16)
        before.append((gain, k, inv, normed, qn, live, dot(k, qn, NT), dot(v, live, NT)))
    between = []
    for *_, s, dp in before:
        s = s * (scale * math.log2(math.e)) + mask
        e = jnp.exp2(s - jnp.max(s, axis=0, keepdims=True))
        p = e * (1.0 / jnp.sum(e, axis=0, keepdims=True))
        delta = jnp.sum(p * dp, axis=0, keepdims=True)
        between.append((p.astype(BF16), (p * ((dp - delta) * scale)).astype(BF16)))
    dks, dvs, groups = [], [], []
    for at, (gain, k, inv, normed, qn, live, _, _), (p, ds) in zip(columns, before, between):
        dks.append(dot(ds, qn, NN))
        dvs.append(dot(p, live, NN))
        dn = dot(k, ds, TN).T
        prod = dn * normed
        total = jnp.sum(prod, axis=0, keepdims=True)
        groups.append(two_terms(total, total.astype(BF16).astype(F32)))
        mean = jnp.mean(prod * gain, axis=-1, keepdims=True)
        dx_rows = inv * (gain * dn - normed * mean)
        qg_ref[:, at] = dot(perm[...], dx_rows.astype(BF16), NN).astype(BF16)
    dk, dv, group = (jnp.concatenate(parts, axis=1) for parts in (dks, dvs, groups))
    dk_ref[...] = dk
    for ref, at in zip(dk_refs, EARLY):
        ref[...] = dk[at : at + HALF].astype(BF16)
    for dx, x in enumerate(xs):
        at = [[dz * ZROWS + (dx * NY + y) * ROWS for dz in range(NZ)] for y in range(NY)]
        part = jnp.concatenate([p for y in range(NY) for p in [dv[k : k + ROWS] for k in at[y]] + [group]], axis=0)
        dv_ref[pl.ds(pl.multiple_of(x * NY * PART, UNIT), NY * PART)] = part.astype(BF16)


def grads(head, heads, scalars, q, d, gain, pos, bias, v, k_parts, before):
    rows, feat = q.shape
    cap = bias.shape[0]
    cols = heads * HEAD_DIM
    at = lambda i, *_: (0, head // PACK + i)
    here = lambda i, *_: (0, i)
    fixed = lambda i, *_: (0, 0)
    outs = [
        (rows, feat, BF16, at),
        (cap, feat, F32, at),
        *[(HALF, feat, BF16, at)] * len(EARLY),
        (NXY * PART, cols, BF16, here),
    ]
    first = before is None
    in_specs = [
        pl.BlockSpec((rows, PACK * HEAD_DIM), at),
        pl.BlockSpec((rows, PACK * HEAD_DIM), at),
        pl.BlockSpec((1, PACK * HEAD_DIM), at),
        pl.BlockSpec(pos.shape, fixed),
        pl.BlockSpec(bias.shape, fixed),
        pl.BlockSpec((cap, PACK * HEAD_DIM), here),
    ] + [pl.BlockSpec((part.shape[0], PACK * HEAD_DIM), at) for part in k_parts]
    args = [scalars, q, d, gain, pos, bias, v, *k_parts]
    aliases = {}
    if not first:
        in_specs += [pl.BlockSpec(memory_space=pl.ANY)] * KEPT
        aliases = {len(args) + n: n for n in range(KEPT)}
        args += before
    scores = heads * rows * cap
    return pl.pallas_call(
        functools.partial(kernel, first),
        grid_spec=pltpu.PrefetchScalarGridSpec(
            num_scalar_prefetch=1,
            grid=(heads // PACK,),
            in_specs=in_specs,
            out_specs=[pl.BlockSpec((r, PACK * HEAD_DIM), where) for r, _, _, where in outs],
            scratch_shapes=[pltpu.VMEM((rows, rows), BF16), pltpu.VMEM((cap, HEAD_DIM), F32)],
        ),
        out_shape=[jax.ShapeDtypeStruct((r, c), t) for r, c, t, _ in outs],
        input_output_aliases=aliases,
        compiler_params=pltpu.CompilerParams(vmem_limit_bytes=60 * 1024 * 1024),
        cost_estimate=pl.CostEstimate(
            flops=12 * scores * HEAD_DIM, bytes_accessed=heads * 5_500_000, transcendentals=scores
        ),
        name="head_grads",
    )(*args)


def exchange(blocks, axes):
    return lax.all_to_all(blocks, axes, 0, 0, tiled=True)


def spread(rows, axes, count):
    return exchange(jnp.broadcast_to(rows[None], (count, *rows.shape)), axes).reshape(-1, rows.shape[1])


def add_up(rows, count):
    blocks = rows.reshape(count, rows.shape[0] // count, rows.shape[1])
    return sum(blocks[i].astype(F32) for i in range(count))


def roll_rows(value, start):
    return lax.dynamic_slice_in_dim(jnp.concatenate([value, value], axis=0), start, value.shape[0])


def both_ways(ahead, behind):
    return send(ahead, "z", NZ, 1), send(behind, "z", NZ, -1)


def gather(cap_keys, cap_values):
    yh = lax.axis_index("yh")
    other = send(cap_keys, "yh", NY, 1)
    keys = [jnp.where(yh == y, cap_keys, other) for y in range(NY)]
    keys = jnp.concatenate(keys, axis=0)
    keys = jnp.concatenate([keys] + [send(keys, "x", NX, -dx) for dx in range(1, NX)], axis=0)
    values = spread(cap_values, "z", NZ)
    values = roll_rows(values, lax.axis_index("z") * ROWS)
    parts = {0: keys}
    ahead = behind = keys
    for step in range(1, FAR):
        ahead, behind = both_ways(ahead, behind)
        parts[NZ - step], parts[step] = ahead, behind
    ahead, behind = both_ways(ahead[:HALF], behind[HALF:])
    pieces = [parts[dz] for dz in range(FAR)] + [ahead, behind] + [parts[dz] for dz in range(FAR + 1, NZ)]
    return pieces, values


def scatter(terms, far_a, far_b, three_b, five_a, value_parts, dv):
    term = lambda dz: terms[dz * ZROWS : (dz + 1) * ZROWS]
    wide = lambda part: part.astype(F32)
    tie = lax.optimization_barrier
    ahead, behind = both_ways(far_a, far_b)
    ahead, behind, first = tie((ahead, behind, value_parts))
    second = exchange(dv, ("x", "yh"))
    ahead = (wide(ahead) + term(FAR - 1)[:HALF]).astype(BF16)
    behind = (wide(behind) + term(FAR + 1)[HALF:]).astype(BF16)
    ahead, behind = both_ways(
        jnp.concatenate([ahead, three_b], axis=0), jnp.concatenate([five_a, behind], axis=0)
    )
    ahead, behind = both_ways(
        (wide(ahead) + term(2)).astype(BF16), (wide(behind) + term(NZ - 2)).astype(BF16)
    )
    ahead, behind, second = tie((ahead, behind, second))
    ahead, behind = both_ways(
        (wide(ahead) + term(1)).astype(BF16), (wide(behind) + term(NZ - 1)).astype(BF16)
    )
    value_sum = jnp.concatenate([add_up(first, NXY), add_up(second, NXY)], axis=1)
    gain = value_sum[XROWS : XROWS + 1] + value_sum[XROWS + 1 : XROWS + 2]
    gain = two_terms(gain, lax.reduce_precision(gain, 8, 7))
    value_sum = roll_rows(value_sum[:XROWS], (NZ - lax.axis_index("z")) % NZ * ROWS)
    value_sum = value_sum.reshape(NZ, ROWS, -1)
    blocks = jnp.concatenate([value_sum, jnp.broadcast_to(gain[None], value_sum.shape)], axis=1)
    blocks = blocks.astype(BF16).reshape(2 * XROWS, -1)
    value_grad = add_up(exchange(blocks, "z"), NZ)
    key_sum = term(0) + wide(ahead) + wide(behind)
    parts = [
        send(key_sum[dx * UNIT : (dx + 1) * UNIT].astype(BF16), "x", NX, dx) for dx in range(1, NX)
    ]
    key_sum = roll_rows(key_sum[:UNIT] + sum(wide(part) for part in parts), lax.axis_index("yh") * ROWS)
    key_grad = key_sum[:ROWS] + send(key_sum[ROWS:], "yh", NY, 1)
    clips, mine = lax.axis_size("clip"), lax.axis_index("clip")
    gain = value_grad[ROWS : ROWS + 1] + value_grad[ROWS + 1 : ROWS + 2]
    gain = roll_rows(gain.reshape(clips, -1), mine)
    gain = gain[:1] + sum(send(gain[by : by + 1], "clip", clips, by) for by in range(1, clips))
    return key_grad, value_grad[:ROWS], gain[0]


def body(queries, grad_out, kept_pos, kept_count, caption_len, cap_keys, cap_values, query_gain):
    z, yh, x = (lax.axis_index(name) for name in SEQ)
    feat = queries.shape[-1]
    cap = cap_keys.shape[1] * NZ * NY * NX
    count = lax.dynamic_index_in_dim(kept_count[0], (z * NY + yh) * NX + x, keepdims=False)
    scalars = jnp.stack([count, x])
    slot = jnp.arange(cap, dtype=jnp.int32)[:, None]
    at_z, at_x, at_y = (z + slot // ZROWS) % NZ, (x + slot // UNIT) % NX, slot // ROWS % NY
    caption = ((at_z * NY + at_y) * NX + at_x) * ROWS + slot % ROWS
    bias = jnp.where(caption < caption_len[0], 0.0, -jnp.inf).astype(F32)
    key_parts, values = gather(cap_keys[0], cap_values[0])
    run = lambda head, heads, v, before: grads(
        head, heads, scalars, queries[0], grad_out[0], query_gain[None], kept_pos, bias, v, key_parts,
        before,
    )
    split = CHUNKS[0] * HEAD_DIM
    v1, v2 = (spread(part, ("x", "yh"), NXY) for part in (values[:, :split], values[:, split:]))
    *kept, dv1 = run(0, CHUNKS[0], v1, None)
    *kept, dv1, v2 = lax.optimization_barrier((*kept, dv1, v2))
    *kept, dv2 = run(CHUNKS[0], CHUNKS[1], v2, kept)
    query_grad, *terms = kept
    key_grad, value_grad, gain_grad = scatter(*terms, exchange(dv1, ("x", "yh")), dv2)
    return query_grad[None], key_grad.astype(BF16)[None], value_grad.astype(BF16)[None], gain_grad


def solution(mesh):
    parts = Mesh(mesh.devices.reshape(-1, NZ, NY, NX), ("clip",) + SEQ)
    return jax.shard_map(
        body,
        mesh=parts,
        in_specs=(
            P("clip", SEQ, None),
            P("clip", SEQ, None),
            P("clip", SEQ),
            P("clip", None),
            P("clip"),
            P("clip", SEQ, None),
            P("clip", SEQ, None),
            P(),
        ),
        out_specs=(P("clip", SEQ, None), P("clip", SEQ, None), P("clip", SEQ, None), P("clip")),
        check_vma=False,
    )
```

time: 289 us -> 205 us (0.71); the launches traced: 284 us -> 204 us
  starting transfers between devices: 112 us -> 80.3 us
  waiting for transfers between devices: 88.5 us -> 57.8 us
  Pallas kernels: 50.5 us -> 38.8 us
  local copies, waits for them, and re-layouts: 16.3 us -> 7.77 us
  other arithmetic: 14.3 us -> 17.5 us
    ppermute x51 -> x27, starting transfers between devices: 103 us -> 43.7 us  [send(): lax.ppermute(value, axis, [(i, (i + by) % size) for i in range(size)])]
    ppermute x51 -> x27, waiting for transfers between devices: 80.4 us -> 33.7 us  [send(): lax.ppermute(value, axis, [(i, (i + by) % size) for i in range(size)])]
    all_to_all x0 -> x6, starting transfers between devices: none -> 36.7 us  [exchange(): return lax.all_to_all(blocks, axes, 0, 0, tiled=True)]
    all_to_all x0 -> x6, waiting for transfers between devices: none -> 24.1 us  [exchange(): return lax.all_to_all(blocks, axes, 0, 0, tiled=True)]
    pallas_call x1 -> x2, Pallas kernels: 50.5 us -> 38.8 us  [grads(): pl.pallas_call(functools.partial(kernel, first), grid_spec=pltpu.Prefetch...]
    unnamed x48 -> x22, local copies, waits for them, and re-layouts: 12.9 us -> 2.14 us
    ppermute x3 -> x0, starting transfers between devices: 8.91 us -> none  [sum_gain(): total = total + lax.ppermute(total, 'z', [(i, i ^ step) for i in range(NZ)])]
    ppermute x3 -> x0, waiting for transfers between devices: 8.08 us -> none  [sum_gain(): total = total + lax.ppermute(total, 'z', [(i, i ^ step) for i in range(NZ)])]
  transfers between devices with their start and end apart: 54 -> 33, of which waited for: 25 -> 13; matrix products, arithmetic and copies ran while one was open for 4% -> 9% of each run, Pallas kernels for 0% -> 19%
where the time goes in v2:
time: 205 us; the launch traced here: 204 us
  starting transfers between devices  80.3 us (39%)
  waiting for transfers between devices  57.8 us (28%)
  Pallas kernels  38.8 us (19%)
  other arithmetic  17.5 us (9%)
  local copies, waits for them, and re-layouts  7.77 us (4%)
    ppermute x27, starting transfers between devices, send(): lax.ppermute(value, axis, [(i, (i + by) % size) for i in range(size)])  43.7 us
    pallas_call x2, Pallas kernels, grads(): pl.pallas_call(functools.partial(kernel, first), grid_spec=pltpu.Prefetch...  38.8 us
    all_to_all x6, starting transfers between devices, exchange(): return lax.all_to_all(blocks, axes, 0, 0, tiled=True)  36.7 us
    ppermute x27, waiting for transfers between devices, send(): lax.ppermute(value, axis, [(i, (i + by) % size) for i in range(size)])  33.7 us
    all_to_all x6, waiting for transfers between devices, exchange(): return lax.all_to_all(blocks, axes, 0, 0, tiled=True)  24.1 us
    broadcast_in_dim x3, local copies, waits for them, and re-layouts, spread(): jnp.broadcast_to(rows[None], (count, *rows.shape))  4.27 us
  transfers between devices with their start and end apart: 33, of which 13 were waited for; matrix products, arithmetic and copies ran while one was open for 9% of the time, Pallas kernels for 19%

profile of v2, /device:TPU:2, one launch (start us, length us, event | category | flops | bytes accessed | tf_op | source)
XLA Modules:
  0.0 204.0 jit_solution(6036699440998078828)
XLA Ops:
  0.6 3.3 %collective-permute-start = (bf16[8,3072]{1,0:T(8,128)(2,1)}, bf16[8,3072]{1,0:T(8,128)(2,1)S(1)}, u32[]{:S(2)}, u32[]{:S(2)}) collective-permute-start(bf16[8,3072]{1,0:T(8,128)(2,1)} %bitcast.39), channel_id=1, source_target_pairs={{0,4},{4,0},{1,5},{5,1},{2,6},{6,2},{3,7},{7,3},{8,12},{12,8},{9,1... | collective-permute-start | bytes 147464 | tf_op jit(solution)/shard_map/ppermute | solution.py:26
  3.9 1.6 broadcast_in_dim.71
  5.5 8.5 %all-to-all-start = ((bf16[8,8,3072]{2,1,0:T(8,128)(2,1)}), bf16[8,8,3072]{2,1,0:T(8,128)(2,1)S(1)}, u32[]{:S(2)}, u32[]{:S(2)}) async-start(bf16[8,8,3072]{2,1,0:T(8,128)(2,1)} %broadcast_in_dim.71), calls=%async_computation | async-start | bytes 786432 | tf_op jit(solution)/shard_map/all_to_all | solution.py:164
  14.0 0.8 constant_dynamic-update-slice_fusion.4
  14.8 0.8 constant_dynamic-update-slice_fusion.3
  16.2 2.4 %collective-permute-start.2 = (bf16[16,3072]{1,0:T(8,128)(2,1)S(1)}, bf16[16,3072]{1,0:T(8,128)(2,1)S(1)}, u32[]{:S(2)}, u32[]{:S(2)}) collective-permute-start(bf16[16,3072]{1,0:T(8,128)(2,1)S(1)} %pad_maximum_fusion.3), channel_id=1, source_target_pairs={{0,2},{1,3},{2,0},{3,1},{4,6},{5,7},{6,4},{7,5},{8,10},{9,11},{10,... | collective-permute-start | bytes 294920 | tf_op jit(solution)/shard_map/ppermute | solution.py:26
  18.7 1.8 collective-permute-start.3
  20.5 7.9 %all-to-all-done = bf16[8,8,3072]{2,1,0:T(8,128)(2,1)S(1)} async-done(((bf16[8,8,3072]{2,1,0:T(8,128)(2,1)}), bf16[8,8,3072]{2,1,0:T(8,128)(2,1)S(1)}, u32[]{:S(2)}, u32[]{:S(2)}) %all-to-all-start) | async-done | bytes 393248 | tf_op jit(solution)/shard_map/all_to_all | solution.py:164
  28.6 1.3 broadcast_in_dim.72
  29.9 4.8 %all-to-all-start.1 = ((bf16[8,64,1536]{2,1,0:T(8,128)(2,1)}), bf16[8,64,1536]{2,1,0:T(8,128)(2,1)S(1)}, u32[]{:S(2)}, u32[]{:S(2)}) async-start(bf16[8,64,1536]{2,1,0:T(8,128)(2,1)} %broadcast_in_dim.72), calls=%async_computation.1 | async-start | bytes 3145728 | tf_op jit(solution)/shard_map/all_to_all | solution.py:164
  35.4 2.7 %collective-permute-start.4 = (bf16[64,3072]{1,0:T(8,128)(2,1)S(1)}, bf16[64,3072]{1,0:T(8,128)(2,1)}, u32[]{:S(2)}, u32[]{:S(2)}) collective-permute-start(bf16[64,3072]{1,0:T(8,128)(2,1)S(1)} %constant_dynamic-update-slice_fusion.refs_7_), channel_id=1, source_target_pairs={{0,56},{8,0},{16,8},{24,16},{32,24},{40,32},{48,40},{56,48},{1,57}... | collective-permute-start | bytes 1179656 | tf_op jit(solution)/shard_map/ppermute | solution.py:26
  38.1 6.8 %collective-permute-done.7.refs_15_ = bf16[64,3072]{1,0:T(8,128)(2,1)} collective-permute-done((bf16[64,3072]{1,0:T(8,128)(2,1)S(1)}, bf16[64,3072]{1,0:T(8,128)(2,1)}, u32[]{:S(2)}, u32[]{:S(2)}) %collective-permute-start.7) | collective-permute-done | bytes 393248 | tf_op jit(solution)/shard_map/ppermute | solution.py:26
  44.9 3.2 %collective-permute-start.5 = (bf16[64,3072]{1,0:T(8,128)(2,1)}, bf16[64,3072]{1,0:T(8,128)(2,1)}, u32[]{:S(2)}, u32[]{:S(2)}) collective-permute-start(bf16[64,3072]{1,0:T(8,128)(2,1)} %collective-permute-done.4.refs_8_), channel_id=1, source_target_pairs={{0,56},{8,0},{16,8},{24,16},{32,24},{40,32},{48,40},{56,48},{1,57}... | collective-permute-start | bytes 1179656 | tf_op jit(solution)/shard_map/ppermute | solution.py:26
  48.1 5.5 %all-to-all-done.1 = bf16[8,64,1536]{2,1,0:T(8,128)(2,1)S(1)} async-done(((bf16[8,64,1536]{2,1,0:T(8,128)(2,1)}), bf16[8,64,1536]{2,1,0:T(8,128)(2,1)S(1)}, u32[]{:S(2)}, u32[]{:S(2)}) %all-to-all-start.1) | async-done | bytes 1572896 | tf_op jit(solution)/shard_map/all_to_all | solution.py:164
  53.6 1.4 broadcast_in_dim.73
  55.3 5.4 %all-to-all-start.2 = ((bf16[8,64,1536]{2,1,0:T(8,128)(2,1)}), bf16[8,64,1536]{2,1,0:T(8,128)(2,1)S(1)}, u32[]{:S(2)}, u32[]{:S(2)}) async-start(bf16[8,64,1536]{2,1,0:T(8,128)(2,1)} %broadcast_in_dim.73), calls=%async_computation.2 | async-start | bytes 3145728 | tf_op jit(solution)/shard_map/all_to_all | solution.py:164
  60.7 3.2 %collective-permute-start.6 = (bf16[64,3072]{1,0:T(8,128)(2,1)}, bf16[64,3072]{1,0:T(8,128)(2,1)S(1)}, u32[]{:S(2)}, u32[]{:S(2)}) collective-permute-start(bf16[64,3072]{1,0:T(8,128)(2,1)} %collective-permute-done.5.refs_9_), channel_id=1, source_target_pairs={{0,56},{8,0},{16,8},{24,16},{32,24},{40,32},{48,40},{56,48},{1,57}... | collective-permute-start | bytes 1179656 | tf_op jit(solution)/shard_map/ppermute | solution.py:26
  65.2 6.5 %collective-permute-done.9.refs_13_ = bf16[64,3072]{1,0:T(8,128)(2,1)S(1)} collective-permute-done((bf16[64,3072]{1,0:T(8,128)(2,1)}, bf16[64,3072]{1,0:T(8,128)(2,1)S(1)}, u32[]{:S(2)}, u32[]{:S(2)}) %collective-permute-start.9) | collective-permute-done | bytes 393248 | tf_op jit(solution)/shard_map/ppermute | solution.py:26
  71.9 3.5 %collective-permute-start.11 = (bf16[32,3072]{1,0:T(8,128)(2,1)S(1)}, bf16[32,3072]{1,0:T(8,128)(2,1)S(1)}, u32[]{:S(2)}, u32[]{:S(2)}) collective-permute-start(bf16[32,3072]{1,0:T(8,128)(2,1)S(1)} %slice.249), channel_id=1, source_target_pairs={{0,56},{8,0},{16,8},{24,16},{32,24},{40,32},{48,40},{56,48},{1,57}... | collective-permute-start | bytes 589832 | tf_op jit(solution)/shard_map/ppermute | solution.py:26
  75.3 1.2 pad_add_fusion.refs_0_
  76.6 1.0 fusion.26.refs_5_
  77.6 1.1 collective-permute-done.10.refs_11_
  79.5 19.4 %head_grads.2 = (bf16[512,3072]{1,0:T(8,128)(2,1)}, f32[512,3072]{1,0:T(8,128)}, bf16[32,3072]{1,0:T(8,128)(2,1)}, bf16[32,3072]{1,0:T(8,128)(2,1)}, bf16[32,307...) custom-call(s32[2]{0:T(128)} %pad_add_fusion.refs_0_, bf16[512,3072]{1,0:T(8,128)(2,1)} %bitcast.30, ...), custom_call_target="tpu_custom_call" | custom-call | flops 4831838208 | bytes 66000000 | tf_op jit(solution)/shard_map/head_grads/pallas_call | solution.py:144
  98.9 1.1 copy-done.1
  100.0 7.2 %all-to-all-start.3 = ((bf16[8,72,1536]{2,1,0:T(8,128)(2,1)}), bf16[8,72,1536]{2,1,0:T(8,128)(2,1)S(1)}, u32[]{:S(2)}, u32[]{:S(2)}) async-start(bf16[8,72,1536]{2,1,0:T(8,128)(2,1)} %bitcast.36), calls=%async_computation.3 | async-start | bytes 3538944 | tf_op jit(solution)/shard_map/all_to_all | solution.py:164
  107.2 19.5 %head_grads.3 = (bf16[512,3072]{1,0:T(8,128)(2,1)}, f32[512,3072]{1,0:T(8,128)}, bf16[32,3072]{1,0:T(8,128)(2,1)}, bf16[32,3072]{1,0:T(8,128)(2,1)}, bf16[32,307...) custom-call(s32[2]{0:T(128)} %pad_add_fusion.refs_0_, ...), custom_call_target="tpu_custom_call", output_to_operand_aliasing={{0}: (16, {}), {1}: (17, {}), {2}: (18, {}), {3}: (19, {}),... | custom-call | flops 4831838208 | bytes 66000000 | tf_op jit(solution)/shard_map/head_grads/pallas_call | solution.py:144
  126.8 3.5 %collective-permute-start.13 = (bf16[32,3072]{1,0:T(8,128)(2,1)}, bf16[32,3072]{1,0:T(8,128)(2,1)S(1)}, u32[]{:S(2)}, u32[]{:S(2)}) collective-permute-start(bf16[32,3072]{1,0:T(8,128)(2,1)} %get-tuple-element.49), channel_id=1, source_target_pairs={{0,56},{8,0},{16,8},{24,16},{32,24},{40,32},{48,40},{56,48},{1,57}... | collective-permute-start | bytes 589832 | tf_op jit(solution)/shard_map/ppermute | solution.py:26
  130.3 3.8 %collective-permute-done.12 = bf16[32,3072]{1,0:T(8,128)(2,1)S(1)} collective-permute-done((bf16[32,3072]{1,0:T(8,128)(2,1)}, bf16[32,3072]{1,0:T(8,128)(2,1)S(1)}, u32[]{:S(2)}, u32[]{:S(2)}) %collective-permute-start.12) | collective-permute-done | bytes 196640 | tf_op jit(solution)/shard_map/ppermute | solution.py:26
  134.1 1.2 add_convert_fusion.4
  135.3 1.7 pad_maximum_fusion.1
  137.8 3.3 %collective-permute-start.16 = (bf16[64,3072]{1,0:T(8,128)(2,1)}, bf16[64,3072]{1,0:T(8,128)(2,1)}, u32[]{:S(2)}, u32[]{:S(2)}) collective-permute-start(bf16[64,3072]{1,0:T(8,128)(2,1)} %pad_maximum_fusion.2), channel_id=1, source_target_pairs={{0,56},{8,0},{16,8},{24,16},{32,24},{40,32},{48,40},{56,48},{1,57}... | collective-permute-start | bytes 1179656 | tf_op jit(solution)/shard_map/ppermute | solution.py:26
  141.1 7.2 %all-to-all-start.4 = ((bf16[8,72,1536]{2,1,0:T(8,128)(2,1)}), bf16[8,72,1536]{2,1,0:T(8,128)(2,1)S(1)}, u32[]{:S(2)}, u32[]{:S(2)}) async-start(bf16[8,72,1536]{2,1,0:T(8,128)(2,1)} %bitcast.35), calls=%async_computation.4 | async-start | bytes 3538944 | tf_op jit(solution)/shard_map/all_to_all | solution.py:164
  148.4 2.6 %add_convert_fusion.2 = (bf16[64,3072]{1,0:T(8,128)(2,1)}, bf16[64,3072]{1,0:T(8,128)(2,1)}) fusion(f32[512,3072]{1,0:T(8,128)} %get-tuple-element.47, bf16[64,3072]{1,0:T(8,128)(2,1)} %collective-permute-done.16, bf16[64,3072]{1,0:T(8,128)(2,1)} %collective-permute-done.14), kind=kLoop, calls=%fused_computation.15 | loop fusion | flops 1179648 | bytes 3145728 | tf_op jit(solution)/shard_map/convert_element_type | solution.py:215
  151.0 3.2 %collective-permute-start.17 = (bf16[64,3072]{1,0:T(8,128)(2,1)}, bf16[64,3072]{1,0:T(8,128)(2,1)}, u32[]{:S(2)}, u32[]{:S(2)}) collective-permute-start(bf16[64,3072]{1,0:T(8,128)(2,1)} %get-tuple-element.70), channel_id=1, source_target_pairs={{0,56},{8,0},{16,8},{24,16},{32,24},{40,32},{48,40},{56,48},{1,57}... | collective-permute-start | bytes 1179656 | tf_op jit(solution)/shard_map/ppermute | solution.py:26
  154.2 1.0 convert_add_fusion.2
  155.3 10.7 %all-to-all-done.4 = bf16[8,72,1536]{2,1,0:T(8,128)(2,1)S(1)} async-done(((bf16[8,72,1536]{2,1,0:T(8,128)(2,1)}), bf16[8,72,1536]{2,1,0:T(8,128)(2,1)S(1)}, u32[]{:S(2)}, u32[]{:S(2)}) %all-to-all-start.4) | async-done | bytes 1769504 | tf_op jit(solution)/shard_map/all_to_all | solution.py:164
  166.3 1.7 add_convert_fusion.1
  168.4 3.2 %collective-permute-start.19 = (bf16[64,3072]{1,0:T(8,128)(2,1)S(1)}, bf16[64,3072]{1,0:T(8,128)(2,1)S(1)}, u32[]{:S(2)}, u32[]{:S(2)}) collective-permute-start(bf16[64,3072]{1,0:T(8,128)(2,1)S(1)} %get-tuple-element.69), channel_id=1, source_target_pairs={{0,56},{8,0},{16,8},{24,16},{32,24},{40,32},{48,40},{56,48},{1,57}... | collective-permute-start | bytes 1179656 | tf_op jit(solution)/shard_map/ppermute | solution.py:26
  171.9 0.9 pad_maximum_fusion
  172.9 3.5 %all-to-all-start.5 = ((bf16[8,16,3072]{2,1,0:T(8,128)(2,1)}), bf16[8,16,3072]{2,1,0:T(8,128)(2,1)S(1)}, u32[]{:S(2)}, u32[]{:S(2)}) async-start(bf16[8,16,3072]{2,1,0:T(8,128)(2,1)} %pad_maximum_fusion), calls=%async_computation.5 | async-start | bytes 1572864 | tf_op jit(solution)/shard_map/all_to_all | solution.py:164
  176.4 8.8 %collective-permute-done.18 = bf16[64,3072]{1,0:T(8,128)(2,1)S(1)} collective-permute-done((bf16[64,3072]{1,0:T(8,128)(2,1)S(1)}, bf16[64,3072]{1,0:T(8,128)(2,1)S(1)}, u32[]{:S(2)}, u32[]{:S(2)}) %collective-permute-start.18) | collective-permute-done | bytes 393248 | tf_op jit(solution)/shard_map/ppermute | solution.py:26
  185.5 1.3 fusion.37
  186.9 4.2 %collective-permute-start.21 = (bf16[16,3072]{1,0:T(8,128)(2,1)S(1)}, bf16[16,3072]{1,0:T(8,128)(2,1)S(1)}, u32[]{:S(2)}, u32[]{:S(2)}) collective-permute-start(bf16[16,3072]{1,0:T(8,128)(2,1)S(1)} %get-tuple-element.76), channel_id=1, source_target_pairs={{0,2},{1,3},{2,0},{3,1},{4,6},{5,7},{6,4},{7,5},{8,10},{9,11},{10,... | collective-permute-start | bytes 294920 | tf_op jit(solution)/shard_map/ppermute | solution.py:26
  191.7 2.1 %collective-permute-done.21 = bf16[16,3072]{1,0:T(8,128)(2,1)S(1)} collective-permute-done((bf16[16,3072]{1,0:T(8,128)(2,1)S(1)}, bf16[16,3072]{1,0:T(8,128)(2,1)S(1)}, u32[]{:S(2)}, u32[]{:S(2)}) %collective-permute-start.21) | collective-permute-done | bytes 98336 | tf_op jit(solution)/shard_map/ppermute | solution.py:26
  193.7 2.0 collective-permute-done.22
  197.0 2.0 collective-permute-start.25
  199.0 1.4 collective-permute-start.26
  200.3 1.8 collective-permute-done.23
  (84 shorter events, 9.0 us)
Async XLA Ops:
  0.6 64.0 %copy-start = (s32[1,64]{1,0:T(1,128)S(1)}, s32[1,64]{1,0:T(1,128)}, u32[]{:S(2)}) copy-start(s32[1,64]{1,0:T(1,128)} %param.11) | copy-start | bytes 772
  0.6 13.3 %collective-permute-start = (bf16[8,3072]{1,0:T(8,128)(2,1)}, bf16[8,3072]{1,0:T(8,128)(2,1)S(1)}, u32[]{:S(2)}, u32[]{:S(2)}) collective-permute-start(bf16[8,3072]{1,0:T(8,128)(2,1)} %bitcast.39), channel_id=1, source_target_pairs={{0,4},{4,0},{1,5},{5,1},{2,6},{6,2},{3,7},{7,3},{8,12},{12,8},{9,1... | collective-permute-start | bytes 147464 | tf_op jit(solution)/shard_map/ppermute | solution.py:26
  5.5 22.9 %all-to-all-start = ((bf16[8,8,3072]{2,1,0:T(8,128)(2,1)}), bf16[8,8,3072]{2,1,0:T(8,128)(2,1)S(1)}, u32[]{:S(2)}, u32[]{:S(2)}) async-start(bf16[8,8,3072]{2,1,0:T(8,128)(2,1)} %broadcast_in_dim.71), calls=%async_computation | async-start | bytes 786432 | tf_op jit(solution)/shard_map/all_to_all | solution.py:164
  15.6 19.1 %collective-permute-start.1 = (bf16[16,3072]{1,0:T(8,128)(2,1)S(1)}, bf16[16,3072]{1,0:T(8,128)(2,1)S(1)}, u32[]{:S(2)}, u32[]{:S(2)}) collective-permute-start(bf16[16,3072]{1,0:T(8,128)(2,1)S(1)} %pad_maximum_fusion.3), channel_id=1, source_target_pairs={{0,3},{1,0},{2,1},{3,2},{4,7},{5,4},{6,5},{7,6},{8,11},{9,8},{10,9... | collective-permute-start | bytes 294920 | tf_op jit(solution)/shard_map/ppermute | solution.py:26
  16.2 18.5 %collective-permute-start.2 = (bf16[16,3072]{1,0:T(8,128)(2,1)S(1)}, bf16[16,3072]{1,0:T(8,128)(2,1)S(1)}, u32[]{:S(2)}, u32[]{:S(2)}) collective-permute-start(bf16[16,3072]{1,0:T(8,128)(2,1)S(1)} %pad_maximum_fusion.3), channel_id=1, source_target_pairs={{0,2},{1,3},{2,0},{3,1},{4,6},{5,7},{6,4},{7,5},{8,10},{9,11},{10,... | collective-permute-start | bytes 294920 | tf_op jit(solution)/shard_map/ppermute | solution.py:26
  18.7 16.1 %collective-permute-start.3 = (bf16[16,3072]{1,0:T(8,128)(2,1)S(1)}, bf16[16,3072]{1,0:T(8,128)(2,1)S(1)}, u32[]{:S(2)}, u32[]{:S(2)}) collective-permute-start(bf16[16,3072]{1,0:T(8,128)(2,1)S(1)} %pad_maximum_fusion.3), channel_id=1, source_target_pairs={{0,1},{1,2},{2,3},{3,0},{4,5},{5,6},{6,7},{7,4},{8,9},{9,10},{10,1... | collective-permute-start | bytes 294920 | tf_op jit(solution)/shard_map/ppermute | solution.py:26
  29.9 23.8 %all-to-all-start.1 = ((bf16[8,64,1536]{2,1,0:T(8,128)(2,1)}), bf16[8,64,1536]{2,1,0:T(8,128)(2,1)S(1)}, u32[]{:S(2)}, u32[]{:S(2)}) async-start(bf16[8,64,1536]{2,1,0:T(8,128)(2,1)} %broadcast_in_dim.72), calls=%async_computation.1 | async-start | bytes 3145728 | tf_op jit(solution)/shard_map/all_to_all | solution.py:164
  34.8 20.3 %copy-start.7 = (bf16[64,3072]{1,0:T(8,128)(2,1)}, bf16[64,3072]{1,0:T(8,128)(2,1)S(1)}, u32[]{:S(2)}) copy-start(bf16[64,3072]{1,0:T(8,128)(2,1)S(1)} %constant_dynamic-update-slice_fusion.refs_7_) | copy-start | bytes 1179652
  34.8 10.1 %collective-permute-start.7 = (bf16[64,3072]{1,0:T(8,128)(2,1)S(1)}, bf16[64,3072]{1,0:T(8,128)(2,1)}, u32[]{:S(2)}, u32[]{:S(2)}) collective-permute-start(bf16[64,3072]{1,0:T(8,128)(2,1)S(1)} %constant_dynamic-update-slice_fusion.refs_7_), channel_id=1, source_target_pairs={{0,8},{8,16},{16,24},{24,32},{32,40},{40,48},{48,56},{56,0},{1,9},... | collective-permute-start | bytes 1179656 | tf_op jit(solution)/shard_map/ppermute | solution.py:26
  35.4 9.5 %collective-permute-start.4 = (bf16[64,3072]{1,0:T(8,128)(2,1)S(1)}, bf16[64,3072]{1,0:T(8,128)(2,1)}, u32[]{:S(2)}, u32[]{:S(2)}) collective-permute-start(bf16[64,3072]{1,0:T(8,128)(2,1)S(1)} %constant_dynamic-update-slice_fusion.refs_7_), channel_id=1, source_target_pairs={{0,56},{8,0},{16,8},{24,16},{32,24},{40,32},{48,40},{56,48},{1,57}... | collective-permute-start | bytes 1179656 | tf_op jit(solution)/shard_map/ppermute | solution.py:26
  44.9 15.8 %collective-permute-start.8 = (bf16[64,3072]{1,0:T(8,128)(2,1)}, bf16[64,3072]{1,0:T(8,128)(2,1)}, u32[]{:S(2)}, u32[]{:S(2)}) collective-permute-start(bf16[64,3072]{1,0:T(8,128)(2,1)} %collective-permute-done.7.refs_15_), channel_id=1, source_target_pairs={{0,8},{8,16},{16,24},{24,32},{32,40},{40,48},{48,56},{56,0},{1,9},... | collective-permute-start | bytes 1179656 | tf_op jit(solution)/shard_map/ppermute | solution.py:26
  44.9 15.8 %collective-permute-start.5 = (bf16[64,3072]{1,0:T(8,128)(2,1)}, bf16[64,3072]{1,0:T(8,128)(2,1)}, u32[]{:S(2)}, u32[]{:S(2)}) collective-permute-start(bf16[64,3072]{1,0:T(8,128)(2,1)} %collective-permute-done.4.refs_8_), channel_id=1, source_target_pairs={{0,56},{8,0},{16,8},{24,16},{32,24},{40,32},{48,40},{56,48},{1,57}... | collective-permute-start | bytes 1179656 | tf_op jit(solution)/shard_map/ppermute | solution.py:26
  53.6 1.7 copy-start.3
  55.3 43.6 %all-to-all-start.2 = ((bf16[8,64,1536]{2,1,0:T(8,128)(2,1)}), bf16[8,64,1536]{2,1,0:T(8,128)(2,1)S(1)}, u32[]{:S(2)}, u32[]{:S(2)}) async-start(bf16[8,64,1536]{2,1,0:T(8,128)(2,1)} %broadcast_in_dim.73), calls=%async_computation.2 | async-start | bytes 3145728 | tf_op jit(solution)/shard_map/all_to_all | solution.py:164
  60.7 11.0 %collective-permute-start.9 = (bf16[64,3072]{1,0:T(8,128)(2,1)}, bf16[64,3072]{1,0:T(8,128)(2,1)S(1)}, u32[]{:S(2)}, u32[]{:S(2)}) collective-permute-start(bf16[64,3072]{1,0:T(8,128)(2,1)} %collective-permute-done.8.refs_14_), channel_id=1, source_target_pairs={{0,8},{8,16},{16,24},{24,32},{32,40},{40,48},{48,56},{56,0},{1,9},... | collective-permute-start | bytes 1179656 | tf_op jit(solution)/shard_map/ppermute | solution.py:26
  60.7 11.1 %collective-permute-start.6 = (bf16[64,3072]{1,0:T(8,128)(2,1)}, bf16[64,3072]{1,0:T(8,128)(2,1)S(1)}, u32[]{:S(2)}, u32[]{:S(2)}) collective-permute-start(bf16[64,3072]{1,0:T(8,128)(2,1)} %collective-permute-done.5.refs_9_), channel_id=1, source_target_pairs={{0,56},{8,0},{16,8},{24,16},{32,24},{40,32},{48,40},{56,48},{1,57}... | collective-permute-start | bytes 1179656 | tf_op jit(solution)/shard_map/ppermute | solution.py:26
  71.7 7.0 %copy-start.4 = (bf16[64,3072]{1,0:T(8,128)(2,1)}, bf16[64,3072]{1,0:T(8,128)(2,1)S(1)}, u32[]{:S(2)}) copy-start(bf16[64,3072]{1,0:T(8,128)(2,1)S(1)} %collective-permute-done.9.refs_13_) | copy-start | bytes 1179652
  71.7 7.0 %collective-permute-start.10 = (bf16[32,3072]{1,0:T(8,128)(2,1)S(1)}, bf16[32,3072]{1,0:T(8,128)(2,1)S(1)}, u32[]{:S(2)}, u32[]{:S(2)}) collective-permute-start(bf16[32,3072]{1,0:T(8,128)(2,1)S(1)} %slice.248), channel_id=1, source_target_pairs={{0,8},{8,16},{16,24},{24,32},{32,40},{40,48},{48,56},{56,0},{1,9},... | collective-permute-start | bytes 589832 | tf_op jit(solution)/shard_map/ppermute | solution.py:26
  71.8 6.9 %copy-start.5 = (bf16[64,3072]{1,0:T(8,128)(2,1)}, bf16[64,3072]{1,0:T(8,128)(2,1)S(1)}, u32[]{:S(2)}) copy-start(bf16[64,3072]{1,0:T(8,128)(2,1)S(1)} %collective-permute-done.6.refs_10_) | copy-start | bytes 1179652
  71.9 6.8 %collective-permute-start.11 = (bf16[32,3072]{1,0:T(8,128)(2,1)S(1)}, bf16[32,3072]{1,0:T(8,128)(2,1)S(1)}, u32[]{:S(2)}, u32[]{:S(2)}) collective-permute-start(bf16[32,3072]{1,0:T(8,128)(2,1)S(1)} %slice.249), channel_id=1, source_target_pairs={{0,56},{8,0},{16,8},{24,16},{32,24},{40,32},{48,40},{56,48},{1,57}... | collective-permute-start | bytes 589832 | tf_op jit(solution)/shard_map/ppermute | solution.py:26
  78.7 0.7 copy-start.8
  78.7 0.8 copy-start.9
  98.9 1.1 copy-start.1
  100.0 34.1 %all-to-all-start.3 = ((bf16[8,72,1536]{2,1,0:T(8,128)(2,1)}), bf16[8,72,1536]{2,1,0:T(8,128)(2,1)S(1)}, u32[]{:S(2)}, u32[]{:S(2)}) async-start(bf16[8,72,1536]{2,1,0:T(8,128)(2,1)} %bitcast.36), calls=%async_computation.3 | async-start | bytes 3538944 | tf_op jit(solution)/shard_map/all_to_all | solution.py:164
  126.7 10.3 %copy-start.6 = (bf16[32,3072]{1,0:T(8,128)(2,1)S(1)}, bf16[32,3072]{1,0:T(8,128)(2,1)}, u32[]{:S(2)}) copy-start(bf16[32,3072]{1,0:T(8,128)(2,1)} %get-tuple-element.53) | copy-start | bytes 589828
  126.7 7.4 %collective-permute-start.12 = (bf16[32,3072]{1,0:T(8,128)(2,1)}, bf16[32,3072]{1,0:T(8,128)(2,1)S(1)}, u32[]{:S(2)}, u32[]{:S(2)}) collective-permute-start(bf16[32,3072]{1,0:T(8,128)(2,1)} %get-tuple-element.48), channel_id=1, source_target_pairs={{0,8},{8,16},{16,24},{24,32},{32,40},{40,48},{48,56},{56,0},{1,9},... | collective-permute-start | bytes 589832 | tf_op jit(solution)/shard_map/ppermute | solution.py:26
  126.8 7.3 %collective-permute-start.13 = (bf16[32,3072]{1,0:T(8,128)(2,1)}, bf16[32,3072]{1,0:T(8,128)(2,1)S(1)}, u32[]{:S(2)}, u32[]{:S(2)}) collective-permute-start(bf16[32,3072]{1,0:T(8,128)(2,1)} %get-tuple-element.49), channel_id=1, source_target_pairs={{0,56},{8,0},{16,8},{24,16},{32,24},{40,32},{48,40},{56,48},{1,57}... | collective-permute-start | bytes 589832 | tf_op jit(solution)/shard_map/ppermute | solution.py:26
  137.0 11.3 %collective-permute-start.14 = (bf16[64,3072]{1,0:T(8,128)(2,1)}, bf16[64,3072]{1,0:T(8,128)(2,1)}, u32[]{:S(2)}, u32[]{:S(2)}) collective-permute-start(bf16[64,3072]{1,0:T(8,128)(2,1)} %pad_maximum_fusion.1), channel_id=1, source_target_pairs={{0,8},{8,16},{16,24},{24,32},{32,40},{40,48},{48,56},{56,0},{1,9},... | collective-permute-start | bytes 1179656 | tf_op jit(solution)/shard_map/ppermute | solution.py:26
  137.8 10.5 %collective-permute-start.16 = (bf16[64,3072]{1,0:T(8,128)(2,1)}, bf16[64,3072]{1,0:T(8,128)(2,1)}, u32[]{:S(2)}, u32[]{:S(2)}) collective-permute-start(bf16[64,3072]{1,0:T(8,128)(2,1)} %pad_maximum_fusion.2), channel_id=1, source_target_pairs={{0,56},{8,0},{16,8},{24,16},{32,24},{40,32},{48,40},{56,48},{1,57}... | collective-permute-start | bytes 1179656 | tf_op jit(solution)/shard_map/ppermute | solution.py:26
  141.1 24.8 %all-to-all-start.4 = ((bf16[8,72,1536]{2,1,0:T(8,128)(2,1)}), bf16[8,72,1536]{2,1,0:T(8,128)(2,1)S(1)}, u32[]{:S(2)}, u32[]{:S(2)}) async-start(bf16[8,72,1536]{2,1,0:T(8,128)(2,1)} %bitcast.35), calls=%async_computation.4 | async-start | bytes 3538944 | tf_op jit(solution)/shard_map/all_to_all | solution.py:164
  151.0 15.0 %collective-permute-start.15 = (bf16[64,3072]{1,0:T(8,128)(2,1)}, bf16[64,3072]{1,0:T(8,128)(2,1)}, u32[]{:S(2)}, u32[]{:S(2)}) collective-permute-start(bf16[64,3072]{1,0:T(8,128)(2,1)} %get-tuple-element.71), channel_id=1, source_target_pairs={{0,8},{8,16},{16,24},{24,32},{32,40},{40,48},{48,56},{56,0},{1,9},... | collective-permute-start | bytes 1179656 | tf_op jit(solution)/shard_map/ppermute | solution.py:26
  151.0 15.0 %collective-permute-start.17 = (bf16[64,3072]{1,0:T(8,128)(2,1)}, bf16[64,3072]{1,0:T(8,128)(2,1)}, u32[]{:S(2)}, u32[]{:S(2)}) collective-permute-start(bf16[64,3072]{1,0:T(8,128)(2,1)} %get-tuple-element.70), channel_id=1, source_target_pairs={{0,56},{8,0},{16,8},{24,16},{32,24},{40,32},{48,40},{56,48},{1,57}... | collective-permute-start | bytes 1179656 | tf_op jit(solution)/shard_map/ppermute | solution.py:26
  155.3 10.9 %copy-start.2 = (f32[72,1536]{1,0:T(8,128)S(1)}, f32[72,1536]{1,0:T(8,128)}, u32[]{:S(2)}) copy-start(f32[72,1536]{1,0:T(8,128)} %convert_add_fusion.2) | copy-start | bytes 1327108
  168.1 17.1 %collective-permute-start.18 = (bf16[64,3072]{1,0:T(8,128)(2,1)S(1)}, bf16[64,3072]{1,0:T(8,128)(2,1)S(1)}, u32[]{:S(2)}, u32[]{:S(2)}) collective-permute-start(bf16[64,3072]{1,0:T(8,128)(2,1)S(1)} %get-tuple-element.68), channel_id=1, source_target_pairs={{0,8},{8,16},{16,24},{24,32},{32,40},{40,48},{48,56},{56,0},{1,9},... | collective-permute-start | bytes 1179656 | tf_op jit(solution)/shard_map/ppermute | solution.py:26
  168.4 17.1 %collective-permute-start.19 = (bf16[64,3072]{1,0:T(8,128)(2,1)S(1)}, bf16[64,3072]{1,0:T(8,128)(2,1)S(1)}, u32[]{:S(2)}, u32[]{:S(2)}) collective-permute-start(bf16[64,3072]{1,0:T(8,128)(2,1)S(1)} %get-tuple-element.69), channel_id=1, source_target_pairs={{0,56},{8,0},{16,8},{24,16},{32,24},{40,32},{48,40},{56,48},{1,57}... | collective-permute-start | bytes 1179656 | tf_op jit(solution)/shard_map/ppermute | solution.py:26
  172.9 23.8 %all-to-all-start.5 = ((bf16[8,16,3072]{2,1,0:T(8,128)(2,1)}), bf16[8,16,3072]{2,1,0:T(8,128)(2,1)S(1)}, u32[]{:S(2)}, u32[]{:S(2)}) async-start(bf16[8,16,3072]{2,1,0:T(8,128)(2,1)} %pad_maximum_fusion), calls=%async_computation.5 | async-start | bytes 1572864 | tf_op jit(solution)/shard_map/all_to_all | solution.py:164
  186.8 4.9 %collective-permute-start.20 = (bf16[16,3072]{1,0:T(8,128)(2,1)S(1)}, bf16[16,3072]{1,0:T(8,128)(2,1)S(1)}, u32[]{:S(2)}, u32[]{:S(2)}) collective-permute-start(bf16[16,3072]{1,0:T(8,128)(2,1)S(1)} %get-tuple-element.74), channel_id=1, source_target_pairs={{0,1},{1,2},{2,3},{3,0},{4,5},{5,6},{6,7},{7,4},{8,9},{9,10},{10,1... | collective-permute-start | bytes 294920 | tf_op jit(solution)/shard_map/ppermute | solution.py:26
  186.9 6.8 %collective-permute-start.21 = (bf16[16,3072]{1,0:T(8,128)(2,1)S(1)}, bf16[16,3072]{1,0:T(8,128)(2,1)S(1)}, u32[]{:S(2)}, u32[]{:S(2)}) collective-permute-start(bf16[16,3072]{1,0:T(8,128)(2,1)S(1)} %get-tuple-element.76), channel_id=1, source_target_pairs={{0,2},{1,3},{2,0},{3,1},{4,6},{5,7},{6,4},{7,5},{8,10},{9,11},{10,... | collective-permute-start | bytes 294920 | tf_op jit(solution)/shard_map/ppermute | solution.py:26
  191.2 4.6 %collective-permute-start.22 = (bf16[16,3072]{1,0:T(8,128)(2,1)S(1)}, bf16[16,3072]{1,0:T(8,128)(2,1)S(1)}, u32[]{:S(2)}, u32[]{:S(2)}) collective-permute-start(bf16[16,3072]{1,0:T(8,128)(2,1)S(1)} %get-tuple-element.75), channel_id=1, source_target_pairs={{0,3},{1,0},{2,1},{3,2},{4,7},{5,4},{6,5},{7,6},{8,11},{9,8},{10,9... | collective-permute-start | bytes 294920 | tf_op jit(solution)/shard_map/ppermute | solution.py:26
  195.9 6.2 %collective-permute-start.23 = (f32[8,3072]{1,0:T(8,128)S(1)}, f32[8,3072]{1,0:T(8,128)S(1)}, u32[]{:S(2)}, u32[]{:S(2)}) collective-permute-start(f32[8,3072]{1,0:T(8,128)S(1)} %slice.256), channel_id=1, source_target_pairs={{0,4},{4,0},{1,5},{5,1},{2,6},{6,2},{3,7},{7,3},{8,12},{12,8},{9,1... | collective-permute-start | bytes 294920 | tf_op jit(solution)/shard_map/ppermute | solution.py:26
  196.9 6.5 %collective-permute-start.24 = (f32[1,768]{1,0:T(1,128)S(1)}, f32[1,768]{1,0:T(1,128)S(1)}, u32[]{:S(2)}, u32[]{:S(2)}) collective-permute-start(f32[1,768]{1,0:T(1,128)S(1)} %get-tuple-element.80), channel_id=1, source_target_pairs={{0,64},{64,128},{128,192},{192,0},{1,65},{65,129},{129,193},{193,1... | collective-permute-start | bytes 9224 | tf_op jit(solution)/shard_map/ppermute | solution.py:26
  197.0 6.4 %collective-permute-start.25 = (f32[1,768]{1,0:T(1,128)S(1)}, f32[1,768]{1,0:T(1,128)S(1)}, u32[]{:S(2)}, u32[]{:S(2)}) collective-permute-start(f32[1,768]{1,0:T(1,128)S(1)} %get-tuple-element.79), channel_id=1, source_target_pairs={{0,128},{64,192},{128,0},{192,64},{1,129},{65,193},{129,1},{193,65... | collective-permute-start | bytes 9224 | tf_op jit(solution)/shard_map/ppermute | solution.py:26
  199.0 4.4 %collective-permute-start.26 = (f32[1,768]{1,0:T(1,128)S(1)}, f32[1,768]{1,0:T(1,128)S(1)}, u32[]{:S(2)}, u32[]{:S(2)}) collective-permute-start(f32[1,768]{1,0:T(1,128)S(1)} %get-tuple-element.81), channel_id=1, source_target_pairs={{0,192},{64,0},{128,64},{192,128},{1,193},{65,1},{129,65},{193,129... | collective-permute-start | bytes 9224 | tf_op jit(solution)/shard_map/ppermute | solution.py:26

commit v3 on v2

--- a/solution.py
+++ b/solution.py
@@ -34,7 +34,7 @@
 CHUNKS = (12, 12)
 PACK = 2
 FAR, HALF = NZ // 2, ZROWS // 2
-EARLY = (FAR * ZROWS, FAR * ZROWS + HALF, FAR * ZROWS - HALF, (FAR + 1) * ZROWS)
+EARLY = (FAR - 1, FAR + 1)
 KEPT = 2 + len(EARLY)
 
 
@@ -47,7 +47,7 @@
     (scalar_ref, q_ref, d_ref, gain_ref, pos_ref, bias_ref, v_ref) = refs[:7]
     k_refs = refs[7:16]
     rest = refs[16 + (0 if first else KEPT):]
-    qg_ref, dk_ref, *dk_refs, dv_ref, perm, bias = rest
+    qg_ref, dk_ref, three_ref, five_ref, far_ref, dv_ref, perm, bias = rest
     at_x = scalar_ref[1]
     rows = q_ref.shape[0]
     count = scalar_ref[0]
@@ -104,8 +104,8 @@
         qg_ref[:, at] = dot(perm[...], dx_rows.astype(BF16), NN).astype(BF16)
     dk, dv, group = (jnp.concatenate(parts, axis=1) for parts in (dks, dvs, groups))
     dk_ref[...] = dk
-    for ref, at in zip(dk_refs, EARLY):
-        ref[...] = dk[at : at + HALF].astype(BF16)
+    for ref, dz in zip((three_ref, five_ref, far_ref), (*EARLY, FAR)):
+        ref[...] = dk[dz * ZROWS : (dz + 1) * ZROWS].astype(BF16)
     for dx, x in enumerate(xs):
         at = [[dz * ZROWS + (dx * NY + y) * ROWS for dz in range(NZ)] for y in range(NY)]
         part = jnp.concatenate([p for y in range(NY) for p in [dv[k : k + ROWS] for k in at[y]] + [group]], axis=0)
@@ -122,7 +122,8 @@
     outs = [
         (rows, feat, BF16, at),
         (cap, feat, F32, at),
-        *[(HALF, feat, BF16, at)] * len(EARLY),
+        *[(ZROWS, feat, BF16, at)] * len(EARLY),
+        (ZROWS, cols, BF16, here),
         (NXY * PART, cols, BF16, here),
     ]
     first = before is None
@@ -199,22 +200,16 @@
     return pieces, values
 
 
-def scatter(terms, far_a, far_b, three_b, five_a, value_parts, dv):
+def scatter(terms, three, five, far, first, dv):
     term = lambda dz: terms[dz * ZROWS : (dz + 1) * ZROWS]
     wide = lambda part: part.astype(F32)
-    tie = lax.optimization_barrier
-    ahead, behind = both_ways(far_a, far_b)
-    ahead, behind, first = tie((ahead, behind, value_parts))
+    far_got, far = far[0], send(far[1], "z", NZ, FAR)
     second = exchange(dv, ("x", "yh"))
-    ahead = (wide(ahead) + term(FAR - 1)[:HALF]).astype(BF16)
-    behind = (wide(behind) + term(FAR + 1)[HALF:]).astype(BF16)
-    ahead, behind = both_ways(
-        jnp.concatenate([ahead, three_b], axis=0), jnp.concatenate([five_a, behind], axis=0)
-    )
+    ahead, behind = both_ways(three, five)
     ahead, behind = both_ways(
         (wide(ahead) + term(2)).astype(BF16), (wide(behind) + term(NZ - 2)).astype(BF16)
     )
-    ahead, behind, second = tie((ahead, behind, second))
+    ahead, behind, second = lax.optimization_barrier((ahead, behind, second))
     ahead, behind = both_ways(
         (wide(ahead) + term(1)).astype(BF16), (wide(behind) + term(NZ - 1)).astype(BF16)
     )
@@ -226,7 +221,7 @@
     blocks = jnp.concatenate([value_sum, jnp.broadcast_to(gain[None], value_sum.shape)], axis=1)
     blocks = blocks.astype(BF16).reshape(2 * XROWS, -1)
     value_grad = add_up(exchange(blocks, "z"), NZ)
-    key_sum = term(0) + wide(ahead) + wide(behind)
+    key_sum = term(0) + wide(ahead) + wide(behind) + wide(jnp.concatenate([far_got, far], axis=1))
     parts = [
         send(key_sum[dx * UNIT : (dx + 1) * UNIT].astype(BF16), "x", NX, dx) for dx in range(1, NX)
     ]
@@ -256,11 +251,13 @@
     )
     split = CHUNKS[0] * HEAD_DIM
     v1, v2 = (spread(part, ("x", "yh"), NXY) for part in (values[:, :split], values[:, split:]))
-    *kept, dv1 = run(0, CHUNKS[0], v1, None)
-    *kept, dv1, v2 = lax.optimization_barrier((*kept, dv1, v2))
-    *kept, dv2 = run(CHUNKS[0], CHUNKS[1], v2, kept)
+    *kept, far1, dv1 = run(0, CHUNKS[0], v1, None)
+    *kept, far1, dv1, v2 = lax.optimization_barrier((*kept, far1, dv1, v2))
+    *kept, far2, dv2 = run(CHUNKS[0], CHUNKS[1], v2, kept)
+    dv1, far1 = exchange(dv1, ("x", "yh")), send(far1, "z", NZ, FAR)
+    *kept, far2, dv2, dv1, far1 = lax.optimization_barrier((*kept, far2, dv2, dv1, far1))
     query_grad, *terms = kept
-    key_grad, value_grad, gain_grad = scatter(*terms, exchange(dv1, ("x", "yh")), dv2)
+    key_grad, value_grad, gain_grad = scatter(*terms, (far1, far2), dv1, dv2)
     return query_grad[None], key_grad.astype(BF16)[None], value_grad.astype(BF16)[None], gain_grad
 
 

time: 205 us -> 198 us (0.966)
  waiting for transfers between devices: 57.8 us -> 42.8 us
  starting transfers between devices: 80.3 us -> 89.6 us
  other arithmetic: 17.5 us -> 13.1 us
    all_to_all x6, waiting for transfers between devices: 24.1 us -> 13.4 us  [exchange(): return lax.all_to_all(blocks, axes, 0, 0, tiled=True)]
    ppermute x27, starting transfers between devices: 43.7 us -> 51.4 us  [send(): lax.ppermute(value, axis, [(i, (i + by) % size) for i in range(size)])]
    ppermute x27, waiting for transfers between devices: 33.7 us -> 29.3 us  [send(): lax.ppermute(value, axis, [(i, (i + by) % size) for i in range(size)])]
    concatenate x2 -> x0, other arithmetic: 2.53 us -> none  [the longest x1 1.74 us: scatter(): jnp.concatenate([ahead, three_b], axis=0)]
  transfers between devices with their start and end apart: 33 -> 33, of which waited for: 13 -> 9; matrix products, arithmetic and copies ran while one was open for 9% -> 9% of each run, Pallas kernels for 19% -> 20%
where the time goes in v3:
time: 198 us; the launch traced here: 195 us
  starting transfers between devices  89.6 us (45%)
  waiting for transfers between devices  42.8 us (22%)
  Pallas kernels  38.9 us (20%)
  other arithmetic  13.1 us (7%)
  local copies, waits for them, and re-layouts  9.22 us (5%)
    ppermute x27, starting transfers between devices, send(): lax.ppermute(value, axis, [(i, (i + by) % size) for i in range(size)])  51.4 us
    pallas_call x2, Pallas kernels, grads(): pl.pallas_call(functools.partial(kernel, first), grid_spec=pltpu.Prefetch...  38.9 us
    all_to_all x6, starting transfers between devices, exchange(): return lax.all_to_all(blocks, axes, 0, 0, tiled=True)  38.2 us
    ppermute x27, waiting for transfers between devices, send(): lax.ppermute(value, axis, [(i, (i + by) % size) for i in range(size)])  29.3 us
    all_to_all x6, waiting for transfers between devices, exchange(): return lax.all_to_all(blocks, axes, 0, 0, tiled=True)  13.4 us
    broadcast_in_dim x3, local copies, waits for them, and re-layouts, spread(): jnp.broadcast_to(rows[None], (count, *rows.shape))  4.29 us
  transfers between devices with their start and end apart: 33, of which 9 were waited for; matrix products, arithmetic and copies ran while one was open for 9% of the time, Pallas kernels for 20%

profile of v3, /device:TPU:2, one launch (start us, length us, event | category | flops | bytes accessed | tf_op | source)
XLA Modules:
  0.0 195.2 jit_solution(752329220251532246)
XLA Ops:
  0.6 3.3 %collective-permute-start = (bf16[8,3072]{1,0:T(8,128)(2,1)}, bf16[8,3072]{1,0:T(8,128)(2,1)S(1)}, u32[]{:S(2)}, u32[]{:S(2)}) collective-permute-start(bf16[8,3072]{1,0:T(8,128)(2,1)} %bitcast.39), channel_id=1, source_target_pairs={{0,4},{4,0},{1,5},{5,1},{2,6},{6,2},{3,7},{7,3},{8,12},{12,8},{9,1... | collective-permute-start | bytes 147464 | tf_op jit(solution)/shard_map/ppermute | solution.py:26
  3.9 1.6 broadcast_in_dim.71
  5.5 8.5 %all-to-all-start = ((bf16[8,8,3072]{2,1,0:T(8,128)(2,1)}), bf16[8,8,3072]{2,1,0:T(8,128)(2,1)S(1)}, u32[]{:S(2)}, u32[]{:S(2)}) async-start(bf16[8,8,3072]{2,1,0:T(8,128)(2,1)} %broadcast_in_dim.71), calls=%async_computation | async-start | bytes 786432 | tf_op jit(solution)/shard_map/all_to_all | solution.py:165
  16.2 2.4 %collective-permute-start.2 = (bf16[16,3072]{1,0:T(8,128)(2,1)S(1)}, bf16[16,3072]{1,0:T(8,128)(2,1)S(1)}, u32[]{:S(2)}, u32[]{:S(2)}) collective-permute-start(bf16[16,3072]{1,0:T(8,128)(2,1)S(1)} %pad_maximum_fusion.1), channel_id=1, source_target_pairs={{0,2},{1,3},{2,0},{3,1},{4,6},{5,7},{6,4},{7,5},{8,10},{9,11},{10,... | collective-permute-start | bytes 294920 | tf_op jit(solution)/shard_map/ppermute | solution.py:26
  18.7 1.8 collective-permute-start.3
  20.5 7.9 %all-to-all-done = bf16[8,8,3072]{2,1,0:T(8,128)(2,1)S(1)} async-done(((bf16[8,8,3072]{2,1,0:T(8,128)(2,1)}), bf16[8,8,3072]{2,1,0:T(8,128)(2,1)S(1)}, u32[]{:S(2)}, u32[]{:S(2)}) %all-to-all-start) | async-done | bytes 393248 | tf_op jit(solution)/shard_map/all_to_all | solution.py:165
  28.6 1.3 broadcast_in_dim.72
  29.9 4.8 %all-to-all-start.1 = ((bf16[8,64,1536]{2,1,0:T(8,128)(2,1)}), bf16[8,64,1536]{2,1,0:T(8,128)(2,1)S(1)}, u32[]{:S(2)}, u32[]{:S(2)}) async-start(bf16[8,64,1536]{2,1,0:T(8,128)(2,1)} %broadcast_in_dim.72), calls=%async_computation.1 | async-start | bytes 3145728 | tf_op jit(solution)/shard_map/all_to_all | solution.py:165
  35.4 2.7 %collective-permute-start.4 = (bf16[64,3072]{1,0:T(8,128)(2,1)S(1)}, bf16[64,3072]{1,0:T(8,128)(2,1)}, u32[]{:S(2)}, u32[]{:S(2)}) collective-permute-start(bf16[64,3072]{1,0:T(8,128)(2,1)S(1)} %constant_dynamic-update-slice_fusion.refs_7_), channel_id=1, source_target_pairs={{0,56},{8,0},{16,8},{24,16},{32,24},{40,32},{48,40},{56,48},{1,57}... | collective-permute-start | bytes 1179656 | tf_op jit(solution)/shard_map/ppermute | solution.py:26
  38.1 6.8 %collective-permute-done.7.refs_15_ = bf16[64,3072]{1,0:T(8,128)(2,1)} collective-permute-done((bf16[64,3072]{1,0:T(8,128)(2,1)S(1)}, bf16[64,3072]{1,0:T(8,128)(2,1)}, u32[]{:S(2)}, u32[]{:S(2)}) %collective-permute-start.7) | collective-permute-done | bytes 393248 | tf_op jit(solution)/shard_map/ppermute | solution.py:26
  44.9 3.2 %collective-permute-start.5 = (bf16[64,3072]{1,0:T(8,128)(2,1)}, bf16[64,3072]{1,0:T(8,128)(2,1)}, u32[]{:S(2)}, u32[]{:S(2)}) collective-permute-start(bf16[64,3072]{1,0:T(8,128)(2,1)} %collective-permute-done.4.refs_8_), channel_id=1, source_target_pairs={{0,56},{8,0},{16,8},{24,16},{32,24},{40,32},{48,40},{56,48},{1,57}... | collective-permute-start | bytes 1179656 | tf_op jit(solution)/shard_map/ppermute | solution.py:26
  48.1 5.5 %all-to-all-done.1 = bf16[8,64,1536]{2,1,0:T(8,128)(2,1)S(1)} async-done(((bf16[8,64,1536]{2,1,0:T(8,128)(2,1)}), bf16[8,64,1536]{2,1,0:T(8,128)(2,1)S(1)}, u32[]{:S(2)}, u32[]{:S(2)}) %all-to-all-start.1) | async-done | bytes 1572896 | tf_op jit(solution)/shard_map/all_to_all | solution.py:165
  53.6 1.4 broadcast_in_dim.73
  55.3 5.4 %all-to-all-start.2 = ((bf16[8,64,1536]{2,1,0:T(8,128)(2,1)}), bf16[8,64,1536]{2,1,0:T(8,128)(2,1)S(1)}, u32[]{:S(2)}, u32[]{:S(2)}) async-start(bf16[8,64,1536]{2,1,0:T(8,128)(2,1)} %broadcast_in_dim.73), calls=%async_computation.2 | async-start | bytes 3145728 | tf_op jit(solution)/shard_map/all_to_all | solution.py:165
  60.8 3.2 %collective-permute-start.6 = (bf16[64,3072]{1,0:T(8,128)(2,1)}, bf16[64,3072]{1,0:T(8,128)(2,1)S(1)}, u32[]{:S(2)}, u32[]{:S(2)}) collective-permute-start(bf16[64,3072]{1,0:T(8,128)(2,1)} %collective-permute-done.5.refs_9_), channel_id=1, source_target_pairs={{0,56},{8,0},{16,8},{24,16},{32,24},{40,32},{48,40},{56,48},{1,57}... | collective-permute-start | bytes 1179656 | tf_op jit(solution)/shard_map/ppermute | solution.py:26
  65.2 6.5 %collective-permute-done.9.refs_13_ = bf16[64,3072]{1,0:T(8,128)(2,1)S(1)} collective-permute-done((bf16[64,3072]{1,0:T(8,128)(2,1)}, bf16[64,3072]{1,0:T(8,128)(2,1)S(1)}, u32[]{:S(2)}, u32[]{:S(2)}) %collective-permute-start.9) | collective-permute-done | bytes 393248 | tf_op jit(solution)/shard_map/ppermute | solution.py:26
  71.9 3.5 %collective-permute-start.11 = (bf16[32,3072]{1,0:T(8,128)(2,1)S(1)}, bf16[32,3072]{1,0:T(8,128)(2,1)S(1)}, u32[]{:S(2)}, u32[]{:S(2)}) collective-permute-start(bf16[32,3072]{1,0:T(8,128)(2,1)S(1)} %slice.237), channel_id=1, source_target_pairs={{0,56},{8,0},{16,8},{24,16},{32,24},{40,32},{48,40},{56,48},{1,57}... | collective-permute-start | bytes 589832 | tf_op jit(solution)/shard_map/ppermute | solution.py:26
  75.4 1.2 pad_add_fusion.refs_0_
  76.6 1.0 fusion.26.refs_5_
  77.6 1.1 collective-permute-done.10.refs_11_
  79.5 19.4 %head_grads.2 = (bf16[512,3072]{1,0:T(8,128)(2,1)}, f32[512,3072]{1,0:T(8,128)}, bf16[64,3072]{1,0:T(8,128)(2,1)}, bf16[64,3072]{1,0:T(8,128)(2,1)}, bf16[64,153...) custom-call(s32[2]{0:T(128)} %pad_add_fusion.refs_0_, bf16[512,3072]{1,0:T(8,128)(2,1)} %bitcast.30, bf16[512,3072]{1,0:T(8,128)(2,1)} %bitcast.32, ...), custom_call_target="tpu_custom_call" | custom-call | flops 4831838208 | bytes 66000000 | tf_op jit(solution)/shard_map/head_grads/pallas_call | solution.py:145
  98.9 1.1 copy-done.1
  100.0 7.2 %all-to-all-start.3 = ((bf16[8,72,1536]{2,1,0:T(8,128)(2,1)}), bf16[8,72,1536]{2,1,0:T(8,128)(2,1)S(1)}, u32[]{:S(2)}, u32[]{:S(2)}) async-start(bf16[8,72,1536]{2,1,0:T(8,128)(2,1)} %bitcast.36), calls=%async_computation.3 | async-start | bytes 3538944 | tf_op jit(solution)/shard_map/all_to_all | solution.py:165
  108.1 19.5 %head_grads.3 = (bf16[512,3072]{1,0:T(8,128)(2,1)}, f32[512,3072]{1,0:T(8,128)}, bf16[64,3072]{1,0:T(8,128)(2,1)}, bf16[64,3072]{1,0:T(8,128)(2,1)}, bf16[64,153...) custom-call(s32[2]{0:T(128)} %pad_add_fusion.refs_0_, ...), custom_call_target="tpu_custom_call", output_to_operand_aliasing={{0}: (16, {}), {1}: (17, {}), {2}: (18, {}), {3}: (19, {})} | custom-call | flops 4831838208 | bytes 66000000 | tf_op jit(solution)/shard_map/head_grads/pallas_call | solution.py:145
  127.7 1.5 collective-permute-start.13
  129.2 2.1 %collective-permute-start.15 = (bf16[64,3072]{1,0:T(8,128)(2,1)}, bf16[64,3072]{1,0:T(8,128)(2,1)}, u32[]{:S(2)}, u32[]{:S(2)}) collective-permute-start(bf16[64,3072]{1,0:T(8,128)(2,1)} %get-tuple-element.56), channel_id=1, source_target_pairs={{0,56},{8,0},{16,8},{24,16},{32,24},{40,32},{48,40},{56,48},{1,57}... | collective-permute-start | bytes 1179656 | tf_op jit(solution)/shard_map/ppermute | solution.py:26
  131.3 7.2 %all-to-all-start.4 = ((bf16[8,72,1536]{2,1,0:T(8,128)(2,1)}), bf16[8,72,1536]{2,1,0:T(8,128)(2,1)S(1)}, u32[]{:S(2)}, u32[]{:S(2)}) async-start(bf16[8,72,1536]{2,1,0:T(8,128)(2,1)} %bitcast.35), calls=%async_computation.4 | async-start | bytes 3538944 | tf_op jit(solution)/shard_map/all_to_all | solution.py:165
  138.5 5.0 %collective-permute-start.19 = (bf16[64,1536]{1,0:T(8,128)(2,1)}, bf16[64,1536]{1,0:T(8,128)(2,1)}, u32[]{:S(2)}, u32[]{:S(2)}) collective-permute-start(bf16[64,1536]{1,0:T(8,128)(2,1)} %get-tuple-element.61), channel_id=1, source_target_pairs={{0,32},{8,40},{16,48},{24,56},{32,0},{40,8},{48,16},{56,24},{1,33}... | collective-permute-start | bytes 589832 | tf_op jit(solution)/shard_map/ppermute | solution.py:26
  143.5 1.7 add_convert_fusion.2
  145.2 1.0 collective-permute-start.14
  146.3 2.3 %collective-permute-start.16 = (bf16[64,3072]{1,0:T(8,128)(2,1)S(1)}, bf16[64,3072]{1,0:T(8,128)(2,1)}, u32[]{:S(2)}, u32[]{:S(2)}) collective-permute-start(bf16[64,3072]{1,0:T(8,128)(2,1)S(1)} %get-tuple-element.74), channel_id=1, source_target_pairs={{0,56},{8,0},{16,8},{24,16},{32,24},{40,32},{48,40},{56,48},{1,57}... | collective-permute-start | bytes 1179656 | tf_op jit(solution)/shard_map/ppermute | solution.py:26
  148.6 1.0 convert_add_fusion.2
  149.6 7.3 %collective-permute-done.14 = bf16[64,3072]{1,0:T(8,128)(2,1)S(1)} collective-permute-done((bf16[64,3072]{1,0:T(8,128)(2,1)S(1)}, bf16[64,3072]{1,0:T(8,128)(2,1)S(1)}, u32[]{:S(2)}, u32[]{:S(2)}) %collective-permute-start.14) | collective-permute-done | bytes 393248 | tf_op jit(solution)/shard_map/ppermute | solution.py:26
  158.7 1.6 add_convert_fusion.1
  160.3 1.1 collective-permute-start.17
  161.4 2.4 %collective-permute-start.18 = (bf16[64,3072]{1,0:T(8,128)(2,1)S(1)}, bf16[64,3072]{1,0:T(8,128)(2,1)S(1)}, u32[]{:S(2)}, u32[]{:S(2)}) collective-permute-start(bf16[64,3072]{1,0:T(8,128)(2,1)S(1)} %get-tuple-element.73), channel_id=1, source_target_pairs={{0,56},{8,0},{16,8},{24,16},{32,24},{40,32},{48,40},{56,48},{1,57}... | collective-permute-start | bytes 1179656 | tf_op jit(solution)/shard_map/ppermute | solution.py:26
  164.2 0.9 pad_maximum_fusion
  165.1 5.1 %all-to-all-start.5 = ((bf16[8,16,3072]{2,1,0:T(8,128)(2,1)}), bf16[8,16,3072]{2,1,0:T(8,128)(2,1)S(1)}, u32[]{:S(2)}, u32[]{:S(2)}) async-start(bf16[8,16,3072]{2,1,0:T(8,128)(2,1)} %pad_maximum_fusion), calls=%async_computation.5 | async-start | bytes 1572864 | tf_op jit(solution)/shard_map/all_to_all | solution.py:165
  170.3 3.6 %collective-permute-done.18 = bf16[64,3072]{1,0:T(8,128)(2,1)S(1)} collective-permute-done((bf16[64,3072]{1,0:T(8,128)(2,1)S(1)}, bf16[64,3072]{1,0:T(8,128)(2,1)S(1)}, u32[]{:S(2)}, u32[]{:S(2)}) %collective-permute-start.18) | collective-permute-done | bytes 393248 | tf_op jit(solution)/shard_map/ppermute | solution.py:26
  173.9 1.6 fusion.37
  175.5 1.8 collective-permute-start.20
  177.3 2.0 %collective-permute-start.21 = (bf16[16,3072]{1,0:T(8,128)(2,1)S(1)}, bf16[16,3072]{1,0:T(8,128)(2,1)S(1)}, u32[]{:S(2)}, u32[]{:S(2)}) collective-permute-start(bf16[16,3072]{1,0:T(8,128)(2,1)S(1)} %get-tuple-element.78), channel_id=1, source_target_pairs={{0,2},{1,3},{2,0},{3,1},{4,6},{5,7},{6,4},{7,5},{8,10},{9,11},{10,... | collective-permute-start | bytes 294920 | tf_op jit(solution)/shard_map/ppermute | solution.py:26
  179.3 1.3 collective-permute-start.22
  180.6 2.9 %collective-permute-done.21 = bf16[16,3072]{1,0:T(8,128)(2,1)S(1)} collective-permute-done((bf16[16,3072]{1,0:T(8,128)(2,1)S(1)}, bf16[16,3072]{1,0:T(8,128)(2,1)S(1)}, u32[]{:S(2)}, u32[]{:S(2)}) %collective-permute-start.21) | collective-permute-done | bytes 98336 | tf_op jit(solution)/shard_map/ppermute | solution.py:26
  183.5 1.0 collective-permute-done.22
  184.6 5.6 %collective-permute-start.23 = (f32[8,3072]{1,0:T(8,128)S(1)}, f32[8,3072]{1,0:T(8,128)S(1)}, u32[]{:S(2)}, u32[]{:S(2)}) collective-permute-start(f32[8,3072]{1,0:T(8,128)S(1)} %slice.244), channel_id=1, source_target_pairs={{0,4},{4,0},{1,5},{5,1},{2,6},{6,2},{3,7},{7,3},{8,12},{12,8},{9,1... | collective-permute-start | bytes 294920 | tf_op jit(solution)/shard_map/ppermute | solution.py:26
  190.6 1.3 collective-permute-start.25
  191.9 1.4 collective-permute-start.26
  (85 shorter events, 10.2 us)
Async XLA Ops:
  0.6 64.0 %copy-start = (s32[1,64]{1,0:T(1,128)S(1)}, s32[1,64]{1,0:T(1,128)}, u32[]{:S(2)}) copy-start(s32[1,64]{1,0:T(1,128)} %param.11) | copy-start | bytes 772
  0.6 13.3 %collective-permute-start = (bf16[8,3072]{1,0:T(8,128)(2,1)}, bf16[8,3072]{1,0:T(8,128)(2,1)S(1)}, u32[]{:S(2)}, u32[]{:S(2)}) collective-permute-start(bf16[8,3072]{1,0:T(8,128)(2,1)} %bitcast.39), channel_id=1, source_target_pairs={{0,4},{4,0},{1,5},{5,1},{2,6},{6,2},{3,7},{7,3},{8,12},{12,8},{9,1... | collective-permute-start | bytes 147464 | tf_op jit(solution)/shard_map/ppermute | solution.py:26
  5.5 22.9 %all-to-all-start = ((bf16[8,8,3072]{2,1,0:T(8,128)(2,1)}), bf16[8,8,3072]{2,1,0:T(8,128)(2,1)S(1)}, u32[]{:S(2)}, u32[]{:S(2)}) async-start(bf16[8,8,3072]{2,1,0:T(8,128)(2,1)} %broadcast_in_dim.71), calls=%async_computation | async-start | bytes 786432 | tf_op jit(solution)/shard_map/all_to_all | solution.py:165
  15.6 19.1 %collective-permute-start.1 = (bf16[16,3072]{1,0:T(8,128)(2,1)S(1)}, bf16[16,3072]{1,0:T(8,128)(2,1)S(1)}, u32[]{:S(2)}, u32[]{:S(2)}) collective-permute-start(bf16[16,3072]{1,0:T(8,128)(2,1)S(1)} %pad_maximum_fusion.1), channel_id=1, source_target_pairs={{0,3},{1,0},{2,1},{3,2},{4,7},{5,4},{6,5},{7,6},{8,11},{9,8},{10,9... | collective-permute-start | bytes 294920 | tf_op jit(solution)/shard_map/ppermute | solution.py:26
  16.2 18.5 %collective-permute-start.2 = (bf16[16,3072]{1,0:T(8,128)(2,1)S(1)}, bf16[16,3072]{1,0:T(8,128)(2,1)S(1)}, u32[]{:S(2)}, u32[]{:S(2)}) collective-permute-start(bf16[16,3072]{1,0:T(8,128)(2,1)S(1)} %pad_maximum_fusion.1), channel_id=1, source_target_pairs={{0,2},{1,3},{2,0},{3,1},{4,6},{5,7},{6,4},{7,5},{8,10},{9,11},{10,... | collective-permute-start | bytes 294920 | tf_op jit(solution)/shard_map/ppermute | solution.py:26
  18.7 16.1 %collective-permute-start.3 = (bf16[16,3072]{1,0:T(8,128)(2,1)S(1)}, bf16[16,3072]{1,0:T(8,128)(2,1)S(1)}, u32[]{:S(2)}, u32[]{:S(2)}) collective-permute-start(bf16[16,3072]{1,0:T(8,128)(2,1)S(1)} %pad_maximum_fusion.1), channel_id=1, source_target_pairs={{0,1},{1,2},{2,3},{3,0},{4,5},{5,6},{6,7},{7,4},{8,9},{9,10},{10,1... | collective-permute-start | bytes 294920 | tf_op jit(solution)/shard_map/ppermute | solution.py:26
  29.9 23.8 %all-to-all-start.1 = ((bf16[8,64,1536]{2,1,0:T(8,128)(2,1)}), bf16[8,64,1536]{2,1,0:T(8,128)(2,1)S(1)}, u32[]{:S(2)}, u32[]{:S(2)}) async-start(bf16[8,64,1536]{2,1,0:T(8,128)(2,1)} %broadcast_in_dim.72), calls=%async_computation.1 | async-start | bytes 3145728 | tf_op jit(solution)/shard_map/all_to_all | solution.py:165
  34.8 20.3 %copy-start.6 = (bf16[64,3072]{1,0:T(8,128)(2,1)}, bf16[64,3072]{1,0:T(8,128)(2,1)S(1)}, u32[]{:S(2)}) copy-start(bf16[64,3072]{1,0:T(8,128)(2,1)S(1)} %constant_dynamic-update-slice_fusion.refs_7_) | copy-start | bytes 1179652
  34.8 10.1 %collective-permute-start.7 = (bf16[64,3072]{1,0:T(8,128)(2,1)S(1)}, bf16[64,3072]{1,0:T(8,128)(2,1)}, u32[]{:S(2)}, u32[]{:S(2)}) collective-permute-start(bf16[64,3072]{1,0:T(8,128)(2,1)S(1)} %constant_dynamic-update-slice_fusion.refs_7_), channel_id=1, source_target_pairs={{0,8},{8,16},{16,24},{24,32},{32,40},{40,48},{48,56},{56,0},{1,9},... | collective-permute-start | bytes 1179656 | tf_op jit(solution)/shard_map/ppermute | solution.py:26
  35.4 9.5 %collective-permute-start.4 = (bf16[64,3072]{1,0:T(8,128)(2,1)S(1)}, bf16[64,3072]{1,0:T(8,128)(2,1)}, u32[]{:S(2)}, u32[]{:S(2)}) collective-permute-start(bf16[64,3072]{1,0:T(8,128)(2,1)S(1)} %constant_dynamic-update-slice_fusion.refs_7_), channel_id=1, source_target_pairs={{0,56},{8,0},{16,8},{24,16},{32,24},{40,32},{48,40},{56,48},{1,57}... | collective-permute-start | bytes 1179656 | tf_op jit(solution)/shard_map/ppermute | solution.py:26
  44.9 15.9 %collective-permute-start.8 = (bf16[64,3072]{1,0:T(8,128)(2,1)}, bf16[64,3072]{1,0:T(8,128)(2,1)}, u32[]{:S(2)}, u32[]{:S(2)}) collective-permute-start(bf16[64,3072]{1,0:T(8,128)(2,1)} %collective-permute-done.7.refs_15_), channel_id=1, source_target_pairs={{0,8},{8,16},{16,24},{24,32},{32,40},{40,48},{48,56},{56,0},{1,9},... | collective-permute-start | bytes 1179656 | tf_op jit(solution)/shard_map/ppermute | solution.py:26
  44.9 15.9 %collective-permute-start.5 = (bf16[64,3072]{1,0:T(8,128)(2,1)}, bf16[64,3072]{1,0:T(8,128)(2,1)}, u32[]{:S(2)}, u32[]{:S(2)}) collective-permute-start(bf16[64,3072]{1,0:T(8,128)(2,1)} %collective-permute-done.4.refs_8_), channel_id=1, source_target_pairs={{0,56},{8,0},{16,8},{24,16},{32,24},{40,32},{48,40},{56,48},{1,57}... | collective-permute-start | bytes 1179656 | tf_op jit(solution)/shard_map/ppermute | solution.py:26
  53.6 1.7 copy-start.3
  55.3 43.5 %all-to-all-start.2 = ((bf16[8,64,1536]{2,1,0:T(8,128)(2,1)}), bf16[8,64,1536]{2,1,0:T(8,128)(2,1)S(1)}, u32[]{:S(2)}, u32[]{:S(2)}) async-start(bf16[8,64,1536]{2,1,0:T(8,128)(2,1)} %broadcast_in_dim.73), calls=%async_computation.2 | async-start | bytes 3145728 | tf_op jit(solution)/shard_map/all_to_all | solution.py:165
  60.7 11.0 %collective-permute-start.9 = (bf16[64,3072]{1,0:T(8,128)(2,1)}, bf16[64,3072]{1,0:T(8,128)(2,1)S(1)}, u32[]{:S(2)}, u32[]{:S(2)}) collective-permute-start(bf16[64,3072]{1,0:T(8,128)(2,1)} %collective-permute-done.8.refs_14_), channel_id=1, source_target_pairs={{0,8},{8,16},{16,24},{24,32},{32,40},{40,48},{48,56},{56,0},{1,9},... | collective-permute-start | bytes 1179656 | tf_op jit(solution)/shard_map/ppermute | solution.py:26
  60.8 11.1 %collective-permute-start.6 = (bf16[64,3072]{1,0:T(8,128)(2,1)}, bf16[64,3072]{1,0:T(8,128)(2,1)S(1)}, u32[]{:S(2)}, u32[]{:S(2)}) collective-permute-start(bf16[64,3072]{1,0:T(8,128)(2,1)} %collective-permute-done.5.refs_9_), channel_id=1, source_target_pairs={{0,56},{8,0},{16,8},{24,16},{32,24},{40,32},{48,40},{56,48},{1,57}... | collective-permute-start | bytes 1179656 | tf_op jit(solution)/shard_map/ppermute | solution.py:26
  71.7 7.0 %copy-start.4 = (bf16[64,3072]{1,0:T(8,128)(2,1)}, bf16[64,3072]{1,0:T(8,128)(2,1)S(1)}, u32[]{:S(2)}) copy-start(bf16[64,3072]{1,0:T(8,128)(2,1)S(1)} %collective-permute-done.9.refs_13_) | copy-start | bytes 1179652
  71.8 7.0 %collective-permute-start.10 = (bf16[32,3072]{1,0:T(8,128)(2,1)S(1)}, bf16[32,3072]{1,0:T(8,128)(2,1)S(1)}, u32[]{:S(2)}, u32[]{:S(2)}) collective-permute-start(bf16[32,3072]{1,0:T(8,128)(2,1)S(1)} %slice.236), channel_id=1, source_target_pairs={{0,8},{8,16},{16,24},{24,32},{32,40},{40,48},{48,56},{56,0},{1,9},... | collective-permute-start | bytes 589832 | tf_op jit(solution)/shard_map/ppermute | solution.py:26
  71.9 6.9 %copy-start.5 = (bf16[64,3072]{1,0:T(8,128)(2,1)}, bf16[64,3072]{1,0:T(8,128)(2,1)S(1)}, u32[]{:S(2)}) copy-start(bf16[64,3072]{1,0:T(8,128)(2,1)S(1)} %collective-permute-done.6.refs_10_) | copy-start | bytes 1179652
  71.9 6.8 %collective-permute-start.11 = (bf16[32,3072]{1,0:T(8,128)(2,1)S(1)}, bf16[32,3072]{1,0:T(8,128)(2,1)S(1)}, u32[]{:S(2)}, u32[]{:S(2)}) collective-permute-start(bf16[32,3072]{1,0:T(8,128)(2,1)S(1)} %slice.237), channel_id=1, source_target_pairs={{0,56},{8,0},{16,8},{24,16},{32,24},{40,32},{48,40},{56,48},{1,57}... | collective-permute-start | bytes 589832 | tf_op jit(solution)/shard_map/ppermute | solution.py:26
  78.7 0.7 copy-start.9
  78.7 0.8 copy-start.10
  98.9 1.1 copy-start.1
  98.9 8.4 %copy-start.11 = (bf16[64,1536]{1,0:T(8,128)(2,1)S(1)}, bf16[64,1536]{1,0:T(8,128)(2,1)}, u32[]{:S(2)}) copy-start(bf16[64,1536]{1,0:T(8,128)(2,1)} %get-tuple-element.52) | copy-start | bytes 589828
  100.0 27.6 %all-to-all-start.3 = ((bf16[8,72,1536]{2,1,0:T(8,128)(2,1)}), bf16[8,72,1536]{2,1,0:T(8,128)(2,1)S(1)}, u32[]{:S(2)}, u32[]{:S(2)}) async-start(bf16[8,72,1536]{2,1,0:T(8,128)(2,1)} %bitcast.36), calls=%async_computation.3 | async-start | bytes 3538944 | tf_op jit(solution)/shard_map/all_to_all | solution.py:165
  107.2 20.4 %collective-permute-start.12 = (bf16[64,1536]{1,0:T(8,128)(2,1)S(1)}, bf16[64,1536]{1,0:T(8,128)(2,1)}, u32[]{:S(2)}, u32[]{:S(2)}) collective-permute-start(bf16[64,1536]{1,0:T(8,128)(2,1)S(1)} %copy-done.11), channel_id=1, source_target_pairs={{0,32},{8,40},{16,48},{24,56},{32,0},{40,8},{48,16},{56,24},{1,33}... | collective-permute-start | bytes 589832 | tf_op jit(solution)/shard_map/ppermute | solution.py:26
  127.7 15.8 %collective-permute-start.13 = (bf16[64,3072]{1,0:T(8,128)(2,1)}, bf16[64,3072]{1,0:T(8,128)(2,1)}, u32[]{:S(2)}, u32[]{:S(2)}) collective-permute-start(bf16[64,3072]{1,0:T(8,128)(2,1)} %get-tuple-element.55), channel_id=1, source_target_pairs={{0,8},{8,16},{16,24},{24,32},{32,40},{40,48},{48,56},{56,0},{1,9},... | collective-permute-start | bytes 1179656 | tf_op jit(solution)/shard_map/ppermute | solution.py:26
  129.2 14.3 %collective-permute-start.15 = (bf16[64,3072]{1,0:T(8,128)(2,1)}, bf16[64,3072]{1,0:T(8,128)(2,1)}, u32[]{:S(2)}, u32[]{:S(2)}) collective-permute-start(bf16[64,3072]{1,0:T(8,128)(2,1)} %get-tuple-element.56), channel_id=1, source_target_pairs={{0,56},{8,0},{16,8},{24,16},{32,24},{40,32},{48,40},{56,48},{1,57}... | collective-permute-start | bytes 1179656 | tf_op jit(solution)/shard_map/ppermute | solution.py:26
  131.3 26.4 %all-to-all-start.4 = ((bf16[8,72,1536]{2,1,0:T(8,128)(2,1)}), bf16[8,72,1536]{2,1,0:T(8,128)(2,1)S(1)}, u32[]{:S(2)}, u32[]{:S(2)}) async-start(bf16[8,72,1536]{2,1,0:T(8,128)(2,1)} %bitcast.35), calls=%async_computation.4 | async-start | bytes 3538944 | tf_op jit(solution)/shard_map/all_to_all | solution.py:165
  138.5 31.8 %collective-permute-start.19 = (bf16[64,1536]{1,0:T(8,128)(2,1)}, bf16[64,1536]{1,0:T(8,128)(2,1)}, u32[]{:S(2)}, u32[]{:S(2)}) collective-permute-start(bf16[64,1536]{1,0:T(8,128)(2,1)} %get-tuple-element.61), channel_id=1, source_target_pairs={{0,32},{8,40},{16,48},{24,56},{32,0},{40,8},{48,16},{56,24},{1,33}... | collective-permute-start | bytes 589832 | tf_op jit(solution)/shard_map/ppermute | solution.py:26
  145.2 11.7 %collective-permute-start.14 = (bf16[64,3072]{1,0:T(8,128)(2,1)S(1)}, bf16[64,3072]{1,0:T(8,128)(2,1)S(1)}, u32[]{:S(2)}, u32[]{:S(2)}) collective-permute-start(bf16[64,3072]{1,0:T(8,128)(2,1)S(1)} %get-tuple-element.75), channel_id=1, source_target_pairs={{0,8},{8,16},{16,24},{24,32},{32,40},{40,48},{48,56},{56,0},{1,9},... | collective-permute-start | bytes 1179656 | tf_op jit(solution)/shard_map/ppermute | solution.py:26
  146.3 11.4 %collective-permute-start.16 = (bf16[64,3072]{1,0:T(8,128)(2,1)S(1)}, bf16[64,3072]{1,0:T(8,128)(2,1)}, u32[]{:S(2)}, u32[]{:S(2)}) collective-permute-start(bf16[64,3072]{1,0:T(8,128)(2,1)S(1)} %get-tuple-element.74), channel_id=1, source_target_pairs={{0,56},{8,0},{16,8},{24,16},{32,24},{40,32},{48,40},{56,48},{1,57}... | collective-permute-start | bytes 1179656 | tf_op jit(solution)/shard_map/ppermute | solution.py:26
  149.6 8.3 %copy-start.2 = (f32[72,1536]{1,0:T(8,128)S(1)}, f32[72,1536]{1,0:T(8,128)}, u32[]{:S(2)}) copy-start(f32[72,1536]{1,0:T(8,128)} %convert_add_fusion.2) | copy-start | bytes 1327108
  156.9 0.8 copy-start.7
  157.7 1.0 copy-start.8
  160.3 9.9 %collective-permute-start.17 = (bf16[64,3072]{1,0:T(8,128)(2,1)S(1)}, bf16[64,3072]{1,0:T(8,128)(2,1)S(1)}, u32[]{:S(2)}, u32[]{:S(2)}) collective-permute-start(bf16[64,3072]{1,0:T(8,128)(2,1)S(1)} %get-tuple-element.72), channel_id=1, source_target_pairs={{0,8},{8,16},{16,24},{24,32},{32,40},{40,48},{48,56},{56,0},{1,9},... | collective-permute-start | bytes 1179656 | tf_op jit(solution)/shard_map/ppermute | solution.py:26
  161.4 12.5 %collective-permute-start.18 = (bf16[64,3072]{1,0:T(8,128)(2,1)S(1)}, bf16[64,3072]{1,0:T(8,128)(2,1)S(1)}, u32[]{:S(2)}, u32[]{:S(2)}) collective-permute-start(bf16[64,3072]{1,0:T(8,128)(2,1)S(1)} %get-tuple-element.73), channel_id=1, source_target_pairs={{0,56},{8,0},{16,8},{24,16},{32,24},{40,32},{48,40},{56,48},{1,57}... | collective-permute-start | bytes 1179656 | tf_op jit(solution)/shard_map/ppermute | solution.py:26
  165.1 25.1 %all-to-all-start.5 = ((bf16[8,16,3072]{2,1,0:T(8,128)(2,1)}), bf16[8,16,3072]{2,1,0:T(8,128)(2,1)S(1)}, u32[]{:S(2)}, u32[]{:S(2)}) async-start(bf16[8,16,3072]{2,1,0:T(8,128)(2,1)} %pad_maximum_fusion), calls=%async_computation.5 | async-start | bytes 1572864 | tf_op jit(solution)/shard_map/all_to_all | solution.py:165
  175.5 5.1 %collective-permute-start.20 = (bf16[16,3072]{1,0:T(8,128)(2,1)S(1)}, bf16[16,3072]{1,0:T(8,128)(2,1)S(1)}, u32[]{:S(2)}, u32[]{:S(2)}) collective-permute-start(bf16[16,3072]{1,0:T(8,128)(2,1)S(1)} %get-tuple-element.76), channel_id=1, source_target_pairs={{0,1},{1,2},{2,3},{3,0},{4,5},{5,6},{6,7},{7,4},{8,9},{9,10},{10,1... | collective-permute-start | bytes 294920 | tf_op jit(solution)/shard_map/ppermute | solution.py:26
  177.3 6.2 %collective-permute-start.21 = (bf16[16,3072]{1,0:T(8,128)(2,1)S(1)}, bf16[16,3072]{1,0:T(8,128)(2,1)S(1)}, u32[]{:S(2)}, u32[]{:S(2)}) collective-permute-start(bf16[16,3072]{1,0:T(8,128)(2,1)S(1)} %get-tuple-element.78), channel_id=1, source_target_pairs={{0,2},{1,3},{2,0},{3,1},{4,6},{5,7},{6,4},{7,5},{8,10},{9,11},{10,... | collective-permute-start | bytes 294920 | tf_op jit(solution)/shard_map/ppermute | solution.py:26
  179.3 5.2 %collective-permute-start.22 = (bf16[16,3072]{1,0:T(8,128)(2,1)S(1)}, bf16[16,3072]{1,0:T(8,128)(2,1)S(1)}, u32[]{:S(2)}, u32[]{:S(2)}) collective-permute-start(bf16[16,3072]{1,0:T(8,128)(2,1)S(1)} %get-tuple-element.77), channel_id=1, source_target_pairs={{0,3},{1,0},{2,1},{3,2},{4,7},{5,4},{6,5},{7,6},{8,11},{9,8},{10,9... | collective-permute-start | bytes 294920 | tf_op jit(solution)/shard_map/ppermute | solution.py:26
  184.6 8.7 %collective-permute-start.23 = (f32[8,3072]{1,0:T(8,128)S(1)}, f32[8,3072]{1,0:T(8,128)S(1)}, u32[]{:S(2)}, u32[]{:S(2)}) collective-permute-start(f32[8,3072]{1,0:T(8,128)S(1)} %slice.244), channel_id=1, source_target_pairs={{0,4},{4,0},{1,5},{5,1},{2,6},{6,2},{3,7},{7,3},{8,12},{12,8},{9,1... | collective-permute-start | bytes 294920 | tf_op jit(solution)/shard_map/ppermute | solution.py:26
  190.5 4.1 %collective-permute-start.24 = (f32[1,768]{1,0:T(1,128)S(1)}, f32[1,768]{1,0:T(1,128)S(1)}, u32[]{:S(2)}, u32[]{:S(2)}) collective-permute-start(f32[1,768]{1,0:T(1,128)S(1)} %get-tuple-element.82), channel_id=1, source_target_pairs={{0,64},{64,128},{128,192},{192,0},{1,65},{65,129},{129,193},{193,1... | collective-permute-start | bytes 9224 | tf_op jit(solution)/shard_map/ppermute | solution.py:26
  190.6 4.0 %collective-permute-start.25 = (f32[1,768]{1,0:T(1,128)S(1)}, f32[1,768]{1,0:T(1,128)S(1)}, u32[]{:S(2)}, u32[]{:S(2)}) collective-permute-start(f32[1,768]{1,0:T(1,128)S(1)} %get-tuple-element.81), channel_id=1, source_target_pairs={{0,128},{64,192},{128,0},{192,64},{1,129},{65,193},{129,1},{193,65... | collective-permute-start | bytes 9224 | tf_op jit(solution)/shard_map/ppermute | solution.py:26
  191.9 2.7 %collective-permute-start.26 = (f32[1,768]{1,0:T(1,128)S(1)}, f32[1,768]{1,0:T(1,128)S(1)}, u32[]{:S(2)}, u32[]{:S(2)}) collective-permute-start(f32[1,768]{1,0:T(1,128)S(1)} %get-tuple-element.83), channel_id=1, source_target_pairs={{0,192},{64,0},{128,64},{192,128},{1,193},{65,1},{129,65},{193,129... | collective-permute-start | bytes 9224 | tf_op jit(solution)/shard_map/ppermute | solution.py:26

commit v4 on v3

--- a/solution.py
+++ b/solution.py
@@ -133,7 +133,7 @@
         pl.BlockSpec((1, PACK * HEAD_DIM), at),
         pl.BlockSpec(pos.shape, fixed),
         pl.BlockSpec(bias.shape, fixed),
-        pl.BlockSpec((cap, PACK * HEAD_DIM), here),
+        pl.BlockSpec((cap, PACK * HEAD_DIM), at),
     ] + [pl.BlockSpec((part.shape[0], PACK * HEAD_DIM), at) for part in k_parts]
     args = [scalars, q, d, gain, pos, bias, v, *k_parts]
     aliases = {}
@@ -249,11 +249,10 @@
         head, heads, scalars, queries[0], grad_out[0], query_gain[None], kept_pos, bias, v, key_parts,
         before,
     )
-    split = CHUNKS[0] * HEAD_DIM
-    v1, v2 = (spread(part, ("x", "yh"), NXY) for part in (values[:, :split], values[:, split:]))
-    *kept, far1, dv1 = run(0, CHUNKS[0], v1, None)
-    *kept, far1, dv1, v2 = lax.optimization_barrier((*kept, far1, dv1, v2))
-    *kept, far2, dv2 = run(CHUNKS[0], CHUNKS[1], v2, kept)
+    values = spread(values, ("x", "yh"), NXY)
+    *kept, far1, dv1 = run(0, CHUNKS[0], values, None)
+    *kept, far1, dv1, values = lax.optimization_barrier((*kept, far1, dv1, values))
+    *kept, far2, dv2 = run(CHUNKS[0], CHUNKS[1], values, kept)
     dv1, far1 = exchange(dv1, ("x", "yh")), send(far1, "z", NZ, FAR)
     *kept, far2, dv2, dv1, far1 = lax.optimization_barrier((*kept, far2, dv2, dv1, far1))
     query_grad, *terms = kept

time: 198 us -> 239 us (1.21)
  waiting for transfers between devices: 42.8 us -> 88.8 us
  starting transfers between devices: 89.6 us -> 80.5 us
  other arithmetic: 13.1 us -> 16.1 us
    ppermute x27, waiting for transfers between devices: 29.3 us -> 77.2 us  [send(): lax.ppermute(value, axis, [(i, (i + by) % size) for i in range(size)])]
    ppermute x27, starting transfers between devices: 51.4 us -> 46.7 us  [send(): lax.ppermute(value, axis, [(i, (i + by) % size) for i in range(size)])]
    all_to_all x6 -> x5, starting transfers between devices: 38.2 us -> 33.8 us  [exchange(): return lax.all_to_all(blocks, axes, 0, 0, tiled=True)]
    all_to_all x6 -> x5, waiting for transfers between devices: 13.4 us -> 11.5 us  [exchange(): return lax.all_to_all(blocks, axes, 0, 0, tiled=True)]
  transfers between devices with their start and end apart: 33 -> 32, of which waited for: 9 -> 15; matrix products, arithmetic and copies ran while one was open for 9% -> 8% of each run, Pallas kernels for 20% -> 8%
where the time goes in v4:
time: 239 us; the launch traced here: 235 us
  waiting for transfers between devices  88.8 us (37%)
  starting transfers between devices  80.5 us (34%)
  Pallas kernels  38.8 us (16%)
  other arithmetic  16.1 us (7%)
  local copies, waits for them, and re-layouts  9.1 us (4%)
    ppermute x27, waiting for transfers between devices, send(): lax.ppermute(value, axis, [(i, (i + by) % size) for i in range(size)])  77.2 us
    ppermute x27, starting transfers between devices, send(): lax.ppermute(value, axis, [(i, (i + by) % size) for i in range(size)])  46.7 us
    pallas_call x2, Pallas kernels, grads(): pl.pallas_call(functools.partial(kernel, first), grid_spec=pltpu.Prefetch...  38.8 us
    all_to_all x5, starting transfers between devices, exchange(): return lax.all_to_all(blocks, axes, 0, 0, tiled=True)  33.8 us
    all_to_all x5, waiting for transfers between devices, exchange(): return lax.all_to_all(blocks, axes, 0, 0, tiled=True)  11.5 us
  transfers between devices with their start and end apart: 32, of which 15 were waited for; matrix products, arithmetic and copies ran while one was open for 8% of the time, Pallas kernels for 8%

profile of v4, /device:TPU:2, one launch (start us, length us, event | category | flops | bytes accessed | tf_op | source)
XLA Modules:
  0.0 234.8 jit_solution(12510157276766331423)
XLA Ops:
  0.6 3.3 %collective-permute-start = (bf16[8,3072]{1,0:T(8,128)(2,1)}, bf16[8,3072]{1,0:T(8,128)(2,1)S(1)}, u32[]{:S(2)}, u32[]{:S(2)}) collective-permute-start(bf16[8,3072]{1,0:T(8,128)(2,1)} %bitcast.38), channel_id=1, source_target_pairs={{0,4},{4,0},{1,5},{5,1},{2,6},{6,2},{3,7},{7,3},{8,12},{12,8},{9,1... | collective-permute-start | bytes 147464 | tf_op jit(solution)/shard_map/ppermute | solution.py:26
  3.9 1.6 broadcast_in_dim.65
  5.5 8.5 %all-to-all-start = ((bf16[8,8,3072]{2,1,0:T(8,128)(2,1)}), bf16[8,8,3072]{2,1,0:T(8,128)(2,1)S(1)}, u32[]{:S(2)}, u32[]{:S(2)}) async-start(bf16[8,8,3072]{2,1,0:T(8,128)(2,1)} %broadcast_in_dim.65), calls=%async_computation | async-start | bytes 786432 | tf_op jit(solution)/shard_map/all_to_all | solution.py:165
  14.0 1.4 constant_dynamic-update-slice_fusion.4
  15.4 1.4 constant_dynamic-update-slice_fusion.3
  16.8 11.5 %all-to-all-done = bf16[8,8,3072]{2,1,0:T(8,128)(2,1)S(1)} async-done(((bf16[8,8,3072]{2,1,0:T(8,128)(2,1)}), bf16[8,8,3072]{2,1,0:T(8,128)(2,1)S(1)}, u32[]{:S(2)}, u32[]{:S(2)}) %all-to-all-start) | async-done | bytes 393248 | tf_op jit(solution)/shard_map/all_to_all | solution.py:165
  28.6 2.0 broadcast_in_dim.66
  30.6 4.8 %all-to-all-start.1 = ((bf16[8,64,3072]{2,1,0:T(8,128)(2,1)}), bf16[8,64,3072]{2,1,0:T(8,128)(2,1)S(1)}, u32[]{:S(2)}, u32[]{:S(2)}) async-start(bf16[8,64,3072]{2,1,0:T(8,128)(2,1)} %broadcast_in_dim.66), calls=%async_computation.1 | async-start | bytes 6291456 | tf_op jit(solution)/shard_map/all_to_all | solution.py:165
  36.3 2.9 %collective-permute-start.2 = (bf16[16,3072]{1,0:T(8,128)(2,1)S(1)}, bf16[16,3072]{1,0:T(8,128)(2,1)S(1)}, u32[]{:S(2)}, u32[]{:S(2)}) collective-permute-start(bf16[16,3072]{1,0:T(8,128)(2,1)S(1)} %pad_maximum_fusion.1), channel_id=1, source_target_pairs={{0,2},{1,3},{2,0},{3,1},{4,6},{5,7},{6,4},{7,5},{8,10},{9,11},{10,... | collective-permute-start | bytes 294920 | tf_op jit(solution)/shard_map/ppermute | solution.py:26
  39.3 1.8 collective-permute-start.3
  41.0 37.0 %collective-permute-done.1 = bf16[16,3072]{1,0:T(8,128)(2,1)S(1)} collective-permute-done((bf16[16,3072]{1,0:T(8,128)(2,1)S(1)}, bf16[16,3072]{1,0:T(8,128)(2,1)S(1)}, u32[]{:S(2)}, u32[]{:S(2)}) %collective-permute-start.1) | collective-permute-done | bytes 98336 | tf_op jit(solution)/shard_map/ppermute | solution.py:26
  78.0 1.7 collective-permute-done.2
  79.8 3.2 %collective-permute-start.4 = (bf16[64,3072]{1,0:T(8,128)(2,1)S(1)}, bf16[64,3072]{1,0:T(8,128)(2,1)S(1)}, u32[]{:S(2)}, u32[]{:S(2)}) collective-permute-start(bf16[64,3072]{1,0:T(8,128)(2,1)S(1)} %constant_dynamic-update-slice_fusion.refs_7_), channel_id=1, source_target_pairs={{0,56},{8,0},{16,8},{24,16},{32,24},{40,32},{48,40},{56,48},{1,57}... | collective-permute-start | bytes 1179656 | tf_op jit(solution)/shard_map/ppermute | solution.py:26
  83.1 6.9 %collective-permute-done.7.refs_15_ = bf16[64,3072]{1,0:T(8,128)(2,1)S(1)} collective-permute-done((bf16[64,3072]{1,0:T(8,128)(2,1)S(1)}, bf16[64,3072]{1,0:T(8,128)(2,1)S(1)}, u32[]{:S(2)}, u32[]{:S(2)}) %collective-permute-start.7) | collective-permute-done | bytes 393248 | tf_op jit(solution)/shard_map/ppermute | solution.py:26
  90.0 3.2 %collective-permute-start.5 = (bf16[64,3072]{1,0:T(8,128)(2,1)S(1)}, bf16[64,3072]{1,0:T(8,128)(2,1)}, u32[]{:S(2)}, u32[]{:S(2)}) collective-permute-start(bf16[64,3072]{1,0:T(8,128)(2,1)S(1)} %collective-permute-done.4.refs_8_), channel_id=1, source_target_pairs={{0,56},{8,0},{16,8},{24,16},{32,24},{40,32},{48,40},{56,48},{1,57}... | collective-permute-start | bytes 1179656 | tf_op jit(solution)/shard_map/ppermute | solution.py:26
  93.2 6.1 %collective-permute-done.8.refs_14_ = bf16[64,3072]{1,0:T(8,128)(2,1)} collective-permute-done((bf16[64,3072]{1,0:T(8,128)(2,1)S(1)}, bf16[64,3072]{1,0:T(8,128)(2,1)}, u32[]{:S(2)}, u32[]{:S(2)}) %collective-permute-start.8) | collective-permute-done | bytes 393248 | tf_op jit(solution)/shard_map/ppermute | solution.py:26
  99.3 3.2 %collective-permute-start.6 = (bf16[64,3072]{1,0:T(8,128)(2,1)}, bf16[64,3072]{1,0:T(8,128)(2,1)}, u32[]{:S(2)}, u32[]{:S(2)}) collective-permute-start(bf16[64,3072]{1,0:T(8,128)(2,1)} %collective-permute-done.5.refs_9_), channel_id=1, source_target_pairs={{0,56},{8,0},{16,8},{24,16},{32,24},{40,32},{48,40},{56,48},{1,57}... | collective-permute-start | bytes 1179656 | tf_op jit(solution)/shard_map/ppermute | solution.py:26
  103.8 5.8 %collective-permute-done.9.refs_13_ = bf16[64,3072]{1,0:T(8,128)(2,1)S(1)} collective-permute-done((bf16[64,3072]{1,0:T(8,128)(2,1)}, bf16[64,3072]{1,0:T(8,128)(2,1)S(1)}, u32[]{:S(2)}, u32[]{:S(2)}) %collective-permute-start.9) | collective-permute-done | bytes 393248 | tf_op jit(solution)/shard_map/ppermute | solution.py:26
  110.7 3.4 %collective-permute-start.11 = (bf16[32,3072]{1,0:T(8,128)(2,1)S(1)}, bf16[32,3072]{1,0:T(8,128)(2,1)}, u32[]{:S(2)}, u32[]{:S(2)}) collective-permute-start(bf16[32,3072]{1,0:T(8,128)(2,1)S(1)} %slice.228), channel_id=1, source_target_pairs={{0,56},{8,0},{16,8},{24,16},{32,24},{40,32},{48,40},{56,48},{1,57}... | collective-permute-start | bytes 589832 | tf_op jit(solution)/shard_map/ppermute | solution.py:26
  114.2 1.2 pad_add_fusion.refs_0_
  115.4 1.0 fusion.26.refs_5_
  117.4 1.7 copy-done.1
  119.1 19.4 %head_grads.2 = (bf16[512,3072]{1,0:T(8,128)(2,1)}, f32[512,3072]{1,0:T(8,128)}, bf16[64,3072]{1,0:T(8,128)(2,1)}, bf16[64,3072]{1,0:T(8,128)(2,1)}, bf16[64,153...) custom-call(s32[2]{0:T(128)} %pad_add_fusion.refs_0_, bf16[512,3072]{1,0:T(8,128)(2,1)} %bitcast.30, bf16[512,3072]{1,0:T(8,128)(2,1)} %bitcast.32, ...), custom_call_target="tpu_custom_call" | custom-call | flops 4831838208 | bytes 66000000 | tf_op jit(solution)/shard_map/head_grads/pallas_call | solution.py:145
  138.4 7.8 %all-to-all-start.2 = ((bf16[8,72,1536]{2,1,0:T(8,128)(2,1)}), bf16[8,72,1536]{2,1,0:T(8,128)(2,1)S(1)}, u32[]{:S(2)}, u32[]{:S(2)}) async-start(bf16[8,72,1536]{2,1,0:T(8,128)(2,1)} %bitcast.36), calls=%async_computation.2 | async-start | bytes 3538944 | tf_op jit(solution)/shard_map/all_to_all | solution.py:165
  147.2 19.4 %head_grads.3 = (bf16[512,3072]{1,0:T(8,128)(2,1)}, f32[512,3072]{1,0:T(8,128)}, bf16[64,3072]{1,0:T(8,128)(2,1)}, bf16[64,3072]{1,0:T(8,128)(2,1)}, bf16[64,153...) custom-call(s32[2]{0:T(128)} %pad_add_fusion.refs_0_, ...), custom_call_target="tpu_custom_call", output_to_operand_aliasing={{0}: (16, {}), {1}: (17, {}), {2}: (18, {}), {3}: (19, {})} | custom-call | flops 4831838208 | bytes 66000000 | tf_op jit(solution)/shard_map/head_grads/pallas_call | solution.py:145
  167.5 3.1 %collective-permute-start.15 = (bf16[64,3072]{1,0:T(8,128)(2,1)}, bf16[64,3072]{1,0:T(8,128)(2,1)}, u32[]{:S(2)}, u32[]{:S(2)}) collective-permute-start(bf16[64,3072]{1,0:T(8,128)(2,1)} %get-tuple-element.56), channel_id=1, source_target_pairs={{0,56},{8,0},{16,8},{24,16},{32,24},{40,32},{48,40},{56,48},{1,57}... | collective-permute-start | bytes 1179656 | tf_op jit(solution)/shard_map/ppermute | solution.py:26
  170.6 7.2 %all-to-all-start.3 = ((bf16[8,72,1536]{2,1,0:T(8,128)(2,1)}), bf16[8,72,1536]{2,1,0:T(8,128)(2,1)S(1)}, u32[]{:S(2)}, u32[]{:S(2)}) async-start(bf16[8,72,1536]{2,1,0:T(8,128)(2,1)} %bitcast.35), calls=%async_computation.3 | async-start | bytes 3538944 | tf_op jit(solution)/shard_map/all_to_all | solution.py:165
  177.8 5.0 %collective-permute-start.19 = (bf16[64,1536]{1,0:T(8,128)(2,1)}, bf16[64,1536]{1,0:T(8,128)(2,1)}, u32[]{:S(2)}, u32[]{:S(2)}) collective-permute-start(bf16[64,1536]{1,0:T(8,128)(2,1)} %get-tuple-element.61), channel_id=1, source_target_pairs={{0,32},{8,40},{16,48},{24,56},{32,0},{40,8},{48,16},{56,24},{1,33}... | collective-permute-start | bytes 589832 | tf_op jit(solution)/shard_map/ppermute | solution.py:26
  182.8 1.7 add_convert_fusion.2
  184.6 2.0 collective-permute-start.14
  186.6 1.3 collective-permute-start.16
  187.9 1.0 convert_add_fusion.2
  188.9 6.9 %collective-permute-done.14 = bf16[64,3072]{1,0:T(8,128)(2,1)S(1)} collective-permute-done((bf16[64,3072]{1,0:T(8,128)(2,1)S(1)}, bf16[64,3072]{1,0:T(8,128)(2,1)S(1)}, u32[]{:S(2)}, u32[]{:S(2)}) %collective-permute-start.14) | collective-permute-done | bytes 393248 | tf_op jit(solution)/shard_map/ppermute | solution.py:26
  196.8 1.0 fusion
  197.9 1.6 add_convert_fusion.1
  199.5 1.3 collective-permute-start.17
  200.8 2.3 collective-permute-start.18
  204.3 5.5 %all-to-all-start.4 = ((bf16[8,16,3072]{2,1,0:T(8,128)(2,1)}), bf16[8,16,3072]{2,1,0:T(8,128)(2,1)S(1)}, u32[]{:S(2)}, u32[]{:S(2)}) async-start(bf16[8,16,3072]{2,1,0:T(8,128)(2,1)} %pad_maximum_fusion), calls=%async_computation.4 | async-start | bytes 1572864 | tf_op jit(solution)/shard_map/all_to_all | solution.py:165
  209.8 1.4 collective-permute-done.17
  211.1 5.3 %collective-permute-done.18 = bf16[64,3072]{1,0:T(8,128)(2,1)S(1)} collective-permute-done((bf16[64,3072]{1,0:T(8,128)(2,1)S(1)}, bf16[64,3072]{1,0:T(8,128)(2,1)S(1)}, u32[]{:S(2)}, u32[]{:S(2)}) %collective-permute-start.18) | collective-permute-done | bytes 393248 | tf_op jit(solution)/shard_map/ppermute | solution.py:26
  216.4 1.6 fusion.37
  218.6 3.4 %collective-permute-start.21 = (bf16[16,3072]{1,0:T(8,128)(2,1)S(1)}, bf16[16,3072]{1,0:T(8,128)(2,1)S(1)}, u32[]{:S(2)}, u32[]{:S(2)}) collective-permute-start(bf16[16,3072]{1,0:T(8,128)(2,1)S(1)} %get-tuple-element.78), channel_id=1, source_target_pairs={{0,2},{1,3},{2,0},{3,1},{4,6},{5,7},{6,4},{7,5},{8,10},{9,11},{10,... | collective-permute-start | bytes 294920 | tf_op jit(solution)/shard_map/ppermute | solution.py:26
  222.7 2.0 collective-permute-done.21
  224.7 1.9 collective-permute-done.22
  226.7 1.6 collective-permute-start.23
  228.7 1.4 collective-permute-start.25
  230.1 1.4 collective-permute-start.26
  231.5 1.5 collective-permute-done.23
  (79 shorter events, 11.4 us)
Async XLA Ops:
  0.6 102.6 %copy-start = (s32[1,64]{1,0:T(1,128)S(1)}, s32[1,64]{1,0:T(1,128)}, u32[]{:S(2)}) copy-start(s32[1,64]{1,0:T(1,128)} %param.11) | copy-start | bytes 772
  0.6 13.3 %collective-permute-start = (bf16[8,3072]{1,0:T(8,128)(2,1)}, bf16[8,3072]{1,0:T(8,128)(2,1)S(1)}, u32[]{:S(2)}, u32[]{:S(2)}) collective-permute-start(bf16[8,3072]{1,0:T(8,128)(2,1)} %bitcast.38), channel_id=1, source_target_pairs={{0,4},{4,0},{1,5},{5,1},{2,6},{6,2},{3,7},{7,3},{8,12},{12,8},{9,1... | collective-permute-start | bytes 147464 | tf_op jit(solution)/shard_map/ppermute | solution.py:26
  5.5 22.9 %all-to-all-start = ((bf16[8,8,3072]{2,1,0:T(8,128)(2,1)}), bf16[8,8,3072]{2,1,0:T(8,128)(2,1)S(1)}, u32[]{:S(2)}, u32[]{:S(2)}) async-start(bf16[8,8,3072]{2,1,0:T(8,128)(2,1)} %broadcast_in_dim.65), calls=%async_computation | async-start | bytes 786432 | tf_op jit(solution)/shard_map/all_to_all | solution.py:165
  30.6 86.7 %all-to-all-start.1 = ((bf16[8,64,3072]{2,1,0:T(8,128)(2,1)}), bf16[8,64,3072]{2,1,0:T(8,128)(2,1)S(1)}, u32[]{:S(2)}, u32[]{:S(2)}) async-start(bf16[8,64,3072]{2,1,0:T(8,128)(2,1)} %broadcast_in_dim.66), calls=%async_computation.1 | async-start | bytes 6291456 | tf_op jit(solution)/shard_map/all_to_all | solution.py:165
  36.3 41.7 %collective-permute-start.1 = (bf16[16,3072]{1,0:T(8,128)(2,1)S(1)}, bf16[16,3072]{1,0:T(8,128)(2,1)S(1)}, u32[]{:S(2)}, u32[]{:S(2)}) collective-permute-start(bf16[16,3072]{1,0:T(8,128)(2,1)S(1)} %pad_maximum_fusion.1), channel_id=1, source_target_pairs={{0,3},{1,0},{2,1},{3,2},{4,7},{5,4},{6,5},{7,6},{8,11},{9,8},{10,9... | collective-permute-start | bytes 294920 | tf_op jit(solution)/shard_map/ppermute | solution.py:26
  36.3 43.4 %collective-permute-start.2 = (bf16[16,3072]{1,0:T(8,128)(2,1)S(1)}, bf16[16,3072]{1,0:T(8,128)(2,1)S(1)}, u32[]{:S(2)}, u32[]{:S(2)}) collective-permute-start(bf16[16,3072]{1,0:T(8,128)(2,1)S(1)} %pad_maximum_fusion.1), channel_id=1, source_target_pairs={{0,2},{1,3},{2,0},{3,1},{4,6},{5,7},{6,4},{7,5},{8,10},{9,11},{10,... | collective-permute-start | bytes 294920 | tf_op jit(solution)/shard_map/ppermute | solution.py:26
  39.3 40.5 %collective-permute-start.3 = (bf16[16,3072]{1,0:T(8,128)(2,1)S(1)}, bf16[16,3072]{1,0:T(8,128)(2,1)S(1)}, u32[]{:S(2)}, u32[]{:S(2)}) collective-permute-start(bf16[16,3072]{1,0:T(8,128)(2,1)S(1)} %pad_maximum_fusion.1), channel_id=1, source_target_pairs={{0,1},{1,2},{2,3},{3,0},{4,5},{5,6},{6,7},{7,4},{8,9},{9,10},{10,1... | collective-permute-start | bytes 294920 | tf_op jit(solution)/shard_map/ppermute | solution.py:26
  79.7 13.5 %copy-start.4 = (bf16[64,3072]{1,0:T(8,128)(2,1)}, bf16[64,3072]{1,0:T(8,128)(2,1)S(1)}, u32[]{:S(2)}) copy-start(bf16[64,3072]{1,0:T(8,128)(2,1)S(1)} %constant_dynamic-update-slice_fusion.refs_7_) | copy-start | bytes 1179652
  79.8 10.2 %collective-permute-start.7 = (bf16[64,3072]{1,0:T(8,128)(2,1)S(1)}, bf16[64,3072]{1,0:T(8,128)(2,1)S(1)}, u32[]{:S(2)}, u32[]{:S(2)}) collective-permute-start(bf16[64,3072]{1,0:T(8,128)(2,1)S(1)} %constant_dynamic-update-slice_fusion.refs_7_), channel_id=1, source_target_pairs={{0,8},{8,16},{16,24},{24,32},{32,40},{40,48},{48,56},{56,0},{1,9},... | collective-permute-start | bytes 1179656 | tf_op jit(solution)/shard_map/ppermute | solution.py:26
  79.8 10.1 %collective-permute-start.4 = (bf16[64,3072]{1,0:T(8,128)(2,1)S(1)}, bf16[64,3072]{1,0:T(8,128)(2,1)S(1)}, u32[]{:S(2)}, u32[]{:S(2)}) collective-permute-start(bf16[64,3072]{1,0:T(8,128)(2,1)S(1)} %constant_dynamic-update-slice_fusion.refs_7_), channel_id=1, source_target_pairs={{0,56},{8,0},{16,8},{24,16},{32,24},{40,32},{48,40},{56,48},{1,57}... | collective-permute-start | bytes 1179656 | tf_op jit(solution)/shard_map/ppermute | solution.py:26
  90.0 9.3 %copy-start.7 = (bf16[64,3072]{1,0:T(8,128)(2,1)}, bf16[64,3072]{1,0:T(8,128)(2,1)S(1)}, u32[]{:S(2)}) copy-start(bf16[64,3072]{1,0:T(8,128)(2,1)S(1)} %collective-permute-done.7.refs_15_) | copy-start | bytes 1179652
  90.0 9.3 %collective-permute-start.8 = (bf16[64,3072]{1,0:T(8,128)(2,1)S(1)}, bf16[64,3072]{1,0:T(8,128)(2,1)}, u32[]{:S(2)}, u32[]{:S(2)}) collective-permute-start(bf16[64,3072]{1,0:T(8,128)(2,1)S(1)} %collective-permute-done.7.refs_15_), channel_id=1, source_target_pairs={{0,8},{8,16},{16,24},{24,32},{32,40},{40,48},{48,56},{56,0},{1,9},... | collective-permute-start | bytes 1179656 | tf_op jit(solution)/shard_map/ppermute | solution.py:26
  90.0 9.3 %copy-start.8 = (bf16[64,3072]{1,0:T(8,128)(2,1)}, bf16[64,3072]{1,0:T(8,128)(2,1)S(1)}, u32[]{:S(2)}) copy-start(bf16[64,3072]{1,0:T(8,128)(2,1)S(1)} %collective-permute-done.4.refs_8_) | copy-start | bytes 1179652
  90.0 9.3 %collective-permute-start.5 = (bf16[64,3072]{1,0:T(8,128)(2,1)S(1)}, bf16[64,3072]{1,0:T(8,128)(2,1)}, u32[]{:S(2)}, u32[]{:S(2)}) collective-permute-start(bf16[64,3072]{1,0:T(8,128)(2,1)S(1)} %collective-permute-done.4.refs_8_), channel_id=1, source_target_pairs={{0,56},{8,0},{16,8},{24,16},{32,24},{40,32},{48,40},{56,48},{1,57}... | collective-permute-start | bytes 1179656 | tf_op jit(solution)/shard_map/ppermute | solution.py:26
  99.3 10.3 %collective-permute-start.9 = (bf16[64,3072]{1,0:T(8,128)(2,1)}, bf16[64,3072]{1,0:T(8,128)(2,1)S(1)}, u32[]{:S(2)}, u32[]{:S(2)}) collective-permute-start(bf16[64,3072]{1,0:T(8,128)(2,1)} %collective-permute-done.8.refs_14_), channel_id=1, source_target_pairs={{0,8},{8,16},{16,24},{24,32},{32,40},{40,48},{48,56},{56,0},{1,9},... | collective-permute-start | bytes 1179656 | tf_op jit(solution)/shard_map/ppermute | solution.py:26
  99.3 10.4 %collective-permute-start.6 = (bf16[64,3072]{1,0:T(8,128)(2,1)}, bf16[64,3072]{1,0:T(8,128)(2,1)}, u32[]{:S(2)}, u32[]{:S(2)}) collective-permute-start(bf16[64,3072]{1,0:T(8,128)(2,1)} %collective-permute-done.5.refs_9_), channel_id=1, source_target_pairs={{0,56},{8,0},{16,8},{24,16},{32,24},{40,32},{48,40},{56,48},{1,57}... | collective-permute-start | bytes 1179656 | tf_op jit(solution)/shard_map/ppermute | solution.py:26
  109.6 7.7 %copy-start.3 = (bf16[64,3072]{1,0:T(8,128)(2,1)}, bf16[64,3072]{1,0:T(8,128)(2,1)S(1)}, u32[]{:S(2)}) copy-start(bf16[64,3072]{1,0:T(8,128)(2,1)S(1)} %collective-permute-done.9.refs_13_) | copy-start | bytes 1179652
  109.6 7.0 %collective-permute-start.10 = (bf16[32,3072]{1,0:T(8,128)(2,1)S(1)}, bf16[32,3072]{1,0:T(8,128)(2,1)S(1)}, u32[]{:S(2)}, u32[]{:S(2)}) collective-permute-start(bf16[32,3072]{1,0:T(8,128)(2,1)S(1)} %slice.227), channel_id=1, source_target_pairs={{0,8},{8,16},{16,24},{24,32},{32,40},{40,48},{48,56},{56,0},{1,9},... | collective-permute-start | bytes 589832 | tf_op jit(solution)/shard_map/ppermute | solution.py:26
  110.7 6.6 %collective-permute-start.11 = (bf16[32,3072]{1,0:T(8,128)(2,1)S(1)}, bf16[32,3072]{1,0:T(8,128)(2,1)}, u32[]{:S(2)}, u32[]{:S(2)}) collective-permute-start(bf16[32,3072]{1,0:T(8,128)(2,1)S(1)} %slice.228), channel_id=1, source_target_pairs={{0,56},{8,0},{16,8},{24,16},{32,24},{40,32},{48,40},{56,48},{1,57}... | collective-permute-start | bytes 589832 | tf_op jit(solution)/shard_map/ppermute | solution.py:26
  116.6 0.7 copy-start.9
  117.4 1.7 copy-start.1
  138.4 7.8 %copy-start.10 = (bf16[64,1536]{1,0:T(8,128)(2,1)S(1)}, bf16[64,1536]{1,0:T(8,128)(2,1)}, u32[]{:S(2)}) copy-start(bf16[64,1536]{1,0:T(8,128)(2,1)} %get-tuple-element.52) | copy-start | bytes 589828
  138.4 28.2 %all-to-all-start.2 = ((bf16[8,72,1536]{2,1,0:T(8,128)(2,1)}), bf16[8,72,1536]{2,1,0:T(8,128)(2,1)S(1)}, u32[]{:S(2)}, u32[]{:S(2)}) async-start(bf16[8,72,1536]{2,1,0:T(8,128)(2,1)} %bitcast.36), calls=%async_computation.2 | async-start | bytes 3538944 | tf_op jit(solution)/shard_map/all_to_all | solution.py:165
  146.2 20.4 %collective-permute-start.12 = (bf16[64,1536]{1,0:T(8,128)(2,1)S(1)}, bf16[64,1536]{1,0:T(8,128)(2,1)}, u32[]{:S(2)}, u32[]{:S(2)}) collective-permute-start(bf16[64,1536]{1,0:T(8,128)(2,1)S(1)} %copy-done.10), channel_id=1, source_target_pairs={{0,32},{8,40},{16,48},{24,56},{32,0},{40,8},{48,16},{56,24},{1,33}... | collective-permute-start | bytes 589832 | tf_op jit(solution)/shard_map/ppermute | solution.py:26
  166.6 16.2 %collective-permute-start.13 = (bf16[64,3072]{1,0:T(8,128)(2,1)}, bf16[64,3072]{1,0:T(8,128)(2,1)}, u32[]{:S(2)}, u32[]{:S(2)}) collective-permute-start(bf16[64,3072]{1,0:T(8,128)(2,1)} %get-tuple-element.55), channel_id=1, source_target_pairs={{0,8},{8,16},{16,24},{24,32},{32,40},{40,48},{48,56},{56,0},{1,9},... | collective-permute-start | bytes 1179656 | tf_op jit(solution)/shard_map/ppermute | solution.py:26
  167.5 15.3 %collective-permute-start.15 = (bf16[64,3072]{1,0:T(8,128)(2,1)}, bf16[64,3072]{1,0:T(8,128)(2,1)}, u32[]{:S(2)}, u32[]{:S(2)}) collective-permute-start(bf16[64,3072]{1,0:T(8,128)(2,1)} %get-tuple-element.56), channel_id=1, source_target_pairs={{0,56},{8,0},{16,8},{24,16},{32,24},{40,32},{48,40},{56,48},{1,57}... | collective-permute-start | bytes 1179656 | tf_op jit(solution)/shard_map/ppermute | solution.py:26
  170.6 25.9 %all-to-all-start.3 = ((bf16[8,72,1536]{2,1,0:T(8,128)(2,1)}), bf16[8,72,1536]{2,1,0:T(8,128)(2,1)S(1)}, u32[]{:S(2)}, u32[]{:S(2)}) async-start(bf16[8,72,1536]{2,1,0:T(8,128)(2,1)} %bitcast.35), calls=%async_computation.3 | async-start | bytes 3538944 | tf_op jit(solution)/shard_map/all_to_all | solution.py:165
  177.8 31.9 %collective-permute-start.19 = (bf16[64,1536]{1,0:T(8,128)(2,1)}, bf16[64,1536]{1,0:T(8,128)(2,1)}, u32[]{:S(2)}, u32[]{:S(2)}) collective-permute-start(bf16[64,1536]{1,0:T(8,128)(2,1)} %get-tuple-element.61), channel_id=1, source_target_pairs={{0,32},{8,40},{16,48},{24,56},{32,0},{40,8},{48,16},{56,24},{1,33}... | collective-permute-start | bytes 589832 | tf_op jit(solution)/shard_map/ppermute | solution.py:26
  184.6 11.2 %collective-permute-start.14 = (bf16[64,3072]{1,0:T(8,128)(2,1)S(1)}, bf16[64,3072]{1,0:T(8,128)(2,1)S(1)}, u32[]{:S(2)}, u32[]{:S(2)}) collective-permute-start(bf16[64,3072]{1,0:T(8,128)(2,1)S(1)} %get-tuple-element.75), channel_id=1, source_target_pairs={{0,8},{8,16},{16,24},{24,32},{32,40},{40,48},{48,56},{56,0},{1,9},... | collective-permute-start | bytes 1179656 | tf_op jit(solution)/shard_map/ppermute | solution.py:26
  186.6 9.9 %collective-permute-start.16 = (bf16[64,3072]{1,0:T(8,128)(2,1)S(1)}, bf16[64,3072]{1,0:T(8,128)(2,1)}, u32[]{:S(2)}, u32[]{:S(2)}) collective-permute-start(bf16[64,3072]{1,0:T(8,128)(2,1)S(1)} %get-tuple-element.74), channel_id=1, source_target_pairs={{0,56},{8,0},{16,8},{24,16},{32,24},{40,32},{48,40},{56,48},{1,57}... | collective-permute-start | bytes 1179656 | tf_op jit(solution)/shard_map/ppermute | solution.py:26
  188.9 8.9 %copy-start.2 = (f32[72,1536]{1,0:T(8,128)S(1)}, f32[72,1536]{1,0:T(8,128)}, u32[]{:S(2)}) copy-start(f32[72,1536]{1,0:T(8,128)} %convert_add_fusion.2) | copy-start | bytes 1327108
  195.8 0.8 copy-start.5
  196.5 1.3 copy-start.6
  199.5 11.6 %collective-permute-start.17 = (bf16[64,3072]{1,0:T(8,128)(2,1)S(1)}, bf16[64,3072]{1,0:T(8,128)(2,1)S(1)}, u32[]{:S(2)}, u32[]{:S(2)}) collective-permute-start(bf16[64,3072]{1,0:T(8,128)(2,1)S(1)} %get-tuple-element.72), channel_id=1, source_target_pairs={{0,8},{8,16},{16,24},{24,32},{32,40},{40,48},{48,56},{56,0},{1,9},... | collective-permute-start | bytes 1179656 | tf_op jit(solution)/shard_map/ppermute | solution.py:26
  200.8 15.6 %collective-permute-start.18 = (bf16[64,3072]{1,0:T(8,128)(2,1)S(1)}, bf16[64,3072]{1,0:T(8,128)(2,1)S(1)}, u32[]{:S(2)}, u32[]{:S(2)}) collective-permute-start(bf16[64,3072]{1,0:T(8,128)(2,1)S(1)} %get-tuple-element.73), channel_id=1, source_target_pairs={{0,56},{8,0},{16,8},{24,16},{32,24},{40,32},{48,40},{56,48},{1,57}... | collective-permute-start | bytes 1179656 | tf_op jit(solution)/shard_map/ppermute | solution.py:26
  204.3 24.1 %all-to-all-start.4 = ((bf16[8,16,3072]{2,1,0:T(8,128)(2,1)}), bf16[8,16,3072]{2,1,0:T(8,128)(2,1)S(1)}, u32[]{:S(2)}, u32[]{:S(2)}) async-start(bf16[8,16,3072]{2,1,0:T(8,128)(2,1)} %pad_maximum_fusion), calls=%async_computation.4 | async-start | bytes 1572864 | tf_op jit(solution)/shard_map/all_to_all | solution.py:165
  218.0 4.7 %collective-permute-start.20 = (bf16[16,3072]{1,0:T(8,128)(2,1)S(1)}, bf16[16,3072]{1,0:T(8,128)(2,1)S(1)}, u32[]{:S(2)}, u32[]{:S(2)}) collective-permute-start(bf16[16,3072]{1,0:T(8,128)(2,1)S(1)} %get-tuple-element.76), channel_id=1, source_target_pairs={{0,1},{1,2},{2,3},{3,0},{4,5},{5,6},{6,7},{7,4},{8,9},{9,10},{10,1... | collective-permute-start | bytes 294920 | tf_op jit(solution)/shard_map/ppermute | solution.py:26
  218.6 6.1 %collective-permute-start.21 = (bf16[16,3072]{1,0:T(8,128)(2,1)S(1)}, bf16[16,3072]{1,0:T(8,128)(2,1)S(1)}, u32[]{:S(2)}, u32[]{:S(2)}) collective-permute-start(bf16[16,3072]{1,0:T(8,128)(2,1)S(1)} %get-tuple-element.78), channel_id=1, source_target_pairs={{0,2},{1,3},{2,0},{3,1},{4,6},{5,7},{6,4},{7,5},{8,10},{9,11},{10,... | collective-permute-start | bytes 294920 | tf_op jit(solution)/shard_map/ppermute | solution.py:26
  222.0 4.6 %collective-permute-start.22 = (bf16[16,3072]{1,0:T(8,128)(2,1)S(1)}, bf16[16,3072]{1,0:T(8,128)(2,1)S(1)}, u32[]{:S(2)}, u32[]{:S(2)}) collective-permute-start(bf16[16,3072]{1,0:T(8,128)(2,1)S(1)} %get-tuple-element.77), channel_id=1, source_target_pairs={{0,3},{1,0},{2,1},{3,2},{4,7},{5,4},{6,5},{7,6},{8,11},{9,8},{10,9... | collective-permute-start | bytes 294920 | tf_op jit(solution)/shard_map/ppermute | solution.py:26
  226.7 6.2 %collective-permute-start.23 = (f32[8,3072]{1,0:T(8,128)S(1)}, f32[8,3072]{1,0:T(8,128)S(1)}, u32[]{:S(2)}, u32[]{:S(2)}) collective-permute-start(f32[8,3072]{1,0:T(8,128)S(1)} %slice.234), channel_id=1, source_target_pairs={{0,4},{4,0},{1,5},{5,1},{2,6},{6,2},{3,7},{7,3},{8,12},{12,8},{9,1... | collective-permute-start | bytes 294920 | tf_op jit(solution)/shard_map/ppermute | solution.py:26
  228.6 5.6 %collective-permute-start.24 = (f32[1,768]{1,0:T(1,128)S(1)}, f32[1,768]{1,0:T(1,128)S(1)}, u32[]{:S(2)}, u32[]{:S(2)}) collective-permute-start(f32[1,768]{1,0:T(1,128)S(1)} %get-tuple-element.80), channel_id=1, source_target_pairs={{0,64},{64,128},{128,192},{192,0},{1,65},{65,129},{129,193},{193,1... | collective-permute-start | bytes 9224 | tf_op jit(solution)/shard_map/ppermute | solution.py:26
  228.7 5.5 %collective-permute-start.25 = (f32[1,768]{1,0:T(1,128)S(1)}, f32[1,768]{1,0:T(1,128)S(1)}, u32[]{:S(2)}, u32[]{:S(2)}) collective-permute-start(f32[1,768]{1,0:T(1,128)S(1)} %get-tuple-element.79), channel_id=1, source_target_pairs={{0,128},{64,192},{128,0},{192,64},{1,129},{65,193},{129,1},{193,65... | collective-permute-start | bytes 9224 | tf_op jit(solution)/shard_map/ppermute | solution.py:26
  230.1 4.1 %collective-permute-start.26 = (f32[1,768]{1,0:T(1,128)S(1)}, f32[1,768]{1,0:T(1,128)S(1)}, u32[]{:S(2)}, u32[]{:S(2)}) collective-permute-start(f32[1,768]{1,0:T(1,128)S(1)} %get-tuple-element.81), channel_id=1, source_target_pairs={{0,192},{64,0},{128,64},{192,128},{1,193},{65,1},{129,65},{193,129... | collective-permute-start | bytes 9224 | tf_op jit(solution)/shard_map/ppermute | solution.py:26
